TPU v7x, 256 devices: a whole 4x4x8 slice. The times are simulated.
256 devices in a mesh: tile: 64 (over y, x, z_lo, core), slab: 4 (over z_hi).
Axes of the slice: x: 4, y: 4, z: 8 (z_hi: 4, z_lo: 2; z = z_hi * 2 + z_lo), core: 2. Of those that a mesh axis runs over, the one named last changes fastest.
Arguments:
- counts: int32 [8192, 8, 512], P('tile', None, 'slab'), may hold values from 0 to 63
- fields: float32 [4, 8192, 8, 512], P(None, 'tile', None, 'slab'), may hold values from -20 to 20
- class_ids: int32 [8192, 8, 512], P('tile', None, 'slab'), may hold values from 0 to 7
- tf_table: float32 [8, 4, 6], replicated, may hold values from -2 to 2
Outputs:
- layers: float32 [4, 4, 8, 8192], P('slab', None, None, 'tile')
All inputs are finite; a program needn't handle non-finite values.
Results may differ from a plain program's by a relative error of at most 0.0003.
Values sent between devices are 32-bit elements; how exact they have to be, the bound alone decides.
No kernel may reach another device: no remote copies, remote signals or barrier semaphores. Data moves between devices by JAX's collectives and lax.ppermute only.
A program may use at most 128 MiB of HBM per device.

v0:
```python
import math

import jax
import jax.numpy as jnp
from jax import lax
from jax.sharding import PartitionSpec as P

CLASSES = 8
RADIUS = 4


SPLAT = 2.0
OPTICAL = 0.5


def padded_2(array, sides, width):
    for axis, dim in sides:
        peers, length = (lax.axis_size(axis), array.shape[dim])
        up = [(i, (i + 1) % peers) for i in range(peers - 1)]
        down = [(j, i) for i, j in up]
        last = lax.slice_in_dim(array, length - width, length, axis=dim)
        first = lax.slice_in_dim(array, 0, width, axis=dim)
        before = lax.ppermute(last, axis, up)
        after = lax.ppermute(first, axis, down)
        array = jnp.concatenate([before, array, after], axis=dim)
    return array


def prefix(value, axis, join, neutral):
    count, mine = (lax.axis_size(axis), lax.axis_index(axis))
    pieces = jax.tree.map(lambda part: lax.all_gather(part, axis), value)
    running = jax.tree.map(
        lambda part, zero: jnp.full_like(part, 0) + jnp.asarray(zero, part.dtype), value, neutral
    )

    def step(position, running):
        longer = join(running, jax.tree.map(lambda part: part[position], pieces))
        return jax.tree.map(lambda new, old: jnp.where(position < mine, new, old), longer, running)

    return lax.fori_loop(0, count - 1, step, running)


def splat_taps():
    raw = [
        math.exp(-((offset - RADIUS) ** 2) / (2.0 * SPLAT * SPLAT))
        for offset in range(2 * RADIUS + 1)
    ]
    norm_total = sum(raw)
    return [value / norm_total for value in raw]


def blur_valid(volume, along):
    weights = splat_taps()
    length = volume.shape[along] - 2 * RADIUS
    running = weights[0] * lax.slice_in_dim(volume, 0, length, axis=along)
    for offset in range(1, 2 * RADIUS + 1):
        running = running + weights[offset] * lax.slice_in_dim(
            volume, offset, offset + length, axis=along
        )
    return running


def blur_padded(volume, along):
    widths = [(0, 0)] * volume.ndim
    widths[along] = (RADIUS, RADIUS)
    return blur_valid(jnp.pad(volume, widths), along)


def combine_pair(nearer, farther):
    return (nearer[0] + nearer[1][None] * farther[0], nearer[1] * farther[1])


def on_device(counts, fields, class_ids, tf_table):
    n_cols, n_rows, n_depth = counts.shape
    n_cells = n_cols * n_rows * n_depth
    density = jnp.log1p(counts.astype(jnp.float32))
    volume = jnp.concatenate([density[None], fields], 0)
    volume = blur_padded(volume, 2)
    padded = padded_2(volume, (("tile", 1), ("slab", 3)), RADIUS)
    along_x = blur_valid(padded, 1)
    smooth = blur_valid(along_x, 3)
    smooth = smooth.reshape(5, n_cells)
    labels = (
        class_ids.reshape(1, n_cells) == jnp.arange(CLASSES, dtype=jnp.int32)[:, None]
    ).astype(jnp.float32)
    linears = []
    for channel in range(4):
        coefficients = jnp.dot(
            jnp.transpose(tf_table[:, channel, :]), labels, precision=lax.Precision.HIGHEST
        )
        linear = coefficients[0] * smooth[0]
        for field_index in range(1, 5):
            linear = linear + coefficients[field_index] * smooth[field_index]
        linears.append(linear + coefficients[5])
    emitted = jax.nn.sigmoid(jnp.stack(linears[:3], 0)).reshape(3, n_cols * n_rows, n_depth)
    depth_total = n_depth * lax.axis_size("slab")
    depth_step = (jax.nn.softplus(linears[3]) * (OPTICAL / depth_total)).reshape(
        n_cols * n_rows, n_depth
    )
    opacity = -jnp.expm1(-depth_step)
    cell_pos = jnp.arange(n_depth, dtype=jnp.int32)
    upper_ones = (cell_pos[:, None] < cell_pos[None, :]).astype(jnp.float32)
    before = jnp.dot(depth_step, upper_ones, precision=lax.Precision.HIGHEST)
    shading = opacity * jnp.exp(-before)
    radiance = jnp.sum(emitted * shading[None], axis=-1).reshape(3, n_cols, n_rows)
    transmit = jnp.exp(-jnp.sum(depth_step, axis=-1)).reshape(n_cols, n_rows)
    identity = (
        jnp.zeros((3, n_cols, n_rows), jnp.float32),
        jnp.ones((n_cols, n_rows), jnp.float32),
    )
    front_rad, front_tra = prefix((radiance, transmit), "slab", combine_pair, identity)
    shown = front_rad + front_tra[None] * radiance
    alpha_out = 1.0 - front_tra * transmit
    image = jnp.concatenate([shown, alpha_out[None]], 0)
    return jnp.transpose(image, (0, 2, 1))[None]


def solution(mesh):
    return jax.shard_map(
        on_device,
        mesh=mesh,
        in_specs=(
            P("tile", None, "slab"),
            P(None, "tile", None, "slab"),
            P("tile", None, "slab"),
            P(),
        ),
        out_specs=P("slab", None, None, "tile"),
        check_vma=False,
    )
```

profile of v0, /device:TPU:24, one launch (start us, length us, event | category | flops | bytes accessed | tf_op | source)
XLA Modules:
  0.0 147.1 jit_solution(13433120993496857685)
XLA Ops:
  1.2 1.8 %pad_maximum_fusion.2 = f32[5,128,8,128]{3,2,1,0:T(8,128)S(1)} fusion(f32[4,128,8,128]{3,2,1,0:T(8,128)} %param.7, f32[1,128,8,128]{3,2,1,0:T(8,128)S(1)} %log-plus-one_bitcast_fusion), kind=kLoop, calls=%fused_computation.69 | loop fusion | flops 655360 | bytes 5242880 | tf_op jit(solution)/shard_map/concatenate | solution.py:77
  3.0 2.9 %fusion.16 = f32[5,128,8,128]{3,2,1,0:T(8,128)S(1)} fusion(f32[5,128,8,128]{3,2,1,0:T(8,128)S(1)} %pad_maximum_fusion.2), kind=kLoop, calls=%fused_computation.44 | loop fusion | flops 11141120 | bytes 5242880 | tf_op jit(solution)/shard_map/add | solution.py:57
  5.9 1.9 %collective-permute-start = (f32[5,4,8,128]{3,2,1,0:T(8,128)S(1)}, f32[5,4,8,128]{3,2,1,0:T(8,128)S(1)}, u32[]{:S(2)}, u32[]{:S(2)}) collective-permute-start(f32[5,4,8,128]{3,2,1,0:T(8,128)S(1)} %get-tuple-element.175), channel_id=1, source_target_pairs={{0,4},{4,8},{8,12},{12,16},{16,20},{20,24},{24,28},{28,32},{32,36}... | collective-permute-start | bytes 245768 | tf_op jit(solution)/shard_map/ppermute | solution.py:23
  7.8 6.7 %collective-permute-start.1 = (f32[5,4,8,128]{3,2,1,0:T(8,128)S(1)}, f32[5,4,8,128]{3,2,1,0:T(8,128)S(1)}, u32[]{:S(2)}, u32[]{:S(2)}) collective-permute-start(f32[5,4,8,128]{3,2,1,0:T(8,128)S(1)} %get-tuple-element.176), channel_id=1, source_target_pairs={{4,0},{8,4},{12,8},{16,12},{20,16},{24,20},{28,24},{32,28},{36,32}... | collective-permute-start | bytes 245768 | tf_op jit(solution)/shard_map/ppermute | solution.py:24
  14.8 3.9 %convolution_bitcast_fusion.2 = f32[6,131072]{1,0:T(8,128)} fusion(s32[131072]{0:T(1024)S(1)} %bitcast.97, f32[8,1,6]{2,0,1:T(8,128)S(1)} %copy.71), kind=kOutput, calls=%fused_computation.6 | convolution fusion | flops 76546048 | bytes 3670208 | tf_op jit(solution)/shard_map/dot_general | solution.py:88
  18.7 1.9 %convolution_bitcast_fusion = f32[6,131072]{1,0:T(8,128)S(1)} fusion(s32[131072]{0:T(1024)S(1)} %bitcast.98, f32[8,1,6]{2,0,1:T(8,128)S(1)} %copy.73), kind=kOutput, calls=%fused_computation.4 | convolution fusion | flops 76546048 | bytes 3670208 | tf_op jit(solution)/shard_map/dot_general | solution.py:88
  20.6 3.5 %fusion.67 = (f32[1,131072]{1,0:T(1,128)}, f32[1,131072]{1,0:T(1,128)}, f32[1,131072]{1,0:T(1,128)}, f32[1,131072]{1,0:T(1,128)}, f32[1,131072]{1,0:T(1,128)}, /*index=5*/f32[1,131072]{1,0:T(1,128)}) fusion(f32[6,131072]{1,0:T(8,128)S(1)} %convolution_bitcast_fusion), kind=kLoop, calls=%fused_computation.136 | loop fusion | bytes 6291456 | tf_op jit(solution)/shard_map/slice | solution.py:91
  24.1 3.9 %convolution_bitcast_fusion.1 = f32[6,131072]{1,0:T(8,128)} fusion(s32[131072]{0:T(1024)S(1)} %bitcast.99, f32[8,1,6]{2,0,1:T(8,128)S(1)} %copy.72), kind=kOutput, calls=%fused_computation.5 | convolution fusion | flops 76546048 | bytes 3670208 | tf_op jit(solution)/shard_map/dot_general | solution.py:88
  28.3 3.3 %fusion.68 = (f32[5,136,8,4]{3,2,1,0:T(8,128)}, f32[5,136,8,4]{3,2,1,0:T(8,128)}) fusion(f32[5,136,8,128]{3,2,1,0:T(8,128)S(1)} %pad_maximum_fusion.1), kind=kLoop, calls=%fused_computation.137 | loop fusion | bytes 348160 | tf_op jit(solution)/shard_map/slice | solution.py:21
  31.5 3.3 %copy.58 = f32[5,136,8,4]{1,2,3,0:T(8,128)S(1)} copy(f32[5,136,8,4]{3,2,1,0:T(8,128)} %get-tuple-element.166) | data formatting | bytes 174080 | tf_op jit(solution)/shard_map/slice | solution.py:21
  34.8 5.9 %collective-permute-start.2 = (f32[5,136,8,4]{1,2,3,0:T(8,128)S(1)}, f32[5,136,8,4]{1,2,3,0:T(8,128)}, u32[]{:S(2)}, u32[]{:S(2)}) collective-permute-start(f32[5,136,8,4]{1,2,3,0:T(8,128)S(1)} %copy.58), channel_id=1, source_target_pairs={{0,1},{1,2},{2,3},{4,5},{5,6},{6,7},{8,9},{9,10},{10,11},{12,13},{... | collective-permute-start | bytes 261128 | tf_op jit(solution)/shard_map/ppermute | solution.py:23
  40.7 4.0 %copy.59 = f32[5,136,8,4]{1,2,3,0:T(8,128)} copy(f32[5,136,8,4]{3,2,1,0:T(8,128)} %get-tuple-element.167) | data formatting | bytes 174080 | tf_op jit(solution)/shard_map/slice | solution.py:22
  44.6 1.3 collective-permute-start.3
  45.9 3.9 %convolution_bitcast_fusion.3 = f32[6,131072]{1,0:T(8,128)} fusion(s32[131072]{0:T(1024)S(1)} %bitcast.100, f32[8,1,6]{2,0,1:T(8,128)S(1)} %copy.70), kind=kOutput, calls=%fused_computation.7 | convolution fusion | flops 76546048 | bytes 3670208 | tf_op jit(solution)/shard_map/dot_general | solution.py:88
  49.8 3.4 %copy.60 = f32[5,136,8,4]{3,2,1,0:T(8,128)} copy(f32[5,136,8,4]{1,2,3,0:T(8,128)} %collective-permute-done.2) | data formatting | bytes 174080 | tf_op jit(solution)/shard_map/ppermute | solution.py:23
  53.2 2.5 %collective-permute-done.3 = f32[5,136,8,4]{1,2,3,0:T(8,128)} collective-permute-done((f32[5,136,8,4]{1,2,3,0:T(8,128)}, f32[5,136,8,4]{1,2,3,0:T(8,128)}, u32[]{:S(2)}, u32[]{:S(2)}) %collective-permute-start.3) | collective-permute-done | bytes 87072 | tf_op jit(solution)/shard_map/ppermute | solution.py:24
  55.7 3.4 %copy.61 = f32[5,136,8,4]{3,2,1,0:T(8,128)} copy(f32[5,136,8,4]{1,2,3,0:T(8,128)} %collective-permute-done.3) | data formatting | bytes 174080 | tf_op jit(solution)/shard_map/ppermute | solution.py:24
  59.1 7.5 %pad_maximum_fusion = f32[5,136,8,136]{3,2,1,0:T(8,128)} fusion(f32[5,136,8,4]{3,2,1,0:T(8,128)} %copy.61, f32[5,4,8,128]{3,2,1,0:T(8,128)S(1)} %collective-permute-done.1, f32[5,128,8,128]{3,2,1,0:T(8,128)S(1)} %fusion.16, f32[5,4,8,128]{3,2,1,0:T(8,128)S(1)} %collective-permute-done, f32[5,136,8,4]{3,2,1,0:T(8,128)} %copy.60), kind=kLoop, calls=%fused_computation.16 | loop fusion | flops 2959360 | bytes 5918720 | tf_op jit(solution)/shard_map/concatenate | solution.py:25
  66.6 18.7 %fusion = f32[5,128,8,136]{3,2,1,0:T(8,128)} fusion(f32[5,136,8,136]{3,2,1,0:T(8,128)} %pad_maximum_fusion), kind=kLoop, calls=%fused_computation.18 | loop fusion | flops 11837440 | bytes 27852800 | tf_op jit(solution)/shard_map/add | solution.py:57
  85.3 18.4 %fusion.24 = f32[5,128,8,128]{3,2,1,0:T(8,128)S(1)} fusion(f32[5,128,8,136]{3,2,1,0:T(8,128)} %fusion), kind=kLoop, calls=%fused_computation.53 | loop fusion | flops 11141120 | bytes 26214400 | tf_op jit(solution)/shard_map/add | solution.py:57
  107.0 2.8 %slice_add_fusion.1 = f32[1,131072]{1,0:T(1,128)S(1)} fusion(f32[6,131072]{1,0:T(8,128)S(1)} %copy-done.2, f32[1,131072]{1,0:T(1,128)S(1)} %bitcast.103, f32[1,131072]{1,0:T(1,128)S(1)} %bitcast.105, f32[1,131072]{1,0:T(1,128)S(1)} %bitcast.107, f32[1,131072]{1,0:T(1,128)S(1)} %bitcast.109, f32[1,131072]{1,0:T(1,128)S(1)} %bitcast.101), kind=kLoop, calls=%fused_computation.95 | loop fusion | flops 1310720 | bytes 6291456 | tf_op jit(solution)/shard_map/add | solution.py:94
  109.8 5.5 %slice_add_fusion.2 = (f32[1,131072]{1,0:T(1,128)S(1)}, f32[1,131072]{1,0:T(1,128)S(1)}) fusion(f32[6,131072]{1,0:T(8,128)S(1)} %copy-done.1, f32[1,131072]{1,0:T(1,128)S(1)} %bitcast.104, f32[1,131072]{1,0:T(1,128)S(1)} %bitcast.106, f32[1,131072]{1,0:T(1,128)S(1)} %bitcast.108, f32[1,131072]{1,0:T(1,128)S(1)} %bitcast.110, f32[1,131072]{1,0:T(1,128)S(1)} %bitcast.102, ...), kind=kLoop, calls=%fused_computation.105 | loop fusion | flops 2621440 | bytes 9961472 | tf_op jit(solution)/shard_map/add | solution.py:94
  116.4 15.9 %all_gather.6 = f32[4,3,128,8]{2,3,1,0:T(8,128)S(1)} all-gather(f32[1,3,128,8]{2,3,1,0:T(8,128)S(1)} %copy.65), channel_id=1, replica_groups=mesh['tile'=64,'slab'=4] {'slab'}, dimensions={0}, use_global_device_ids=true | all-gather | bytes 61440 | tf_op jit(solution)/shard_map/all_gather | solution.py:31
  132.3 13.7 %all_gather.7 = f32[4,128,8]{1,2,0:T(8,128)S(1)} all-gather(f32[1,128,8]{1,2,0:T(8,128)S(1)} %copy.66), channel_id=1, replica_groups=mesh['tile'=64,'slab'=4] {'slab'}, dimensions={0}, use_global_device_ids=true | all-gather | bytes 20480 | tf_op jit(solution)/shard_map/all_gather | solution.py:31
  (59 shorter events, 7.1 us)
Async XLA Ops:
  3.0 11.5 %copy-start.10 = (f32[8,4,6]{0,1,2:T(4,128)S(1)}, f32[8,4,6]{0,1,2:T(4,128)}, u32[]{:S(2)}) copy-start(f32[8,4,6]{0,1,2:T(4,128)} %param.9) | copy-start | bytes 2308
  3.0 11.8 %copy-start.3 = (s32[128,8,128]{2,1,0:T(8,128)S(1)}, s32[128,8,128]{2,1,0:T(8,128)}, u32[]{:S(2)}) copy-start(s32[128,8,128]{2,1,0:T(8,128)} %param.8) | copy-start | bytes 1572868
  5.9 22.2 %collective-permute-start = (f32[5,4,8,128]{3,2,1,0:T(8,128)S(1)}, f32[5,4,8,128]{3,2,1,0:T(8,128)S(1)}, u32[]{:S(2)}, u32[]{:S(2)}) collective-permute-start(f32[5,4,8,128]{3,2,1,0:T(8,128)S(1)} %get-tuple-element.175), channel_id=1, source_target_pairs={{0,4},{4,8},{8,12},{12,16},{16,20},{20,24},{24,28},{28,32},{32,36}... | collective-permute-start | bytes 245768 | tf_op jit(solution)/shard_map/ppermute | solution.py:23
  7.8 20.3 %collective-permute-start.1 = (f32[5,4,8,128]{3,2,1,0:T(8,128)S(1)}, f32[5,4,8,128]{3,2,1,0:T(8,128)S(1)}, u32[]{:S(2)}, u32[]{:S(2)}) collective-permute-start(f32[5,4,8,128]{3,2,1,0:T(8,128)S(1)} %get-tuple-element.176), channel_id=1, source_target_pairs={{4,0},{8,4},{12,8},{16,12},{20,16},{24,20},{28,24},{32,28},{36,32}... | collective-permute-start | bytes 245768 | tf_op jit(solution)/shard_map/ppermute | solution.py:24
  34.8 15.0 %collective-permute-start.2 = (f32[5,136,8,4]{1,2,3,0:T(8,128)S(1)}, f32[5,136,8,4]{1,2,3,0:T(8,128)}, u32[]{:S(2)}, u32[]{:S(2)}) collective-permute-start(f32[5,136,8,4]{1,2,3,0:T(8,128)S(1)} %copy.58), channel_id=1, source_target_pairs={{0,1},{1,2},{2,3},{4,5},{5,6},{6,7},{8,9},{9,10},{10,11},{12,13},{... | collective-permute-start | bytes 261128 | tf_op jit(solution)/shard_map/ppermute | solution.py:23
  44.6 11.0 %collective-permute-start.3 = (f32[5,136,8,4]{1,2,3,0:T(8,128)}, f32[5,136,8,4]{1,2,3,0:T(8,128)}, u32[]{:S(2)}, u32[]{:S(2)}) collective-permute-start(f32[5,136,8,4]{1,2,3,0:T(8,128)} %copy.59), channel_id=1, source_target_pairs={{1,0},{2,1},{3,2},{5,4},{6,5},{7,6},{9,8},{10,9},{11,10},{13,12},{... | collective-permute-start | bytes 261128 | tf_op jit(solution)/shard_map/ppermute | solution.py:24
  103.7 1.0 copy-start.4
  103.8 1.2 copy-start.5
  103.8 1.3 copy-start.6
  103.8 1.5 %copy-start.7 = (f32[1,131072]{1,0:T(1,128)S(1)}, f32[1,131072]{1,0:T(1,128)}, u32[]{:S(2)}) copy-start(f32[1,131072]{1,0:T(1,128)} %get-tuple-element.163) | copy-start | bytes 1572868
  103.8 1.6 %copy-start.8 = (f32[1,131072]{1,0:T(1,128)S(1)}, f32[1,131072]{1,0:T(1,128)}, u32[]{:S(2)}) copy-start(f32[1,131072]{1,0:T(1,128)} %get-tuple-element.164) | copy-start | bytes 1572868
  103.8 1.8 %copy-start.9 = (f32[1,131072]{1,0:T(1,128)S(1)}, f32[1,131072]{1,0:T(1,128)}, u32[]{:S(2)}) copy-start(f32[1,131072]{1,0:T(1,128)} %get-tuple-element.165) | copy-start | bytes 1572868
  104.0 3.0 %copy-start.2 = (f32[6,131072]{1,0:T(8,128)S(1)}, f32[6,131072]{1,0:T(8,128)}, u32[]{:S(2)}) copy-start(f32[6,131072]{1,0:T(8,128)} %convolution_bitcast_fusion.2) | copy-start | bytes 9437188
  105.6 4.2 %copy-start.1 = (f32[6,131072]{1,0:T(8,128)S(1)}, f32[6,131072]{1,0:T(8,128)}, u32[]{:S(2)}) copy-start(f32[6,131072]{1,0:T(8,128)} %convolution_bitcast_fusion.3) | copy-start | bytes 9437188
  107.0 2.8 %copy-start = (f32[6,131072]{1,0:T(8,128)S(1)}, f32[6,131072]{1,0:T(8,128)}, u32[]{:S(2)}) copy-start(f32[6,131072]{1,0:T(8,128)} %convolution_bitcast_fusion.1) | copy-start | bytes 9437188
where the time goes:
time: 147 us
  other arithmetic  60.8 us (41%)
  blocking collectives  29.6 us (20%)
  local copies, waits for them, and re-layouts  24 us (16%)
  starting transfers between devices  15.7 us (11%)
  matrix products  14.1 us (10%)
  waiting for transfers between devices  2.49 us (2%)
    add x3, other arithmetic, blur_valid(): running + weights[offset] * lax.slice_in_dim(volume, offset, offset + len...  40 us
    all_gather x2, blocking collectives, prefix(): pieces = jax.tree.map(lambda part: lax.all_gather(part, axis), value)  29.6 us
    dot_general x4, matrix products, on_device(): jnp.dot(jnp.transpose(tf_table[:, channel, :]), labels, precision=lax.Pre...  13.6 us
    add x2, other arithmetic, on_device(): linears.append(linear + coefficients[5])  8.28 us
    ppermute x2, starting transfers between devices, padded_2(): after = lax.ppermute(first, axis, down)  7.93 us
    ppermute x2, starting transfers between devices, padded_2(): before = lax.ppermute(last, axis, up)  7.78 us
    concatenate x2, other arithmetic, padded_2(): array = jnp.concatenate([before, array, after], axis=dim)  7.69 us
    slice x3, local copies, waits for them, and re-layouts, padded_2(): last = lax.slice_in_dim(array, length - width, length, axis=dim)  6.56 us
  transfers between devices with their start and end apart: 4, of which 1 were waited for; matrix products, arithmetic and copies ran while one was open for 17% of the time, Pallas kernels for 0%

commit v1 on v0

v1 whole, which is shorter than its diff:
```python
import functools
import math

import jax
import jax.numpy as jnp
import numpy as np
from jax import lax
from jax.experimental import pallas as pl
from jax.experimental.pallas import tpu as pltpu
from jax.sharding import PartitionSpec as P

CLASSES = 8
RADIUS = 4
SPLAT = 2.0
OPTICAL = 0.5
COLS, ROWS, DEPTH = 128, 8, 128
F32, BF16 = jnp.float32, jnp.bfloat16
VMEM = pltpu.VMEM


def splat_taps():
    raw = [
        math.exp(-((offset - RADIUS) ** 2) / (2.0 * SPLAT * SPLAT))
        for offset in range(2 * RADIUS + 1)
    ]
    norm_total = sum(raw)
    return [value / norm_total for value in raw]


W = splat_taps()


def tap(offset):
    return W[offset + RADIUS] if abs(offset) <= RADIUS else 0.0


def depth_matrix():
    full = np.zeros((DEPTH + 8, DEPTH), np.float64)
    targets = list(range(DEPTH)) + [-4, -3, -2, -1] + [DEPTH + i for i in range(4)]
    for row, target in enumerate(targets):
        for cell in range(DEPTH):
            full[row, cell] = tap(cell - target)
    high = full.astype(jnp.bfloat16)
    low = (full - high.astype(np.float64)).astype(jnp.bfloat16)
    top = np.concatenate([high, high], 1)
    bottom = np.concatenate([low, np.zeros_like(low)], 1)
    return np.concatenate([top, bottom], 0)


def symmetric(values):
    total = values[4] * W[4]
    for reach in range(1, RADIUS + 1):
        total = total + (values[4 - reach] + values[4 + reach]) * W[4 + reach]
    return total


def blur_rows(rows):
    out = []
    for target in range(ROWS):
        total = rows[target] * W[4]
        for reach in range(1, RADIUS + 1):
            low, high = target - reach, target + reach
            if low >= 0 and high < ROWS:
                total = total + (rows[low] + rows[high]) * W[4 + reach]
            elif low >= 0:
                total = total + rows[low] * W[4 + reach]
            elif high < ROWS:
                total = total + rows[high] * W[4 + reach]
        out.append(total)
    return out


def columns_kernel(table, counts, fields, classes, blurred, class_t, tables, density, mix):
    lane = lax.broadcasted_iota(jnp.int32, (ROWS, 128), 1)
    for channel in range(4):
        for coefficient in range(6):
            scale = 0.5 if channel < 3 else 1.0
            entry = jnp.zeros((ROWS, 128), F32)
            for label in range(CLASSES):
                entry = jnp.where(lane == label, table[label, channel, coefficient] * scale, entry)
            tables[channel * 6 + coefficient] = entry

    density[...] = jnp.log1p(counts[...].astype(F32))

    def block(source, field, first, lo, hi):
        def column(offset):
            if not lo <= offset < hi:
                return None
            return source(first + offset)

        near = {offset: column(offset) for offset in range(-4, 12)}
        for target in range(8):
            total = near[target] * W[4]
            for reach in range(1, RADIUS + 1):
                low, high = near[target - reach], near[target + reach]
                if low is not None and high is not None:
                    total = total + (low + high) * W[4 + reach]
                elif low is not None:
                    total = total + low * W[4 + reach]
                elif high is not None:
                    total = total + high * W[4 + reach]
            mix[pl.ds(target * 8, 8), :] = total
        rows = blur_rows([mix[pl.ds(row, 8, stride=8), :] for row in range(ROWS)])
        for row in range(ROWS):
            blurred[field, row, pl.ds(first, 8), :] = rows[row]

    def sweep(source, field):
        block(source, field, 0, 0, 12)

        def body(index, carry):
            block(source, field, pl.multiple_of(index * 8, 8), -4, 12)
            return carry

        lax.fori_loop(1, COLS // 8 - 1, body, 0)
        block(source, field, COLS - 8, -4, 8)

    sweep(lambda column: density[column], 0)

    def over_fields(field, carry):
        sweep(lambda column: fields[field, column], field + 1)
        return carry

    lax.fori_loop(0, 4, over_fields, 0)

    flat = classes.reshape(COLS * ROWS, DEPTH)
    flat_t = class_t.reshape(DEPTH * ROWS, COLS)
    for row in range(ROWS):
        plane = flat[pl.ds(row, COLS, stride=ROWS), :]
        flat_t[pl.ds(row, DEPTH, stride=ROWS), :] = plane.T


def depth_kernel(n_tile, blurred, left, right, matrix, smooth, outward, edge, mix):
    tile = lax.axis_index("tile")
    has_left = (tile > 0).astype(F32)
    has_right = (tile < n_tile - 1).astype(F32)
    for field in range(5):
        for j in range(4):
            total = left[field, j] * tap(-4)
            for h in range(j + 1, 4):
                total = total + left[field, h] * tap(h - 4 - j)
            mix[pl.ds(j * 8, 8), :] = total * has_left
            total = right[field, j] * tap(4)
            for h in range(j):
                total = total + right[field, h] * tap(4 + h - j)
            mix[pl.ds(32 + j * 8, 8), :] = total * has_right
        rows = blur_rows([mix[pl.ds(row, 8, stride=8), :] for row in range(ROWS)])
        for row in range(ROWS):
            edge[field, row] = rows[row]

    sub = lax.broadcasted_iota(jnp.int32, (8, 128), 0)
    is_left = sub < 4
    flat = smooth.reshape(5, DEPTH * ROWS, COLS)
    flat_out = outward.reshape(5, 8 * ROWS, COLS)

    def body(index, carry):
        field = index // 4
        pair = index % 4
        parts = []
        for j in range(2):
            row = pair * 2 + j
            extra = edge[field, row]
            plane = blurred[field, row]
            parts.append(plane[:8] + jnp.where(is_left, extra, 0.0))
            parts.append(plane[8:120])
            parts.append(plane[120:] + jnp.where(is_left, 0.0, extra))
        both = jnp.concatenate(parts, 0)
        high = both.astype(BF16)
        low = (both - high.astype(F32)).astype(BF16)
        stack = jnp.concatenate([high, low], 1)
        out = lax.dot_general(
            matrix[...], stack, (((1,), (1,)), ((), ())), preferred_element_type=F32
        )
        out = out[: DEPTH + 8] + out[DEPTH + 8 :]
        for j in range(2):
            row = pair * 2 + j
            half = out[:, j * 128 : (j + 1) * 128]
            flat[field, pl.ds(row, DEPTH, stride=ROWS), :] = half[:DEPTH]
            flat_out[field, pl.ds(row, 8, stride=ROWS), :] = half[DEPTH:]
        return carry

    lax.fori_loop(0, 20, body, 0)


def shade_cell(values, label, tables, scale, state):
    trans, s_sum, r_sum, g_sum, b_sum, step_sum = state
    linears = []
    for channel in range(4):
        entry = [
            jnp.take_along_axis(
                tables[channel * 6 + i], label, axis=1, mode="promise_in_bounds"
            )
            for i in range(6)
        ]
        linear = entry[0] * values[0] + entry[5]
        for i in range(1, 5):
            linear = linear + entry[i] * values[i]
        linears.append(linear)
    tints = [jnp.tanh(linear) for linear in linears[:3]]
    x = linears[3]
    t = jnp.exp(-jnp.abs(x))
    series = t * (1.0 - t * (1.0 / 2 - t * (1.0 / 3 - t * (1.0 / 4))))
    soft = jnp.maximum(x, 0.0) + jnp.where(t < 0.01, series, jnp.log(1.0 + t))
    step = soft * scale
    opacity = step * (
        1.0 - step * (1.0 / 2 - step * (1.0 / 6 - step * (1.0 / 24 - step * (1.0 / 120))))
    )
    shade = trans * opacity
    return (
        trans - shade,
        s_sum + shade,
        r_sum + shade * tints[0],
        g_sum + shade * tints[1],
        b_sum + shade * tints[2],
        step_sum + step,
    )


def fresh_state():
    zero = jnp.zeros((ROWS, COLS), F32)
    return (jnp.ones((ROWS, COLS), F32), zero, zero, zero, zero, zero)


def inner_kernel(scale, smooth, class_t, tables, out):
    unroll = 8

    def body(index, state):
        start = 4 + index * unroll
        for k in range(unroll):
            depth = start + k
            state = shade_cell(
                [smooth[f, depth] for f in range(5)], class_t[depth], tables, scale, state
            )
        return state

    state = lax.fori_loop(0, (DEPTH - 8) // unroll, body, fresh_state())
    for i in range(6):
        out[i] = state[i]


def edge_kernel(scale, n_slab, smooth, class_t, tables, inner, front, behind, out):
    slab = lax.axis_index("slab")
    has_front = (slab > 0).astype(F32)
    has_behind = (slab < n_slab - 1).astype(F32)
    state = fresh_state()
    for k in range(4):
        values = [smooth[f, k] + front[f, k] * has_front for f in range(5)]
        state = shade_cell(values, class_t[k], tables, scale, state)
    trans = state[0]
    state = (
        trans * inner[0],
        state[1] + trans * inner[1],
        state[2] + trans * inner[2],
        state[3] + trans * inner[3],
        state[4] + trans * inner[4],
        state[5] + inner[5],
    )
    for k in range(4):
        depth = DEPTH - 4 + k
        values = [smooth[f, depth] + behind[f, k] * has_behind for f in range(5)]
        state = shade_cell(values, class_t[depth], tables, scale, state)
    for i in range(3):
        out[i] = 0.5 * (state[1] + state[2 + i])
    out[3] = jnp.exp(-state[5])


def in_vmem(*arrays):
    return tuple(pltpu.with_memory_space_constraint(a, VMEM) for a in arrays)


SPEC = pl.BlockSpec(memory_space=VMEM)
SMEM_SPEC = pl.BlockSpec(memory_space=pltpu.SMEM)
PARAMS = pltpu.CompilerParams(vmem_limit_bytes=32 * 1024 * 1024)


def ring(value, axis, shift):
    count = lax.axis_size(axis)
    return lax.ppermute(value, axis, [(i, (i + shift) % count) for i in range(count)])


def on_device(counts, fields, class_ids, tf_table):
    n_tile, n_slab = lax.axis_size("tile"), lax.axis_size("slab")
    scale = OPTICAL / (DEPTH * n_slab)

    def side(start):
        dens = jnp.log1p(counts[start : start + RADIUS].astype(F32))
        return jnp.concatenate([dens[None], fields[:, start : start + RADIUS]], 0)

    from_left = ring(side(COLS - RADIUS), "tile", 1)
    from_right = ring(side(0), "tile", -1)

    blurred, class_t, tables = pl.pallas_call(
        columns_kernel,
        out_shape=[
            VMEM((5, ROWS, COLS, DEPTH), F32),
            VMEM((DEPTH, ROWS, COLS), jnp.int32),
            VMEM((24, ROWS, 128), F32),
        ],
        in_specs=[SMEM_SPEC, SPEC, SPEC, SPEC],
        out_specs=[SPEC] * 3,
        scratch_shapes=[VMEM((COLS, ROWS, DEPTH), F32), VMEM((64, 128), F32)],
        compiler_params=PARAMS,
        name="columns",
    )(tf_table, *in_vmem(counts, fields, class_ids))

    smooth, outward = pl.pallas_call(
        functools.partial(depth_kernel, n_tile),
        out_shape=[VMEM((5, DEPTH, ROWS, COLS), F32), VMEM((5, 8, ROWS, COLS), F32)],
        in_specs=[SPEC] * 4,
        out_specs=[SPEC] * 2,
        scratch_shapes=[VMEM((5, ROWS, 8, DEPTH), F32), VMEM((64, 128), F32)],
        compiler_params=PARAMS,
        name="depth",
    )(*in_vmem(blurred, from_left, from_right, jnp.asarray(depth_matrix())))

    from_behind = ring(outward[:, :4], "slab", -1)
    from_front = ring(outward[:, 4:], "slab", 1)

    inner = pl.pallas_call(
        functools.partial(inner_kernel, scale),
        out_shape=VMEM((6, ROWS, COLS), F32),
        in_specs=[SPEC] * 3,
        out_specs=SPEC,
        compiler_params=PARAMS,
        name="inner",
    )(*in_vmem(smooth, class_t, tables))

    pair = pl.pallas_call(
        functools.partial(edge_kernel, scale, n_slab),
        out_shape=VMEM((4, ROWS, COLS), F32),
        in_specs=[SPEC] * 6,
        out_specs=SPEC,
        compiler_params=PARAMS,
        name="edges",
    )(*in_vmem(smooth, class_t, tables, inner, from_front, from_behind))

    slab = lax.axis_index("slab")
    others = {shift: ring(pair, "slab", shift) for shift in range(1, n_slab)}
    front_rad = jnp.zeros((3, ROWS, COLS), F32)
    front_tra = jnp.ones((ROWS, COLS), F32)
    for shift in range(n_slab - 1, 0, -1):
        there = slab >= shift
        front_rad = front_rad + front_tra * jnp.where(there, others[shift][:3], 0.0)
        front_tra = front_tra * jnp.where(there, others[shift][3], 1.0)
    shown = front_rad + front_tra * pair[:3]
    alpha = 1.0 - front_tra * pair[3]
    return jnp.concatenate([shown, alpha[None]], 0)[None]


def solution(mesh):
    return jax.shard_map(
        on_device,
        mesh=mesh,
        in_specs=(
            P("tile", None, "slab"),
            P(None, "tile", None, "slab"),
            P("tile", None, "slab"),
            P(),
        ),
        out_specs=P("slab", None, None, "tile"),
        check_vma=False,
    )
```

time: 147 us -> 45 us (0.31)
  other arithmetic: 60.8 us -> 1.4 us
  blocking collectives: 29.6 us -> 0 us
  local copies, waits for them, and re-layouts: 24 us -> 5.41 us
  Pallas kernels: 0 us -> 14.5 us
  matrix products: 14.1 us -> 0 us
  starting transfers between devices: 15.7 us -> 20.4 us
    add x6 -> x1, other arithmetic: 48.3 us -> 0.01 us  [on_device(): shown = front_rad + front_tra * pair[:3]]
    all_gather x2 -> x0, blocking collectives: 29.6 us -> none  [prefix(): pieces = jax.tree.map(lambda part: lax.all_gather(part, axis), value)]
    pallas_call x0 -> x4, Pallas kernels: none -> 14.5 us  [the longest x1 4.88 us: on_device(): pl.pallas_call(functools.partial(inner_kernel, scale), out_shape=VMEM((6,...]
    dot_general x5 -> x0, matrix products: 14.1 us -> none  [the longest x4 13.6 us: on_device(): jnp.dot(jnp.transpose(tf_table[:, channel, :]), labels, precision=lax.Pre...]
    slice x7 -> x2, local copies, waits for them, and re-layouts: 14.3 us -> 0.93 us  [the longest x1 0.92 us: side(): return jnp.concatenate([dens[None], fields[:, start:start + RADIUS]], 0)]
    concatenate x3 -> x2, other arithmetic: 9.46 us -> 0.02 us  [side(): return jnp.concatenate([dens[None], fields[:, start:start + RADIUS]], 0)]
    ppermute x2 -> x0, local copies, waits for them, and re-layouts: 6.8 us -> none  [the longest x1 3.42 us: padded_2(): after = lax.ppermute(first, axis, down)]
    ppermute x4 -> x7, starting transfers between devices: 15.7 us -> 20.4 us  [ring(): lax.ppermute(value, axis, [(i, (i + shift) % count) for i in range(count)])]
  transfers between devices with their start and end apart: 4 -> 7, of which waited for: 1 -> 1; matrix products, arithmetic and copies ran while one was open for 17% -> 2% of each run, Pallas kernels for 0% -> 21%
where the time goes in v1:
time: 45 us; the launch traced here: 44.6 us
  starting transfers between devices  20.4 us (45%)
  Pallas kernels  14.5 us (32%)
  local copies, waits for them, and re-layouts  5.41 us (12%)
  waiting for transfers between devices  2.73 us (6%)
  other arithmetic  1.4 us (3%)
    ppermute x7, starting transfers between devices, ring(): lax.ppermute(value, axis, [(i, (i + shift) % count) for i in range(count)])  20.4 us
    pallas_call x1, Pallas kernels, on_device(): pl.pallas_call(functools.partial(inner_kernel, scale), out_shape=VMEM((6,...  4.88 us
    pallas_call x1, Pallas kernels, on_device(): pl.pallas_call(functools.partial(depth_kernel, n_tile), out_shape=[VMEM((...  4.83 us
    pallas_call x1, Pallas kernels, on_device(): pl.pallas_call(columns_kernel, out_shape=[VMEM((5, ROWS, COLS, DEPTH), F3...  4.5 us
    unnamed x9, local copies, waits for them, and re-layouts  4.48 us
    ppermute x7, waiting for transfers between devices, ring(): lax.ppermute(value, axis, [(i, (i + shift) % count) for i in range(count)])  2.73 us
    slice x1, local copies, waits for them, and re-layouts, side(): return jnp.concatenate([dens[None], fields[:, start:start + RADIUS]], 0)  0.92 us
  transfers between devices with their start and end apart: 7, of which 1 were waited for; matrix products, arithmetic and copies ran while one was open for 2% of the time, Pallas kernels for 21%

profile of v1, /device:TPU:24, one launch (start us, length us, event | category | flops | bytes accessed | tf_op | source)
XLA Modules:
  0.0 44.6 jit_solution(8134013253864651367)
XLA Ops:
  0.0 0.9 %fusion.11 = (f32[4,4,8,128]{3,2,1,0:T(8,128)S(1)}, f32[4,4,8,128]{3,2,1,0:T(8,128)S(1)}) fusion(f32[4,128,8,128]{3,2,1,0:T(8,128)} %fields.1), kind=kLoop, calls=%fused_computation.23 | loop fusion | bytes 262144 | tf_op jit(solution)/shard_map/slice | solution.py:286
  0.9 0.8 %log-plus-one_bitcast_fusion = (f32[1,4,8,128]{3,2,1,0:T(8,128)S(1)}, f32[1,4,8,128]{3,2,1,0:T(8,128)S(1)}) fusion(s32[128,8,128]{2,1,0:T(8,128)} %counts.1), kind=kLoop, calls=%fused_computation.3 | loop fusion | flops 8192 | bytes 65536 | tf_op jit(solution)/shard_map/broadcast_in_dim | solution.py:286
  1.7 0.1 collective-permute-start
  1.8 4.7 %collective-permute-start.1 = (f32[5,4,8,128]{3,2,1,0:T(8,128)S(1)}, f32[5,4,8,128]{3,2,1,0:T(8,128)S(1)}, u32[]{:S(2)}, u32[]{:S(2)}) collective-permute-start(f32[5,4,8,128]{3,2,1,0:T(8,128)S(1)} %pad_maximum_fusion.1), channel_id=1, source_target_pairs={{0,252},{4,0},{8,4},{12,8},{16,12},{20,16},{24,20},{28,24},{32,28}... | collective-permute-start | bytes 245768 | tf_op jit(solution)/shard_map/ppermute | solution.py:277
  6.5 0.8 %copy.6.table = f32[8,4,6]{2,1,0:T(4,128)S(1)} copy(f32[8,4,6]{0,1,2:T(4,128)} %param.8) | data formatting | bytes 1536 | tf_op args[3]
  7.3 1.6 %copy-done = f32[4,128,8,128]{3,2,1,0:T(8,128)S(1)} copy-done((f32[4,128,8,128]{3,2,1,0:T(8,128)S(1)}, f32[4,128,8,128]{3,2,1,0:T(8,128)}, u32[]{:S(2)}) %copy-start) | copy-done | bytes 2097176
  8.9 1.0 %copy-done.1 = s32[128,8,128]{2,1,0:T(8,128)S(1)} copy-done((s32[128,8,128]{2,1,0:T(8,128)S(1)}, s32[128,8,128]{2,1,0:T(8,128)}, u32[]{:S(2)}) %copy-start.1) | copy-done | bytes 524312
  10.0 1.0 %copy-done.2 = s32[128,8,128]{2,1,0:T(8,128)S(1)} copy-done((s32[128,8,128]{2,1,0:T(8,128)S(1)}, s32[128,8,128]{2,1,0:T(8,128)}, u32[]{:S(2)}) %copy-start.2) | copy-done | bytes 524312
  11.0 4.5 %columns.1 = (f32[5,8,128,128]{3,2,1,0:T(8,128)S(1)}, s32[128,8,128]{2,1,0:T(8,128)S(1)}, f32[24,8,128]{2,1,0:T(8,128)S(1)}) custom-call(f32[8,4,6]{2,1,0:T(4,128)S(1)} %copy.6.table, s32[128,8,128]{2,1,0:T(8,128)S(1)} %copy-done.1, f32[4,128,8,128]{3,2,1,0:T(8,128)S(1)} %copy-done, s32[128,8,128]{2,1,0:T(8,128)S(1)} %copy-done.2), custom_call_target="tpu_custom_call" | custom-call | tf_op jit(solution)/shard_map/columns/pallas_call | solution.py:291
  15.5 0.0 collective-permute-done.left
  15.5 0.0 collective-permute-done.1.right
  15.6 4.8 %depth.1 = (f32[5,128,8,128]{3,2,1,0:T(8,128)S(1)}, f32[5,8,8,128]{3,2,1,0:T(8,128)S(1)}) custom-call(f32[5,8,128,128]{3,2,1,0:T(8,128)S(1)} %get-tuple-element.10.blurred, f32[5,4,8,128]{3,2,1,0:T(8,128)S(1)} %collective-permute-done.left, f32[5,4,8,128]{3,2,1,0:T(8,128)S(1)} %collective-permute-done.1.right, bf16[272,256]{1,0:T(8,128)(2,1)S(1)} %copy-done.3), custom_call_target="tpu_custom_call" | custom-call | tf_op jit(solution)/shard_map/depth/pallas_call | solution.py:305
  20.4 3.3 %collective-permute-start.2 = (f32[5,4,8,128]{3,2,1,0:T(8,128)S(1)}, f32[5,4,8,128]{3,2,1,0:T(8,128)S(1)}, u32[]{:S(2)}, u32[]{:S(2)}) collective-permute-start(f32[5,4,8,128]{3,2,1,0:T(8,128)S(1)} %get-tuple-element.22), channel_id=1, source_target_pairs={{0,1},{1,2},{2,3},{3,0},{4,5},{5,6},{6,7},{7,4},{8,9},{9,10},{10,1... | collective-permute-start | bytes 245768 | tf_op jit(solution)/shard_map/ppermute | solution.py:277
  23.8 3.1 %collective-permute-start.3 = (f32[5,4,8,128]{3,2,1,0:T(8,128)S(1)}, f32[5,4,8,128]{3,2,1,0:T(8,128)S(1)}, u32[]{:S(2)}, u32[]{:S(2)}) collective-permute-start(f32[5,4,8,128]{3,2,1,0:T(8,128)S(1)} %get-tuple-element.21), channel_id=1, source_target_pairs={{0,3},{1,0},{2,1},{3,2},{4,7},{5,4},{6,5},{7,6},{8,11},{9,8},{10,9... | collective-permute-start | bytes 245768 | tf_op jit(solution)/shard_map/ppermute | solution.py:277
  26.9 4.9 %inner.1 = f32[6,8,128]{2,1,0:T(8,128)S(1)} custom-call(f32[5,128,8,128]{3,2,1,0:T(8,128)S(1)} %get-tuple-element.11.smooth, s32[128,8,128]{2,1,0:T(8,128)S(1)} %get-tuple-element.12.class_t, f32[24,8,128]{2,1,0:T(8,128)S(1)} %get-tuple-element.13.tables), custom_call_target="tpu_custom_call" | custom-call | tf_op jit(solution)/shard_map/inner/pallas_call | solution.py:318
  31.8 0.0 collective-permute-done.3.behind
  31.8 0.3 edges.1
  32.1 3.1 %collective-permute-start.6 = (f32[4,8,128]{2,1,0:T(8,128)S(1)}, f32[4,8,128]{2,1,0:T(8,128)S(1)}, u32[]{:S(2)}, u32[]{:S(2)}) collective-permute-start(f32[4,8,128]{2,1,0:T(8,128)S(1)} %edges.1), channel_id=1, source_target_pairs={{0,1},{1,2},{2,3},{3,0},{4,5},{5,6},{6,7},{7,4},{8,9},{9,10},{10,1... | collective-permute-start | bytes 49160 | tf_op jit(solution)/shard_map/ppermute | solution.py:277
  35.2 1.1 %collective-permute-start.4 = (f32[4,8,128]{2,1,0:T(8,128)S(1)}, f32[4,8,128]{2,1,0:T(8,128)S(1)}, u32[]{:S(2)}, u32[]{:S(2)}) collective-permute-start(f32[4,8,128]{2,1,0:T(8,128)S(1)} %edges.1), channel_id=1, source_target_pairs={{0,3},{1,0},{2,1},{3,2},{4,7},{5,4},{6,5},{7,6},{8,11},{9,8},{10,9... | collective-permute-start | bytes 49160 | tf_op jit(solution)/shard_map/ppermute | solution.py:277
  36.3 4.9 %collective-permute-start.5 = (f32[4,8,128]{2,1,0:T(8,128)S(1)}, f32[4,8,128]{2,1,0:T(8,128)S(1)}, u32[]{:S(2)}, u32[]{:S(2)}) collective-permute-start(f32[4,8,128]{2,1,0:T(8,128)S(1)} %edges.1), channel_id=1, source_target_pairs={{0,2},{1,3},{2,0},{3,1},{4,6},{5,7},{6,4},{7,5},{8,10},{9,11},{10,... | collective-permute-start | bytes 49160 | tf_op jit(solution)/shard_map/ppermute | solution.py:277
  41.3 0.0 collective-permute-done.6
  41.3 0.0 collective-permute-done.4
  41.3 2.7 %collective-permute-done.5 = f32[4,8,128]{2,1,0:T(8,128)S(1)} collective-permute-done((f32[4,8,128]{2,1,0:T(8,128)S(1)}, f32[4,8,128]{2,1,0:T(8,128)S(1)}, u32[]{:S(2)}, u32[]{:S(2)}) %collective-permute-start.5) | collective-permute-done | bytes 16416 | tf_op jit(solution)/shard_map/ppermute | solution.py:277
  44.0 0.6 %maximum_bitcast_fusion = f32[1,4,8,128]{3,2,1,0:T(8,128)} fusion(f32[1,8,128]{2,1,0:T(8,128)S(1)} %fusion.5, f32[3,8,128]{2,1,0:T(8,128)S(1)} %fusion), kind=kLoop, calls=%fused_computation.2 | loop fusion | flops 4096 | bytes 32768 | tf_op jit(solution)/shard_map/broadcast_in_dim | solution.py:346
  (12 shorter events, 0.1 us)
Async XLA Ops:
  0.0 15.5 %copy-start.3 = (bf16[272,256]{1,0:T(8,128)(2,1)S(1)}, bf16[272,256]{1,0:T(8,128)(2,1)}, u32[]{:S(2)}) copy-start(bf16[272,256]{1,0:T(8,128)(2,1)} %constant.6.clone.matrix) | copy-start | bytes 417796
  1.7 13.8 %collective-permute-start = (f32[5,4,8,128]{3,2,1,0:T(8,128)S(1)}, f32[5,4,8,128]{3,2,1,0:T(8,128)S(1)}, u32[]{:S(2)}, u32[]{:S(2)}) collective-permute-start(f32[5,4,8,128]{3,2,1,0:T(8,128)S(1)} %pad_maximum_fusion), channel_id=1, source_target_pairs={{0,4},{4,8},{8,12},{12,16},{16,20},{20,24},{24,28},{28,32},{32,36}... | collective-permute-start | bytes 245768 | tf_op jit(solution)/shard_map/ppermute | solution.py:277
  1.8 13.7 %collective-permute-start.1 = (f32[5,4,8,128]{3,2,1,0:T(8,128)S(1)}, f32[5,4,8,128]{3,2,1,0:T(8,128)S(1)}, u32[]{:S(2)}, u32[]{:S(2)}) collective-permute-start(f32[5,4,8,128]{3,2,1,0:T(8,128)S(1)} %pad_maximum_fusion.1), channel_id=1, source_target_pairs={{0,252},{4,0},{8,4},{12,8},{16,12},{20,16},{24,20},{28,24},{32,28}... | collective-permute-start | bytes 245768 | tf_op jit(solution)/shard_map/ppermute | solution.py:277
  7.3 1.6 %copy-start = (f32[4,128,8,128]{3,2,1,0:T(8,128)S(1)}, f32[4,128,8,128]{3,2,1,0:T(8,128)}, u32[]{:S(2)}) copy-start(f32[4,128,8,128]{3,2,1,0:T(8,128)} %fields.1) | copy-start | bytes 6291460
  8.9 1.0 %copy-start.1 = (s32[128,8,128]{2,1,0:T(8,128)S(1)}, s32[128,8,128]{2,1,0:T(8,128)}, u32[]{:S(2)}) copy-start(s32[128,8,128]{2,1,0:T(8,128)} %counts.1) | copy-start | bytes 1572868
  10.0 1.0 %copy-start.2 = (s32[128,8,128]{2,1,0:T(8,128)S(1)}, s32[128,8,128]{2,1,0:T(8,128)}, u32[]{:S(2)}) copy-start(s32[128,8,128]{2,1,0:T(8,128)} %classes.1) | copy-start | bytes 1572868
  20.4 11.4 %collective-permute-start.2 = (f32[5,4,8,128]{3,2,1,0:T(8,128)S(1)}, f32[5,4,8,128]{3,2,1,0:T(8,128)S(1)}, u32[]{:S(2)}, u32[]{:S(2)}) collective-permute-start(f32[5,4,8,128]{3,2,1,0:T(8,128)S(1)} %get-tuple-element.22), channel_id=1, source_target_pairs={{0,1},{1,2},{2,3},{3,0},{4,5},{5,6},{6,7},{7,4},{8,9},{9,10},{10,1... | collective-permute-start | bytes 245768 | tf_op jit(solution)/shard_map/ppermute | solution.py:277
  23.8 8.0 %collective-permute-start.3 = (f32[5,4,8,128]{3,2,1,0:T(8,128)S(1)}, f32[5,4,8,128]{3,2,1,0:T(8,128)S(1)}, u32[]{:S(2)}, u32[]{:S(2)}) collective-permute-start(f32[5,4,8,128]{3,2,1,0:T(8,128)S(1)} %get-tuple-element.21), channel_id=1, source_target_pairs={{0,3},{1,0},{2,1},{3,2},{4,7},{5,4},{6,5},{7,6},{8,11},{9,8},{10,9... | collective-permute-start | bytes 245768 | tf_op jit(solution)/shard_map/ppermute | solution.py:277
  32.1 9.1 %collective-permute-start.6 = (f32[4,8,128]{2,1,0:T(8,128)S(1)}, f32[4,8,128]{2,1,0:T(8,128)S(1)}, u32[]{:S(2)}, u32[]{:S(2)}) collective-permute-start(f32[4,8,128]{2,1,0:T(8,128)S(1)} %edges.1), channel_id=1, source_target_pairs={{0,1},{1,2},{2,3},{3,0},{4,5},{5,6},{6,7},{7,4},{8,9},{9,10},{10,1... | collective-permute-start | bytes 49160 | tf_op jit(solution)/shard_map/ppermute | solution.py:277
  35.2 6.1 %collective-permute-start.4 = (f32[4,8,128]{2,1,0:T(8,128)S(1)}, f32[4,8,128]{2,1,0:T(8,128)S(1)}, u32[]{:S(2)}, u32[]{:S(2)}) collective-permute-start(f32[4,8,128]{2,1,0:T(8,128)S(1)} %edges.1), channel_id=1, source_target_pairs={{0,3},{1,0},{2,1},{3,2},{4,7},{5,4},{6,5},{7,6},{8,11},{9,8},{10,9... | collective-permute-start | bytes 49160 | tf_op jit(solution)/shard_map/ppermute | solution.py:277
  36.3 7.6 %collective-permute-start.5 = (f32[4,8,128]{2,1,0:T(8,128)S(1)}, f32[4,8,128]{2,1,0:T(8,128)S(1)}, u32[]{:S(2)}, u32[]{:S(2)}) collective-permute-start(f32[4,8,128]{2,1,0:T(8,128)S(1)} %edges.1), channel_id=1, source_target_pairs={{0,2},{1,3},{2,0},{3,1},{4,6},{5,7},{6,4},{7,5},{8,10},{9,11},{10,... | collective-permute-start | bytes 49160 | tf_op jit(solution)/shard_map/ppermute | solution.py:277

commit v2 on v1

v2 whole, which is shorter than its diff:
```python
import functools
import math

import jax
import jax.numpy as jnp
import numpy as np
from jax import lax
from jax.experimental import pallas as pl
from jax.experimental.pallas import tpu as pltpu
from jax.sharding import PartitionSpec as P

CLASSES = 8
RADIUS = 4
SPLAT = 2.0
OPTICAL = 0.5
COLS, ROWS, DEPTH = 128, 8, 128
F32, BF16 = jnp.float32, jnp.bfloat16
VMEM = pltpu.VMEM


def splat_taps():
    raw = [
        math.exp(-((offset - RADIUS) ** 2) / (2.0 * SPLAT * SPLAT))
        for offset in range(2 * RADIUS + 1)
    ]
    norm_total = sum(raw)
    return [value / norm_total for value in raw]


W = splat_taps()


def tap(offset):
    return W[offset + RADIUS] if abs(offset) <= RADIUS else 0.0


def split_const(full):
    high = full.astype(jnp.bfloat16)
    return high, (full - high.astype(np.float64)).astype(jnp.bfloat16)


def depth_matrix():
    full = np.zeros((DEPTH + 8, DEPTH), np.float64)
    targets = list(range(DEPTH)) + [-4, -3, -2, -1] + [DEPTH + i for i in range(4)]
    for row, target in enumerate(targets):
        for cell in range(DEPTH):
            full[row, cell] = tap(cell - target)
    high, low = split_const(full)
    top = np.concatenate([high, high], 1)
    bottom = np.concatenate([low, np.zeros_like(low)], 1)
    return np.concatenate([top, bottom], 0)


def plane_matrix(targets, cells):
    full = np.zeros((ROWS, len(targets), len(cells), ROWS), np.float64)
    for to_row in range(ROWS):
        for i, target in enumerate(targets):
            for j, cell in enumerate(cells):
                for row in range(ROWS):
                    full[to_row, i, j, row] = tap(cell - target) * tap(row - to_row)
    return np.concatenate(split_const(full.reshape(ROWS * len(targets), len(cells) * ROWS)), 0)


WIDE = 24
INNER = COLS - 2 * RADIUS
RIM = list(range(-RADIUS, 8)) + list(range(COLS - 8, COLS + RADIUS))
RIM_TARGETS = list(range(COLS - RADIUS, COLS)) + list(range(RADIUS))


def split(value):
    high = value.astype(BF16)
    return high, (value - high.astype(F32)).astype(BF16)


def plane_blur(matrix, cells):
    rows = matrix.shape[0] // 2
    out = jnp.dot(
        matrix[...], jnp.concatenate(split(cells), 1), preferred_element_type=F32
    )
    return out[:rows, :DEPTH] + out[:rows, DEPTH:] + out[rows:, :DEPTH]


def pack_kernel(counts, fields, first, last, count_rows, sems):
    copies = []
    for i, (ref, start) in enumerate(((first, 0), (last, COLS - RADIUS))):
        copies.append(
            pltpu.make_async_copy(
                counts.at[pl.ds(start, RADIUS)], count_rows.at[i], sems.at[2 * i]
            )
        )
        copies.append(
            pltpu.make_async_copy(
                fields.at[:, pl.ds(start, RADIUS)], ref.at[pl.ds(1, 4)], sems.at[2 * i + 1]
            )
        )
    for copy in copies:
        copy.start()
    for copy in copies:
        copy.wait()
    first[0] = jnp.log(1.0 + count_rows[0].astype(F32))
    last[0] = jnp.log(1.0 + count_rows[1].astype(F32))


def columns_kernel(
    table, matrix, counts, fields, classes,
    blurred, rim, class_t, tables,
    count_v, field_v, class_v, density, sems,
):
    copies = [pltpu.make_async_copy(counts, count_v, sems.at[0])]
    for field in range(4):
        copies.append(
            pltpu.make_async_copy(fields.at[field], field_v.at[field], sems.at[field + 1])
        )
    copies.append(pltpu.make_async_copy(classes, class_v, sems.at[5]))
    for copy in copies:
        copy.start()

    lane = lax.broadcasted_iota(jnp.int32, (CLASSES, CLASSES), 1)
    row_index = lax.broadcasted_iota(jnp.int32, (CLASSES, CLASSES), 0)
    for channel in range(4):
        scale = 0.5 if channel < 3 else 1.0
        for coefficient in range(6):
            per_class = jnp.broadcast_to(
                table[coefficient, channel : channel + 1, :], (CLASSES, CLASSES)
            )
            column = jnp.sum(
                jnp.where(lane == row_index, per_class, 0.0), axis=1, keepdims=True
            )
            tables[channel * 6 + coefficient] = jnp.broadcast_to(column * scale, (CLASSES, 128))

    def sweep(source, field):
        rim[field, pl.ds(0, 64), :] = source[pl.ds(0, 64), :]
        rim[field, pl.ds(64, 64), :] = source[pl.ds((COLS - 8) * ROWS, 64), :]

        for step in range(INNER // WIDE):
            out = plane_blur(matrix, source[pl.ds(step * WIDE * ROWS, (WIDE + 8) * ROWS), :])
            for row in range(ROWS):
                blurred[field, row, pl.ds(step * WIDE, WIDE), :] = out[
                    row * WIDE : (row + 1) * WIDE
                ]

    copies[0].wait()
    density[...] = jnp.log(1.0 + count_v[...].astype(F32))
    sweep(density.reshape(COLS * ROWS, DEPTH), 0)

    for field in range(4):
        copies[field + 1].wait()
        sweep(field_v.at[field].reshape(COLS * ROWS, DEPTH), field + 1)

    copies[5].wait()
    flat = class_v.reshape(COLS * ROWS, DEPTH)
    flat_t = class_t.reshape(DEPTH * ROWS, COLS)
    for row in range(ROWS):
        plane = flat[pl.ds(row, COLS, stride=ROWS), :]
        flat_t[pl.ds(row, DEPTH, stride=ROWS), :] = pltpu.roll(plane.T, COLS - RADIUS, 1)


def depth_kernel(n_tile, blurred, rim, left, right, rim_matrix, matrix, smooth, outward, edge):
    tile = lax.axis_index("tile")
    has_left = (tile > 0).astype(F32)
    has_right = (tile < n_tile - 1).astype(F32)
    side = RADIUS * ROWS
    for field in range(5):
        cells = jnp.concatenate(
            [
                left[field].reshape(side, DEPTH) * has_left,
                rim[field],
                right[field].reshape(side, DEPTH) * has_right,
            ],
            0,
        )
        edge[field] = plane_blur(rim_matrix, cells).reshape(ROWS, 8, DEPTH)

    flat = smooth.reshape(5, DEPTH * ROWS, COLS)
    flat_out = outward.reshape(5, 8 * ROWS, COLS)

    def body(index, carry):
        field = index // 4
        pair = index % 4
        parts = []
        for j in range(2):
            parts += [blurred[field, pair * 2 + j], edge[field, pair * 2 + j]]
        stack = jnp.concatenate(split(jnp.concatenate(parts, 0)), 1)
        out = lax.dot_general(
            matrix[...], stack, (((1,), (1,)), ((), ())), preferred_element_type=F32
        )
        out = out[: DEPTH + 8] + out[DEPTH + 8 :]
        for j in range(2):
            row = pair * 2 + j
            half = out[:, j * 128 : (j + 1) * 128]
            flat[field, pl.ds(row, DEPTH, stride=ROWS), :] = half[:DEPTH]
            flat_out[field, pl.ds(row, 8, stride=ROWS), :] = half[DEPTH:]
        return carry

    lax.fori_loop(0, 20, body, 0, unroll=10)


def shade_cell(values, label, tables, scale, state):
    trans, s_sum, r_sum, g_sum, b_sum, step_sum = state
    linears = []
    for channel in range(4):
        entry = [
            jnp.take_along_axis(
                tables[channel * 6 + i], label, axis=0, mode="promise_in_bounds"
            )
            for i in range(6)
        ]
        linear = entry[0] * values[0] + entry[5]
        for i in range(1, 5):
            linear = linear + entry[i] * values[i]
        linears.append(linear)
    tints = [jnp.tanh(linear) for linear in linears[:3]]
    x = linears[3]
    t = jnp.exp(-jnp.abs(x))
    series = t * (1.0 - t * (1.0 / 2 - t * (1.0 / 3 - t * (1.0 / 4))))
    soft = jnp.maximum(x, 0.0) + jnp.where(t < 0.01, series, jnp.log(1.0 + t))
    step = soft * scale
    opacity = step * (
        1.0 - step * (1.0 / 2 - step * (1.0 / 6 - step * (1.0 / 24 - step * (1.0 / 120))))
    )
    shade = trans * opacity
    return (
        trans - shade,
        s_sum + shade,
        r_sum + shade * tints[0],
        g_sum + shade * tints[1],
        b_sum + shade * tints[2],
        step_sum + step,
    )


def fresh_state():
    zero = jnp.zeros((ROWS, COLS), F32)
    return (jnp.ones((ROWS, COLS), F32), zero, zero, zero, zero, zero)


def inner_kernel(scale, smooth, class_t, tables, out):
    unroll = 8

    def body(index, state):
        start = 4 + index * unroll
        for k in range(unroll):
            depth = start + k
            state = shade_cell(
                [smooth[f, depth] for f in range(5)], class_t[depth], tables, scale, state
            )
        return state

    state = lax.fori_loop(0, (DEPTH - 8) // unroll, body, fresh_state())
    for i in range(6):
        out[i] = state[i]


def edge_kernel(scale, n_slab, smooth, class_t, tables, inner, front, behind, out):
    slab = lax.axis_index("slab")
    has_front = (slab > 0).astype(F32)
    has_behind = (slab < n_slab - 1).astype(F32)
    state = fresh_state()
    for k in range(4):
        values = [smooth[f, k] + front[f, k] * has_front for f in range(5)]
        state = shade_cell(values, class_t[k], tables, scale, state)
    trans = state[0]
    state = (
        trans * inner[0],
        state[1] + trans * inner[1],
        state[2] + trans * inner[2],
        state[3] + trans * inner[3],
        state[4] + trans * inner[4],
        state[5] + inner[5],
    )
    for k in range(4):
        depth = DEPTH - 4 + k
        values = [smooth[f, depth] + behind[f, k] * has_behind for f in range(5)]
        state = shade_cell(values, class_t[depth], tables, scale, state)
    for i in range(3):
        out[i] = pltpu.roll(0.5 * (state[1] + state[2 + i]), RADIUS, 1)
    out[3] = pltpu.roll(jnp.exp(-state[5]), RADIUS, 1)


def in_vmem(*arrays):
    return tuple(pltpu.with_memory_space_constraint(a, VMEM) for a in arrays)


def in_hbm(*arrays):
    return tuple(pltpu.with_memory_space_constraint(a, pltpu.HBM) for a in arrays)


SPEC = pl.BlockSpec(memory_space=VMEM)
HBM_SPEC = pl.BlockSpec(memory_space=pltpu.HBM)
PARAMS = pltpu.CompilerParams(vmem_limit_bytes=32 * 1024 * 1024)


def ring(value, axis, shift):
    count = lax.axis_size(axis)
    return lax.ppermute(value, axis, [(i, (i + shift) % count) for i in range(count)])


def on_device(counts, fields, class_ids, tf_table):
    n_tile, n_slab = lax.axis_size("tile"), lax.axis_size("slab")
    scale = OPTICAL / (DEPTH * n_slab)

    first, last = pl.pallas_call(
        pack_kernel,
        out_shape=[VMEM((5, RADIUS, ROWS, DEPTH), F32)] * 2,
        in_specs=[HBM_SPEC] * 2,
        out_specs=[SPEC] * 2,
        scratch_shapes=[VMEM((2, RADIUS, ROWS, DEPTH), jnp.int32), pltpu.SemaphoreType.DMA((4,))],
        compiler_params=PARAMS,
        name="pack",
    )(*in_hbm(counts, fields))

    from_left = ring(last, "tile", 1)
    from_right = ring(first, "tile", -1)

    step_matrix = plane_matrix(list(range(RADIUS, RADIUS + WIDE)), list(range(WIDE + 8)))
    blurred, rim, class_t, tables = pl.pallas_call(
        columns_kernel,
        out_shape=[
            VMEM((5, ROWS, INNER, DEPTH), F32),
            VMEM((5, 16 * ROWS, DEPTH), F32),
            VMEM((DEPTH, ROWS, COLS), jnp.int32),
            VMEM((24, ROWS, 128), F32),
        ],
        in_specs=[SPEC] * 2 + [HBM_SPEC] * 3,
        out_specs=[SPEC] * 4,
        scratch_shapes=[
            VMEM((COLS, ROWS, DEPTH), jnp.int32),
            VMEM((4, COLS, ROWS, DEPTH), F32),
            VMEM((COLS, ROWS, DEPTH), jnp.int32),
            VMEM((COLS, ROWS, DEPTH), F32),
            pltpu.SemaphoreType.DMA((6,)),
        ],
        compiler_params=PARAMS,
        name="columns",
    )(*in_vmem(jnp.transpose(tf_table, (2, 1, 0)), jnp.asarray(step_matrix)), *in_hbm(counts, fields, class_ids))

    rim_matrix = plane_matrix(RIM_TARGETS, RIM)
    smooth, outward = pl.pallas_call(
        functools.partial(depth_kernel, n_tile),
        out_shape=[VMEM((5, DEPTH, ROWS, COLS), F32), VMEM((5, 8, ROWS, COLS), F32)],
        in_specs=[SPEC] * 6,
        out_specs=[SPEC] * 2,
        scratch_shapes=[VMEM((5, ROWS, 8, DEPTH), F32)],
        compiler_params=PARAMS,
        name="depth",
    )(
        *in_vmem(
            blurred, rim, from_left, from_right,
            jnp.asarray(rim_matrix), jnp.asarray(depth_matrix()),
        )
    )

    from_behind = ring(outward[:, :4], "slab", -1)
    from_front = ring(outward[:, 4:], "slab", 1)

    inner = pl.pallas_call(
        functools.partial(inner_kernel, scale),
        out_shape=VMEM((6, ROWS, COLS), F32),
        in_specs=[SPEC] * 3,
        out_specs=SPEC,
        compiler_params=PARAMS,
        name="inner",
    )(*in_vmem(smooth, class_t, tables))

    pair = pl.pallas_call(
        functools.partial(edge_kernel, scale, n_slab),
        out_shape=VMEM((4, ROWS, COLS), F32),
        in_specs=[SPEC] * 6,
        out_specs=SPEC,
        compiler_params=PARAMS,
        name="edges",
    )(*in_vmem(smooth, class_t, tables, inner, from_front, from_behind))

    slab = lax.axis_index("slab")
    others = {shift: ring(pair, "slab", shift) for shift in (2, 1, 3)}
    front_rad = jnp.zeros((3, ROWS, COLS), F32)
    front_tra = jnp.ones((ROWS, COLS), F32)
    for shift in (3, 2, 1):
        there = slab >= shift
        front_rad = front_rad + front_tra * jnp.where(there, others[shift][:3], 0.0)
        front_tra = front_tra * jnp.where(there, others[shift][3], 1.0)
    shown = front_rad + front_tra * pair[:3]
    alpha = 1.0 - front_tra * pair[3]
    return jnp.concatenate([shown, alpha[None]], 0)[None]


def solution(mesh):
    return jax.shard_map(
        on_device,
        mesh=mesh,
        in_specs=(
            P("tile", None, "slab"),
            P(None, "tile", None, "slab"),
            P("tile", None, "slab"),
            P(),
        ),
        out_specs=P("slab", None, None, "tile"),
        check_vma=False,
    )
```

time: 45 us -> 36.3 us (0.81)
  Pallas kernels: 14.5 us -> 8.93 us
  local copies, waits for them, and re-layouts: 5.41 us -> 0.03 us
  waiting for transfers between devices: 2.73 us -> 7.53 us
  starting transfers between devices: 20.4 us -> 19 us
  other arithmetic: 1.4 us -> 0.63 us
    ppermute x7, waiting for transfers between devices: 2.73 us -> 7.53 us  [ring(): lax.ppermute(value, axis, [(i, (i + shift) % count) for i in range(count)])]
    unnamed x9 -> x8, local copies, waits for them, and re-layouts: 4.48 us -> 0.02 us
    pallas_call x1, Pallas kernels: 4.83 us -> 1.71 us  [on_device(): pl.pallas_call(functools.partial(depth_kernel, n_tile), out_shape=[VMEM((...]
    pallas_call x1, Pallas kernels: 4.88 us -> 2.11 us  [on_device(): pl.pallas_call(functools.partial(inner_kernel, scale), out_shape=VMEM((6,...]
    ppermute x7, starting transfers between devices: 20.4 us -> 19 us  [ring(): lax.ppermute(value, axis, [(i, (i + shift) % count) for i in range(count)])]
    slice x1 -> x0, local copies, waits for them, and re-layouts: 0.92 us -> none  [side(): return jnp.concatenate([dens[None], fields[:, start:start + RADIUS]], 0)]
    broadcast_in_dim x1 -> x0, other arithmetic: 0.75 us -> none  [side(): return jnp.concatenate([dens[None], fields[:, start:start + RADIUS]], 0)]
    pallas_call x1 -> x2, Pallas kernels: 4.5 us -> 4.9 us  [the longest x1 3.89 us: on_device(): pl.pallas_call(columns_kernel, out_shape=[VMEM((5, ROWS, INNER, DEPTH), F...]
  transfers between devices with their start and end apart: 7 -> 7, of which waited for: 1 -> 4; matrix products, arithmetic and copies ran while one was open for 2% -> 0% of each run, Pallas kernels for 21% -> 17%
where the time goes in v2:
time: 36.3 us; the launch traced here: 36.2 us
  starting transfers between devices  19 us (52%)
  Pallas kernels  8.93 us (25%)
  waiting for transfers between devices  7.53 us (21%)
  other arithmetic  0.63 us (2%)
    ppermute x7, starting transfers between devices, ring(): lax.ppermute(value, axis, [(i, (i + shift) % count) for i in range(count)])  19 us
    ppermute x7, waiting for transfers between devices, ring(): lax.ppermute(value, axis, [(i, (i + shift) % count) for i in range(count)])  7.53 us
    pallas_call x1, Pallas kernels, on_device(): pl.pallas_call(columns_kernel, out_shape=[VMEM((5, ROWS, INNER, DEPTH), F...  3.89 us
    pallas_call x1, Pallas kernels, on_device(): pl.pallas_call(functools.partial(inner_kernel, scale), out_shape=VMEM((6,...  2.11 us
    pallas_call x1, Pallas kernels, on_device(): pl.pallas_call(functools.partial(depth_kernel, n_tile), out_shape=[VMEM((...  1.71 us
    pallas_call x1, Pallas kernels, on_device(): pl.pallas_call(pack_kernel, out_shape=[VMEM((5, RADIUS, ROWS, DEPTH), F32...  1.01 us
  transfers between devices with their start and end apart: 7, of which 4 were waited for; matrix products, arithmetic and copies ran while one was open for 0% of the time, Pallas kernels for 17%

profile of v2, /device:TPU:24, one launch (start us, length us, event | category | flops | bytes accessed | tf_op | source)
XLA Modules:
  0.0 36.2 jit_solution(5873408554589561850)
XLA Ops:
  0.0 0.0 copy-start.3
  0.0 1.0 %pack.1 = (f32[5,4,8,128]{3,2,1,0:T(8,128)S(1)}, f32[5,4,8,128]{3,2,1,0:T(8,128)S(1)}) custom-call(s32[128,8,128]{2,1,0:T(8,128)} %counts.3, f32[4,128,8,128]{3,2,1,0:T(8,128)} %fields.3), custom_call_target="tpu_custom_call" | custom-call | tf_op jit(solution)/shard_map/pack/pallas_call | solution.py:302
  1.0 0.1 collective-permute-start
  1.1 4.7 %collective-permute-start.1 = (f32[5,4,8,128]{3,2,1,0:T(8,128)S(1)}, f32[5,4,8,128]{3,2,1,0:T(8,128)S(1)}, u32[]{:S(2)}, u32[]{:S(2)}) collective-permute-start(f32[5,4,8,128]{3,2,1,0:T(8,128)S(1)} %get-tuple-element.16), channel_id=1, source_target_pairs={{0,252},{4,0},{8,4},{12,8},{16,12},{20,16},{24,20},{28,24},{32,28}... | collective-permute-start | bytes 245768 | tf_op jit(solution)/shard_map/ppermute | solution.py:295
  5.9 0.0 copy-done
  5.9 0.0 copy-done.3
  5.9 3.9 %columns.1 = (f32[5,8,120,128]{3,2,1,0:T(8,128)S(1)}, f32[5,128,128]{2,1,0:T(8,128)S(1)}, s32[128,8,128]{2,1,0:T(8,128)S(1)}, f32[24,8,128]{2,1,0:T(8,128)S(1)}) custom-call(f32[6,4,8]{2,1,0:T(4,128)S(1)} %bitcast.8, bf16[384,256]{1,0:T(8,128)(2,1)S(1)} %copy-done, s32[128,8,128]{2,1,0:T(8,128)} %counts.3, f32[4,128,8,128]{3,2,1,0:T(8,128)} %fields.3, ...), custom_call_target="tpu_custom_call" | custom-call | tf_op jit(solution)/shard_map/columns/pallas_call | solution.py:316
  9.8 0.0 collective-permute-done.left
  9.8 0.0 collective-permute-done.1.right
  9.8 0.0 copy-done.1
  9.8 1.7 %depth.1 = (f32[5,128,8,128]{3,2,1,0:T(8,128)S(1)}, f32[5,8,8,128]{3,2,1,0:T(8,128)S(1)}) custom-call(f32[5,8,120,128]{3,2,1,0:T(8,128)S(1)} %get-tuple-element.13.blurred, f32[5,128,128]{2,1,0:T(8,128)S(1)} %get-tuple-element.14.rim, f32[5,4,8,128]{3,2,1,0:T(8,128)S(1)} %collective-permute-done.left, f32[5,4,8,128]{3,2,1,0:T(8,128)S(1)} %collective-permute-done.1.right, ...), custom_call_target="tpu_custom_call" | custom-call | tf_op jit(solution)/shard_map/depth/pallas_call | solution.py:338
  11.5 3.4 %collective-permute-start.2 = (f32[5,4,8,128]{3,2,1,0:T(8,128)S(1)}, f32[5,4,8,128]{3,2,1,0:T(8,128)S(1)}, u32[]{:S(2)}, u32[]{:S(2)}) collective-permute-start(f32[5,4,8,128]{3,2,1,0:T(8,128)S(1)} %get-tuple-element.24), channel_id=1, source_target_pairs={{0,1},{1,2},{2,3},{3,0},{4,5},{5,6},{6,7},{7,4},{8,9},{9,10},{10,1... | collective-permute-start | bytes 245768 | tf_op jit(solution)/shard_map/ppermute | solution.py:295
  14.9 3.1 %collective-permute-start.3 = (f32[5,4,8,128]{3,2,1,0:T(8,128)S(1)}, f32[5,4,8,128]{3,2,1,0:T(8,128)S(1)}, u32[]{:S(2)}, u32[]{:S(2)}) collective-permute-start(f32[5,4,8,128]{3,2,1,0:T(8,128)S(1)} %get-tuple-element.23), channel_id=1, source_target_pairs={{0,3},{1,0},{2,1},{3,2},{4,7},{5,4},{6,5},{7,6},{8,11},{9,8},{10,9... | collective-permute-start | bytes 245768 | tf_op jit(solution)/shard_map/ppermute | solution.py:295
  18.0 2.1 %inner.1 = f32[6,8,128]{2,1,0:T(8,128)S(1)} custom-call(f32[5,128,8,128]{3,2,1,0:T(8,128)S(1)} %get-tuple-element.17.smooth, s32[128,8,128]{2,1,0:T(8,128)S(1)} %get-tuple-element.18.class_t, f32[24,8,128]{2,1,0:T(8,128)S(1)} %get-tuple-element.19.tables), custom_call_target="tpu_custom_call" | custom-call | tf_op jit(solution)/shard_map/inner/pallas_call | solution.py:356
  20.1 1.3 %collective-permute-done.2.front = f32[5,4,8,128]{3,2,1,0:T(8,128)S(1)} collective-permute-done((f32[5,4,8,128]{3,2,1,0:T(8,128)S(1)}, f32[5,4,8,128]{3,2,1,0:T(8,128)S(1)}, u32[]{:S(2)}, u32[]{:S(2)}) %collective-permute-start.2) | collective-permute-done | bytes 81952 | tf_op jit(solution)/shard_map/ppermute | solution.py:295
  21.5 0.3 collective-permute-done.3.behind
  21.8 0.2 edges.1
  22.0 2.8 %collective-permute-start.4 = (f32[4,8,128]{2,1,0:T(8,128)S(1)}, f32[4,8,128]{2,1,0:T(8,128)S(1)}, u32[]{:S(2)}, u32[]{:S(2)}) collective-permute-start(f32[4,8,128]{2,1,0:T(8,128)S(1)} %edges.1), channel_id=1, source_target_pairs={{0,3},{1,0},{2,1},{3,2},{4,7},{5,4},{6,5},{7,6},{8,11},{9,8},{10,9... | collective-permute-start | bytes 49160 | tf_op jit(solution)/shard_map/ppermute | solution.py:295
  24.8 5.0 %collective-permute-start.5 = (f32[4,8,128]{2,1,0:T(8,128)S(1)}, f32[4,8,128]{2,1,0:T(8,128)S(1)}, u32[]{:S(2)}, u32[]{:S(2)}) collective-permute-start(f32[4,8,128]{2,1,0:T(8,128)S(1)} %edges.1), channel_id=1, source_target_pairs={{0,2},{1,3},{2,0},{3,1},{4,6},{5,7},{6,4},{7,5},{8,10},{9,11},{10,... | collective-permute-start | bytes 49160 | tf_op jit(solution)/shard_map/ppermute | solution.py:295
  29.8 0.0 collective-permute-start.6
  29.8 0.0 collective-permute-done.4
  29.8 2.8 %collective-permute-done.5 = f32[4,8,128]{2,1,0:T(8,128)S(1)} collective-permute-done((f32[4,8,128]{2,1,0:T(8,128)S(1)}, f32[4,8,128]{2,1,0:T(8,128)S(1)}, u32[]{:S(2)}, u32[]{:S(2)}) %collective-permute-start.5) | collective-permute-done | bytes 16416 | tf_op jit(solution)/shard_map/ppermute | solution.py:295
  32.5 3.1 %collective-permute-done.6 = f32[4,8,128]{2,1,0:T(8,128)S(1)} collective-permute-done((f32[4,8,128]{2,1,0:T(8,128)S(1)}, f32[4,8,128]{2,1,0:T(8,128)S(1)}, u32[]{:S(2)}, u32[]{:S(2)}) %collective-permute-start.6) | collective-permute-done | bytes 16416 | tf_op jit(solution)/shard_map/ppermute | solution.py:295
  35.6 0.6 %maximum_bitcast_fusion = f32[1,4,8,128]{3,2,1,0:T(8,128)} fusion(f32[1,8,128]{2,1,0:T(8,128)S(1)} %fusion.5, f32[3,8,128]{2,1,0:T(8,128)S(1)} %fusion), kind=kLoop, calls=%fused_computation | loop fusion | flops 4096 | bytes 32768 | tf_op jit(solution)/shard_map/broadcast_in_dim | solution.py:384
  (8 shorter events, 0.0 us)
Async XLA Ops:
  0.0 5.9 %copy-start = (bf16[384,256]{1,0:T(8,128)(2,1)S(1)}, bf16[384,256]{1,0:T(8,128)(2,1)}, u32[]{:S(2)}) copy-start(bf16[384,256]{1,0:T(8,128)(2,1)} %constant.8.clone.matrix) | copy-start | bytes 589828
  0.0 9.8 %copy-start.1 = (bf16[272,256]{1,0:T(8,128)(2,1)S(1)}, bf16[272,256]{1,0:T(8,128)(2,1)}, u32[]{:S(2)}) copy-start(bf16[272,256]{1,0:T(8,128)(2,1)} %constant.23.clone.matrix) | copy-start | bytes 417796
  0.0 9.8 %copy-start.2 = (bf16[128,192]{1,0:T(8,128)(2,1)S(1)}, bf16[128,192]{1,0:T(8,128)(2,1)}, u32[]{:S(2)}) copy-start(bf16[128,192]{1,0:T(8,128)(2,1)} %constant.22.clone.rim_matrix) | copy-start | bytes 147460
  0.0 5.9 %copy-start.3 = (f32[8,4,6]{0,1,2:T(4,128)S(1)}, f32[8,4,6]{0,1,2:T(4,128)}, u32[]{:S(2)}) copy-start(f32[8,4,6]{0,1,2:T(4,128)} %param.10) | copy-start | bytes 2308
  1.0 8.7 %collective-permute-start = (f32[5,4,8,128]{3,2,1,0:T(8,128)S(1)}, f32[5,4,8,128]{3,2,1,0:T(8,128)S(1)}, u32[]{:S(2)}, u32[]{:S(2)}) collective-permute-start(f32[5,4,8,128]{3,2,1,0:T(8,128)S(1)} %get-tuple-element.15), channel_id=1, source_target_pairs={{0,4},{4,8},{8,12},{12,16},{16,20},{20,24},{24,28},{28,32},{32,36}... | collective-permute-start | bytes 245768 | tf_op jit(solution)/shard_map/ppermute | solution.py:295
  1.1 8.7 %collective-permute-start.1 = (f32[5,4,8,128]{3,2,1,0:T(8,128)S(1)}, f32[5,4,8,128]{3,2,1,0:T(8,128)S(1)}, u32[]{:S(2)}, u32[]{:S(2)}) collective-permute-start(f32[5,4,8,128]{3,2,1,0:T(8,128)S(1)} %get-tuple-element.16), channel_id=1, source_target_pairs={{0,252},{4,0},{8,4},{12,8},{16,12},{20,16},{24,20},{28,24},{32,28}... | collective-permute-start | bytes 245768 | tf_op jit(solution)/shard_map/ppermute | solution.py:295
  11.5 9.9 %collective-permute-start.2 = (f32[5,4,8,128]{3,2,1,0:T(8,128)S(1)}, f32[5,4,8,128]{3,2,1,0:T(8,128)S(1)}, u32[]{:S(2)}, u32[]{:S(2)}) collective-permute-start(f32[5,4,8,128]{3,2,1,0:T(8,128)S(1)} %get-tuple-element.24), channel_id=1, source_target_pairs={{0,1},{1,2},{2,3},{3,0},{4,5},{5,6},{6,7},{7,4},{8,9},{9,10},{10,1... | collective-permute-start | bytes 245768 | tf_op jit(solution)/shard_map/ppermute | solution.py:295
  14.9 6.9 %collective-permute-start.3 = (f32[5,4,8,128]{3,2,1,0:T(8,128)S(1)}, f32[5,4,8,128]{3,2,1,0:T(8,128)S(1)}, u32[]{:S(2)}, u32[]{:S(2)}) collective-permute-start(f32[5,4,8,128]{3,2,1,0:T(8,128)S(1)} %get-tuple-element.23), channel_id=1, source_target_pairs={{0,3},{1,0},{2,1},{3,2},{4,7},{5,4},{6,5},{7,6},{8,11},{9,8},{10,9... | collective-permute-start | bytes 245768 | tf_op jit(solution)/shard_map/ppermute | solution.py:295
  22.0 7.7 %collective-permute-start.4 = (f32[4,8,128]{2,1,0:T(8,128)S(1)}, f32[4,8,128]{2,1,0:T(8,128)S(1)}, u32[]{:S(2)}, u32[]{:S(2)}) collective-permute-start(f32[4,8,128]{2,1,0:T(8,128)S(1)} %edges.1), channel_id=1, source_target_pairs={{0,3},{1,0},{2,1},{3,2},{4,7},{5,4},{6,5},{7,6},{8,11},{9,8},{10,9... | collective-permute-start | bytes 49160 | tf_op jit(solution)/shard_map/ppermute | solution.py:295
  24.8 7.8 %collective-permute-start.5 = (f32[4,8,128]{2,1,0:T(8,128)S(1)}, f32[4,8,128]{2,1,0:T(8,128)S(1)}, u32[]{:S(2)}, u32[]{:S(2)}) collective-permute-start(f32[4,8,128]{2,1,0:T(8,128)S(1)} %edges.1), channel_id=1, source_target_pairs={{0,2},{1,3},{2,0},{3,1},{4,6},{5,7},{6,4},{7,5},{8,10},{9,11},{10,... | collective-permute-start | bytes 49160 | tf_op jit(solution)/shard_map/ppermute | solution.py:295
  29.8 5.8 %collective-permute-start.6 = (f32[4,8,128]{2,1,0:T(8,128)S(1)}, f32[4,8,128]{2,1,0:T(8,128)S(1)}, u32[]{:S(2)}, u32[]{:S(2)}) collective-permute-start(f32[4,8,128]{2,1,0:T(8,128)S(1)} %edges.1), channel_id=1, source_target_pairs={{0,1},{1,2},{2,3},{3,0},{4,5},{5,6},{6,7},{7,4},{8,9},{9,10},{10,1... | collective-permute-start | bytes 49160 | tf_op jit(solution)/shard_map/ppermute | solution.py:295

commit v3 on v2

v3 whole, which is shorter than its diff:
```python
import functools
import math

import jax
import jax.numpy as jnp
import numpy as np
from jax import lax
from jax.experimental import pallas as pl
from jax.experimental.pallas import tpu as pltpu
from jax.sharding import PartitionSpec as P

CLASSES = 8
RADIUS = 4
SPLAT = 2.0
OPTICAL = 0.5
COLS, ROWS, DEPTH = 128, 8, 128
F32, BF16 = jnp.float32, jnp.bfloat16
VMEM = pltpu.VMEM


def splat_taps():
    raw = [
        math.exp(-((offset - RADIUS) ** 2) / (2.0 * SPLAT * SPLAT))
        for offset in range(2 * RADIUS + 1)
    ]
    norm_total = sum(raw)
    return [value / norm_total for value in raw]


W = splat_taps()


def tap(offset):
    return W[offset + RADIUS] if abs(offset) <= RADIUS else 0.0


def split_const(full):
    high = full.astype(jnp.bfloat16)
    return high, (full - high.astype(np.float64)).astype(jnp.bfloat16)


def split_rows(full):
    high, low = split_const(full)
    top = np.concatenate([high, high], 1)
    bottom = np.concatenate([low, np.zeros_like(low)], 1)
    return np.concatenate([top, bottom], 0)


def depth_matrix(targets):
    return split_rows(
        np.array([[tap(cell - target) for cell in range(DEPTH)] for target in targets])
    )


def plane_matrix(targets, cells):
    full = np.zeros((ROWS, len(targets), len(cells), ROWS), np.float64)
    for to_row in range(ROWS):
        for i, target in enumerate(targets):
            for j, cell in enumerate(cells):
                for row in range(ROWS):
                    full[to_row, i, j, row] = tap(cell - target) * tap(row - to_row)
    return split_rows(full.reshape(ROWS * len(targets), len(cells) * ROWS))


WIDE = 8
INNER = COLS - 2 * RADIUS
FRONT_TARGETS = list(range(-RADIUS, RADIUS))
INNER_TARGETS = list(range(RADIUS, DEPTH - RADIUS))
BACK_TARGETS = list(range(DEPTH - RADIUS, DEPTH + RADIUS))
BODY = 112


def split(value):
    high = value.astype(BF16)
    return high, (value - high.astype(F32)).astype(BF16)


def plane_blur(matrix, stack):
    out = jnp.dot(matrix[...], stack, preferred_element_type=F32)
    rows = matrix.shape[0] // 2
    return out[:rows] + out[rows:]


def pack_kernel(counts, fields, far, near, count_rows, sems):
    even = lax.axis_index("tile") % 2 == 0
    copies = []
    for i, (ref, at_start) in enumerate(((far, even), (near, jnp.logical_not(even)))):
        cells = pl.ds(jnp.where(at_start, 0, COLS - RADIUS), RADIUS)
        copies.append(pltpu.make_async_copy(counts.at[cells], count_rows.at[i], sems.at[2 * i]))
        copies.append(
            pltpu.make_async_copy(fields.at[:, cells], ref.at[pl.ds(1, 4)], sems.at[2 * i + 1])
        )
    for copy in copies:
        copy.start()
    for copy in copies:
        copy.wait()
    far[0] = jnp.log(1.0 + count_rows[0].astype(F32))
    near[0] = jnp.log(1.0 + count_rows[1].astype(F32))


def columns_kernel(
    matrix, end_matrix, counts, fields, classes,
    bodies, last, rim, class_v, send,
    count_v, field_v, high, low, sems,
):
    copies = [pltpu.make_async_copy(counts, count_v, sems.at[0])]
    for field in range(4):
        copies.append(
            pltpu.make_async_copy(fields.at[field], field_v.at[field], sems.at[field + 1])
        )
    copies.append(pltpu.make_async_copy(classes, class_v, sems.at[5]))
    for copy in copies:
        copy.start()

    def prepare(source, field):
        rim[field, pl.ds(0, 64), :] = source[pl.ds(0, 64), :]
        rim[field, pl.ds(64, 64), :] = source[pl.ds((COLS - 8) * ROWS, 64), :]
        high[field], low[field] = split(source[...])

    def product(windows):
        sides = []
        for field, step in windows:
            cells = pl.ds(step * WIDE * ROWS, 2 * WIDE * ROWS)
            sides.append(jnp.concatenate([high[field, cells, :], low[field, cells, :]], 0))
        return plane_blur(matrix, jnp.concatenate(sides, 1))

    def sweep(field):
        for step in range(0, BODY // WIDE, 2):
            out = product([(field, step), (field, step + 1)])
            for row in range(ROWS):
                cut = out[row * WIDE : (row + 1) * WIDE]
                tile = jnp.concatenate([cut[:, :DEPTH], cut[:, DEPTH:]], 0)
                bodies[field * 4 + row // 2, row % 2, pl.ds(step * WIDE, 16)] = jnp.concatenate(
                    split(tile), 1
                )

    copies[0].wait()
    prepare(jnp.log(1.0 + count_v[...].astype(F32)).reshape(COLS * ROWS, DEPTH), 0)
    copies[1].wait()
    prepare(field_v.at[0].reshape(COLS * ROWS, DEPTH), 1)
    sweep(0)
    sweep(1)
    for field in range(1, 4):
        copies[field + 1].wait()
        prepare(field_v.at[field].reshape(COLS * ROWS, DEPTH), field + 1)
    for field in range(2, 5):
        sweep(field)
    for first in range(0, 5, 2):
        windows = [(field, BODY // WIDE) for field in range(first, min(first + 2, 5))]
        out = product(windows)
        for j, (field, _) in enumerate(windows):
            last[field] = out[:, j * DEPTH : (j + 1) * DEPTH].reshape(ROWS, WIDE, DEPTH)

    flat_send = send.reshape(40 * ROWS, COLS)
    own_matrix = end_matrix[lax.axis_index("tile") % 2]
    zero = jnp.zeros((8, DEPTH), F32)
    for index in range(20):
        field, pair = index // 4, index % 4
        parts = []
        for j in range(2):
            tail = jnp.concatenate([last[field, pair * 2 + j], zero], 0)
            parts += [bodies[index, j], jnp.concatenate(split(tail), 1)]
        out = depth_product(own_matrix, jnp.concatenate(parts, 0))
        for j in range(2):
            flat_send[pl.ds(field * 64 + pair * 2 + j, 8, stride=ROWS), :] = out[
                :, j * 128 : (j + 1) * 128
            ]
    copies[5].wait()


def depth_product(matrix, stack):
    out = lax.dot_general(
        matrix, stack, (((1,), (1,)), ((), ())), preferred_element_type=F32
    )
    half = matrix.shape[0] // 2
    return out[:half] + out[half:]


def rim_kernel(
    n_tile, table, class_v, last, rim, far, near, rim_matrix, matrix,
    class_t, tables, tails, send,
):
    lane = lax.broadcasted_iota(jnp.int32, (CLASSES, CLASSES), 1)
    row_index = lax.broadcasted_iota(jnp.int32, (CLASSES, CLASSES), 0)
    for channel in range(4):
        scale = 0.5 if channel < 3 else 1.0
        for coefficient in range(6):
            per_class = jnp.broadcast_to(
                table[coefficient, channel : channel + 1, :], (CLASSES, CLASSES)
            )
            column = jnp.sum(
                jnp.where(lane == row_index, per_class, 0.0), axis=1, keepdims=True
            )
            tables[channel * 6 + coefficient] = jnp.broadcast_to(column * scale, (CLASSES, 128))

    flat = class_v.reshape(COLS * ROWS, DEPTH)
    flat_t = class_t.reshape(DEPTH * ROWS, COLS)
    for row in range(ROWS):
        plane = flat[pl.ds(row, COLS, stride=ROWS), :]
        flat_t[pl.ds(row, DEPTH, stride=ROWS), :] = pltpu.roll(plane.T, COLS - RADIUS, 1)

    tile = lax.axis_index("tile")
    even = tile % 2 == 0
    has_left = (tile > 0).astype(F32)
    has_right = (tile < n_tile - 1).astype(F32)
    side = RADIUS * ROWS
    is_right = lax.broadcasted_iota(jnp.int32, (8 * ROWS, DEPTH), 0) % 8 < RADIUS
    edges = []
    for field in range(5):
        from_far = far[field].reshape(side, DEPTH)
        from_near = near[field].reshape(side, DEPTH)
        left = jnp.where(even, from_far, from_near) * has_left
        right = jnp.where(even, from_near, from_far) * has_right
        out = []
        for cells in ([left, rim[field, :64]], [rim[field, 64:], right]):
            parts = split(jnp.concatenate(cells, 0))
            out.append(jnp.concatenate(parts, 0))
        out = plane_blur(rim_matrix, jnp.concatenate(out, 1))
        out = jnp.where(is_right, out[:, DEPTH:], out[:, :DEPTH])
        edges.append(out)
        for row in range(ROWS):
            tail = jnp.concatenate(
                [last[field, row], out[row * 8 : (row + 1) * 8]], 0
            )
            tails[field * 4 + row // 2, row % 2] = jnp.concatenate(split(tail), 1)
    zero = jnp.zeros((64, DEPTH), F32)
    for first in range(0, 5, 2):
        parts = []
        for out in edges[first : first + 2]:
            parts += [out, zero]
        stack = jnp.concatenate(split(jnp.concatenate(parts, 0)), 1)
        out = depth_product(matrix[tile % 2], stack)
        for j in range(stack.shape[0] // 128):
            send[first + j] = out[:, j * 128 : (j + 1) * 128]
    for k in range(RADIUS):
        send[5 + k] = jnp.where(even, class_t[DEPTH - RADIUS + k], class_t[k]).astype(F32)


def shade_cell(values, label, tables, scale, state):
    trans, s_sum, r_sum, g_sum, b_sum, step_sum = state
    linears = []
    for channel in range(4):
        entry = [
            jnp.take_along_axis(
                tables[channel * 6 + i], label, axis=0, mode="promise_in_bounds"
            )
            for i in range(6)
        ]
        linear = entry[0] * values[0] + entry[5]
        for i in range(1, 5):
            linear = linear + entry[i] * values[i]
        linears.append(linear)
    tints = [jnp.tanh(linear) for linear in linears[:3]]
    x = linears[3]
    t = jnp.exp(-jnp.abs(x))
    series = t * (1.0 - t * (1.0 / 2 - t * (1.0 / 3 - t * (1.0 / 4))))
    soft = jnp.maximum(x, 0.0) + jnp.where(t < 0.01, series, jnp.log(1.0 + t))
    step = soft * scale
    opacity = step * (
        1.0 - step * (1.0 / 2 - step * (1.0 / 6 - step * (1.0 / 24 - step * (1.0 / 120))))
    )
    shade = trans * opacity
    return (
        trans - shade,
        s_sum + shade,
        r_sum + shade * tints[0],
        g_sum + shade * tints[1],
        b_sum + shade * tints[2],
        step_sum + step,
    )


def fresh_state():
    zero = jnp.zeros((ROWS, COLS), F32)
    return (jnp.ones((ROWS, COLS), F32), zero, zero, zero, zero, zero)


def join(near, far):
    trans = near[0]
    sums = [near[i] + trans * far[i] for i in range(1, 5)]
    return (trans * far[0], *sums, near[5] + far[5])


def choose(flag, one, other):
    return tuple(jnp.where(flag, a, b) for a, b in zip(one, other))


def inner_kernel(scale, bodies, tails, class_t, tables, matrix, out, halo, end, smooth):
    even = lax.axis_index("tile") % 2 == 0
    depths = len(INNER_TARGETS)
    flat = smooth.reshape(5, depths * ROWS, COLS)
    flat_halo = halo.reshape(5, 8 * ROWS, COLS)
    flat_end = end.reshape(5, RADIUS * ROWS, COLS)

    def blur(index, carry):
        field = index // 4
        pair = index % 4
        stack = jnp.concatenate(
            [bodies[index, 0], tails[index, 0], bodies[index, 1], tails[index, 1]], 0
        )
        product = depth_product(matrix[...], stack)
        front, back = product[:8], product[8 + depths :]
        keep = jnp.where(even, front, back)
        last = jnp.where(even, back[:4], front[4:])
        for j in range(2):
            row = pair * 2 + j
            lanes = slice(j * 128, (j + 1) * 128)
            flat[field, pl.ds(row, depths, stride=ROWS), :] = product[8 : 8 + depths, lanes]
            flat_halo[field, pl.ds(row, 8, stride=ROWS), :] = keep[:, lanes]
            flat_end[field, pl.ds(row, RADIUS, stride=ROWS), :] = last[:, lanes]
        return carry

    lax.fori_loop(0, 20, blur, 0, unroll=10)
    unroll = 12

    def body(index, state):
        for k in range(unroll):
            depth = index * unroll + k
            state = shade_cell(
                [smooth[f, depth] for f in range(5)],
                class_t[RADIUS + depth],
                tables,
                scale,
                state,
            )
        return state

    state = lax.fori_loop(0, depths // unroll, body, fresh_state())
    for i in range(6):
        out[i] = state[i]


def edge_kernel(
    scale, n_slab, halo, end_cells, class_t, tables, inner, place, given, given_rim,
    full, other, mine, total,
):
    slab = lax.axis_index("slab")
    even = lax.axis_index("tile") % 2 == 0
    is_first, is_last = slab == 0, slab == n_slab - 1
    alone = jnp.where(even, is_first, is_last)
    arrived = jnp.where(alone, 0.0, 1.0)
    step_one = jnp.where(jnp.logical_and(even, is_first), 0.0, scale)
    step_two = jnp.where(jnp.logical_and(jnp.logical_not(even), is_last), 0.0, scale)
    step_end = jnp.where(jnp.where(even, is_last, is_first), scale, 0.0)

    shape = (8, ROWS, COLS)
    own_row = lax.broadcasted_iota(jnp.int32, shape, 2) // 8 == lax.broadcasted_iota(
        jnp.int32, shape, 1
    )
    for f in range(5):
        sums = jnp.broadcast_to(given_rim[f][:, None, :], shape)
        sums = jnp.where(own_row, sums, 0.0).reshape(8 * ROWS, COLS)
        moved = jnp.dot(
            jnp.concatenate(split(sums), 1), place[...], preferred_element_type=F32
        ).reshape(shape)
        total[f] = halo[f] + (given[pl.ds(f * 8, 8)] + moved) * arrived

    one = two = end = fresh_state()
    for k in range(RADIUS):
        theirs = given_rim[5 + k].astype(jnp.int32)
        front, back = class_t[k], class_t[DEPTH - RADIUS + k]
        values = [total[f, k] for f in range(5)]
        one = shade_cell(values, jnp.where(even, theirs, back), tables, step_one, one)
        values = [total[f, RADIUS + k] for f in range(5)]
        two = shade_cell(values, jnp.where(even, front, theirs), tables, step_two, two)
        values = [end_cells[f, k] for f in range(5)]
        end = shade_cell(values, jnp.where(even, back, front), tables, step_end, end)
    middle = tuple(inner[i] for i in range(6))

    before = join(end, middle)
    odd_part = join(before, one)
    odd_full = join(odd_part, two)
    even_full = join(join(join(one, two), middle), end)
    all_of_it = choose(even, even_full, odd_full)

    def store(ref, state):
        for i in range(3):
            ref[i] = pltpu.roll(0.5 * (state[1] + state[2 + i]), RADIUS, 1)
        ref[3] = pltpu.roll(jnp.exp(-state[5]), RADIUS, 1)

    store(full, all_of_it)
    store(other, choose(jnp.logical_and(even, slab > 0), one, all_of_it))
    store(mine, choose(even, even_full, odd_part))


def in_vmem(*arrays):
    return tuple(pltpu.with_memory_space_constraint(a, VMEM) for a in arrays)


def in_hbm(*arrays):
    return tuple(pltpu.with_memory_space_constraint(a, pltpu.HBM) for a in arrays)


SPEC = pl.BlockSpec(memory_space=VMEM)
HBM_SPEC = pl.BlockSpec(memory_space=pltpu.HBM)
PARAMS = pltpu.CompilerParams(vmem_limit_bytes=32 * 1024 * 1024)


def cost(microseconds):
    return pl.CostEstimate(
        flops=int(microseconds * 1e9), bytes_accessed=int(microseconds * 3.6e6), transcendentals=0
    )


def permute(value, target):
    n_tile, n_slab = lax.axis_size("tile"), lax.axis_size("slab")
    pairs = []
    for t in range(n_tile):
        for s in range(n_slab):
            to_tile, to_slab = target(t, s)
            pairs.append((t * n_slab + s, to_tile * n_slab + to_slab))
    return lax.ppermute(value, ("tile", "slab"), pairs)


def on_device(counts, fields, class_ids, tf_table):
    n_tile, n_slab = lax.axis_size("tile"), lax.axis_size("slab")
    scale = OPTICAL / (DEPTH * n_slab)

    far, near = pl.pallas_call(
        pack_kernel,
        out_shape=[VMEM((5, RADIUS, ROWS, DEPTH), F32)] * 2,
        in_specs=[HBM_SPEC] * 2,
        out_specs=[SPEC] * 2,
        scratch_shapes=[VMEM((2, RADIUS, ROWS, DEPTH), jnp.int32), pltpu.SemaphoreType.DMA((4,))],
        compiler_params=PARAMS,
        cost_estimate=cost(1),
        name="pack",
    )(*in_hbm(counts, fields))

    def across(t, s):
        other = ((t + 1) ^ 1) - 1
        return (other, s) if 0 <= other < n_tile else (t, s ^ 1)

    far = permute(far, across)
    near = lax.ppermute(near, "tile", [(t, t ^ 1) for t in range(n_tile)])

    step_matrix = plane_matrix(list(range(RADIUS, RADIUS + WIDE)), list(range(2 * WIDE)))
    end_matrix = jnp.asarray(np.stack([depth_matrix(BACK_TARGETS), depth_matrix(FRONT_TARGETS)]))
    bodies, last, rim, class_v, send = pl.pallas_call(
        columns_kernel,
        out_shape=[
            VMEM((20, 2, BODY, 2 * DEPTH), BF16),
            VMEM((5, ROWS, WIDE, DEPTH), F32),
            VMEM((5, 16 * ROWS, DEPTH), F32),
            VMEM((COLS, ROWS, DEPTH), jnp.int32),
            VMEM((40, ROWS, COLS), F32),
        ],
        in_specs=[SPEC] * 2 + [HBM_SPEC] * 3,
        out_specs=[SPEC] * 5,
        scratch_shapes=[
            VMEM((COLS, ROWS, DEPTH), jnp.int32),
            VMEM((4, COLS, ROWS, DEPTH), F32),
            VMEM((5, COLS * ROWS, DEPTH), BF16),
            VMEM((5, COLS * ROWS, DEPTH), BF16),
            pltpu.SemaphoreType.DMA((6,)),
        ],
        compiler_params=PARAMS,
        cost_estimate=cost(3),
        name="columns",
    )(*in_vmem(jnp.asarray(step_matrix), end_matrix), *in_hbm(counts, fields, class_ids))

    def beside(t, s):
        to = s + 1 if t % 2 == 0 else s - 1
        return (t, to) if 0 <= to < n_slab else (t ^ 1, s)

    given = permute(send, beside)

    rim_matrix = plane_matrix(2 * list(range(RADIUS, 2 * RADIUS)), list(range(3 * RADIUS)))
    class_t, tables, tails, send_rim = pl.pallas_call(
        functools.partial(rim_kernel, n_tile),
        out_shape=[
            VMEM((DEPTH, ROWS, COLS), jnp.int32),
            VMEM((24, ROWS, 128), F32),
            VMEM((20, 2, COLS - BODY, 2 * DEPTH), BF16),
            VMEM((9, 8, 128), F32),
        ],
        in_specs=[SPEC] * 8,
        out_specs=[SPEC] * 4,
        compiler_params=PARAMS,
        cost_estimate=cost(1),
        name="rim",
    )(
        *in_vmem(
            jnp.transpose(tf_table, (2, 1, 0)), class_v, last, rim, far, near,
            jnp.asarray(rim_matrix), end_matrix,
        )
    )
    given_rim = permute(send_rim, beside)

    depths = len(INNER_TARGETS)
    inner, halo, end_cells = pl.pallas_call(
        functools.partial(inner_kernel, scale),
        out_shape=[
            VMEM((6, ROWS, COLS), F32),
            VMEM((5, 8, ROWS, COLS), F32),
            VMEM((5, RADIUS, ROWS, COLS), F32),
        ],
        in_specs=[SPEC] * 5,
        out_specs=[SPEC] * 3,
        scratch_shapes=[VMEM((5, depths, ROWS, COLS), F32)],
        compiler_params=PARAMS,
        cost_estimate=cost(3.5),
        name="inner",
    )(
        *in_vmem(
            bodies, tails, class_t, tables,
            jnp.asarray(depth_matrix(FRONT_TARGETS + INNER_TARGETS + BACK_TARGETS)),
        )
    )

    place = np.zeros((2, COLS, COLS), np.float32)
    for lane in range(64):
        place[:, lane, INNER + lane % 8] = 1.0
    full, other, mine = pl.pallas_call(
        functools.partial(edge_kernel, scale, n_slab),
        out_shape=[VMEM((4, ROWS, COLS), F32)] * 3,
        in_specs=[SPEC] * 8,
        out_specs=[SPEC] * 3,
        scratch_shapes=[VMEM((5, 8, ROWS, COLS), F32)],
        compiler_params=PARAMS,
        cost_estimate=cost(0.5),
        name="edges",
    )(
        *in_vmem(
            halo, end_cells, class_t, tables, inner,
            jnp.asarray(place.reshape(2 * COLS, COLS), BF16), given, given_rim,
        )
    )

    slab = lax.axis_index("slab")
    even = lax.axis_index("tile") % 2 == 0
    from_2, from_1, from_3 = (
        permute(full, lambda t, s: (t, (2, 3, 1, 0)[s])),
        permute(full, lambda t, s: (t, (s + 1) % n_slab)),
        permute(other, lambda t, s: (t, (s + 3) % n_slab)),
    )

    def only(flag, value):
        return jnp.where(flag, value[:3], 0.0), jnp.where(flag, value[3], 1.0)

    def over(near, far):
        return near[1] * far[0] + near[0], near[1] * far[1]

    last = slab == n_slab - 1
    seen = over(only(slab >= 2, from_2), only(slab >= 1, from_1))
    seen = over(seen, (mine[:3], mine[3]))
    seen = over(seen, only(jnp.logical_and(even, jnp.logical_not(last)), from_3))
    seen = over(only(last, from_3), seen)
    return jnp.concatenate([seen[0], (1.0 - seen[1])[None]], 0)[None]


def solution(mesh):
    return jax.shard_map(
        on_device,
        mesh=mesh,
        in_specs=(
            P("tile", None, "slab"),
            P(None, "tile", None, "slab"),
            P("tile", None, "slab"),
            P(),
        ),
        out_specs=P("slab", None, None, "tile"),
        check_vma=False,
    )
```

time: 36.3 us -> 29.8 us (0.82)
  waiting for transfers between devices: 7.53 us -> 1.73 us
  Pallas kernels: 8.93 us -> 8.43 us
    ppermute x7, waiting for transfers between devices: 7.53 us -> 1.73 us  [the longest x6 1.72 us: permute(): return lax.ppermute(value, ('tile', 'slab'), pairs)]
    pallas_call x4, Pallas kernels: 7.92 us -> 7.45 us  [the longest x1 3.44 us: on_device(): pl.pallas_call(functools.partial(inner_kernel, scale), out_shape=[VMEM((6...]
  transfers between devices with their start and end apart: 7 -> 7, of which waited for: 4 -> 1; matrix products, arithmetic and copies ran while one was open for 0% -> 0% of each run, Pallas kernels for 17% -> 24%
where the time goes in v3:
time: 29.8 us; the launch traced here: 29.7 us
  starting transfers between devices  18.7 us (63%)
  Pallas kernels  8.43 us (28%)
  waiting for transfers between devices  1.73 us (6%)
  other arithmetic  0.65 us (2%)
    ppermute x6, starting transfers between devices, permute(): return lax.ppermute(value, ('tile', 'slab'), pairs)  18.7 us
    pallas_call x1, Pallas kernels, on_device(): pl.pallas_call(functools.partial(inner_kernel, scale), out_shape=[VMEM((6...  3.44 us
    pallas_call x1, Pallas kernels, on_device(): pl.pallas_call(columns_kernel, out_shape=[VMEM((20, 2, BODY, 2 * DEPTH),...  3.15 us
    ppermute x6, waiting for transfers between devices, permute(): return lax.ppermute(value, ('tile', 'slab'), pairs)  1.72 us
    pallas_call x1, Pallas kernels, on_device(): pl.pallas_call(pack_kernel, out_shape=[VMEM((5, RADIUS, ROWS, DEPTH), F32...  0.98 us
    broadcast_in_dim x1, other arithmetic, on_device(): return jnp.concatenate([seen[0], (1.0 - seen[1])[None]], 0)[None]  0.61 us
  transfers between devices with their start and end apart: 7, of which 1 were waited for; matrix products, arithmetic and copies ran while one was open for 0% of the time, Pallas kernels for 24%

profile of v3, /device:TPU:24, one launch (start us, length us, event | category | flops | bytes accessed | tf_op | source)
XLA Modules:
  0.0 29.7 jit_solution(691872036659765488)
XLA Ops:
  0.0 1.0 %pack.1 = (f32[5,4,8,128]{3,2,1,0:T(8,128)S(1)}, f32[5,4,8,128]{3,2,1,0:T(8,128)S(1)}) custom-call(s32[128,8,128]{2,1,0:T(8,128)} %counts.3, f32[4,128,8,128]{3,2,1,0:T(8,128)} %fields.3), custom_call_target="tpu_custom_call" | custom-call | flops 1000000000 | bytes 3600000 | tf_op jit(solution)/shard_map/pack/pallas_call | solution.py:419
  1.0 3.8 %collective-permute-start = (f32[5,4,8,128]{3,2,1,0:T(8,128)S(1)}, f32[5,4,8,128]{3,2,1,0:T(8,128)S(1)}, u32[]{:S(2)}, u32[]{:S(2)}) collective-permute-start(f32[5,4,8,128]{3,2,1,0:T(8,128)S(1)} %get-tuple-element.26), channel_id=1, source_target_pairs={{0,1},{1,0},{2,3},{3,2},{4,8},{5,9},{6,10},{7,11},{8,4},{9,5},{10,... | collective-permute-start | bytes 245768 | tf_op jit(solution)/shard_map/ppermute | solution.py:412
  4.8 0.0 collective-permute-start.1
  4.8 0.0 copy-done.5
  4.8 3.2 %columns.1 = (bf16[20,2,112,256]{3,2,1,0:T(8,128)(2,1)S(1)}, f32[5,8,8,128]{3,2,1,0:T(8,128)S(1)}, f32[5,128,128]{2,1,0:T(8,128)S(1)}, s32[128,8,128]{2,1,0:T(8,128)S(1)}, f32[40,8,128]{2,1,0:T(8,128)S(1)}) custom-call(bf16[128,256]{1,0:T(8,128)(2,1)S(1)} %copy-done.4, bf16[2,16,256]{2,1,0:T(8,128)(2,1)S(1)} %copy-done.5, s32[128,8,128]{2,1,0:T(8,128)} %counts.3, ...), custom_call_target="tpu_custom_call" | custom-call | flops 3000000000 | bytes 10800000 | tf_op jit(solution)/shard_map/columns/pallas_call | solution.py:439
  8.0 0.0 copy-start.1
  8.0 3.4 %collective-permute-start.2 = (f32[40,8,128]{2,1,0:T(8,128)S(1)}, f32[40,8,128]{2,1,0:T(8,128)S(1)}, u32[]{:S(2)}, u32[]{:S(2)}) collective-permute-start(f32[40,8,128]{2,1,0:T(8,128)S(1)} %get-tuple-element.34), channel_id=1, source_target_pairs={{0,1},{1,2},{2,3},{3,7},{4,0},{5,4},{6,5},{7,6},{8,9},{9,10},{10,1... | collective-permute-start | bytes 491528 | tf_op jit(solution)/shard_map/ppermute | solution.py:412
  11.4 0.0 collective-permute-done.far
  11.4 0.0 collective-permute-done.1.near
  11.4 0.0 copy-done
  11.4 0.0 copy-done.3
  11.4 0.4 %rim.1 = (s32[128,8,128]{2,1,0:T(8,128)S(1)}, f32[24,8,128]{2,1,0:T(8,128)S(1)}, bf16[20,2,16,256]{3,2,1,0:T(8,128)(2,1)S(1)}, f32[9,8,128]{2,1,0:T(8,128)S(1)}) custom-call(f32[6,4,8]{2,1,0:T(4,128)S(1)} %bitcast.10, s32[128,8,128]{2,1,0:T(8,128)S(1)} %get-tuple-element.23.class_v, f32[5,8,8,128]{3,2,1,0:T(8,128)S(1)} %get-tuple-element.24.last, ...), custom_call_target="tpu_custom_call" | custom-call | flops 1000000000 | bytes 3600000 | tf_op jit(solution)/shard_map/rim/pallas_call | solution.py:469
  11.8 3.7 %collective-permute-start.3 = (f32[9,8,128]{2,1,0:T(8,128)S(1)}, f32[9,8,128]{2,1,0:T(8,128)S(1)}, u32[]{:S(2)}, u32[]{:S(2)}) collective-permute-start(f32[9,8,128]{2,1,0:T(8,128)S(1)} %get-tuple-element.35), channel_id=1, source_target_pairs={{0,1},{1,2},{2,3},{3,7},{4,0},{5,4},{6,5},{7,6},{8,9},{9,10},{10,1... | collective-permute-start | bytes 110600 | tf_op jit(solution)/shard_map/ppermute | solution.py:412
  15.5 3.4 %inner.1 = (f32[6,8,128]{2,1,0:T(8,128)S(1)}, f32[5,8,8,128]{3,2,1,0:T(8,128)S(1)}, f32[5,4,8,128]{3,2,1,0:T(8,128)S(1)}) custom-call(bf16[20,2,112,256]{3,2,1,0:T(8,128)(2,1)S(1)} %get-tuple-element.22.bodies, bf16[20,2,16,256]{3,2,1,0:T(8,128)(2,1)S(1)} %get-tuple-element.28.tails, s32[128,8,128]{2,1,0:T(8,128)S(1)} %get-tuple-element.29.class_t, ...), custom_call_target="tpu_custom_call" | custom-call | flops 3500000000 | bytes 12600000 | tf_op jit(solution)/shard_map/inner/pallas_call | solution.py:491
  18.9 0.0 collective-permute-done.3.given_rim
  18.9 0.0 collective-permute-done.2.given
  19.0 0.4 %edges.1 = (f32[4,8,128]{2,1,0:T(8,128)S(1)}, f32[4,8,128]{2,1,0:T(8,128)S(1)}, f32[4,8,128]{2,1,0:T(8,128)S(1)}) custom-call(f32[5,8,8,128]{3,2,1,0:T(8,128)S(1)} %get-tuple-element.31.halo, f32[5,4,8,128]{3,2,1,0:T(8,128)S(1)} %get-tuple-element.32.end_cells, s32[128,8,128]{2,1,0:T(8,128)S(1)} %get-tuple-element.29.class_t, ...), custom_call_target="tpu_custom_call" | custom-call | flops 500000000 | bytes 1800000 | tf_op jit(solution)/shard_map/edges/pallas_call | solution.py:514
  19.4 3.8 %collective-permute-start.5 = (f32[4,8,128]{2,1,0:T(8,128)S(1)}, f32[4,8,128]{2,1,0:T(8,128)S(1)}, u32[]{:S(2)}, u32[]{:S(2)}) collective-permute-start(f32[4,8,128]{2,1,0:T(8,128)S(1)} %get-tuple-element.37), channel_id=1, source_target_pairs={{0,2},{1,3},{2,1},{3,0},{4,6},{5,7},{6,5},{7,4},{8,10},{9,11},{10,... | collective-permute-start | bytes 49160 | tf_op jit(solution)/shard_map/ppermute | solution.py:412
  23.1 1.2 %collective-permute-start.6 = (f32[4,8,128]{2,1,0:T(8,128)S(1)}, f32[4,8,128]{2,1,0:T(8,128)S(1)}, u32[]{:S(2)}, u32[]{:S(2)}) collective-permute-start(f32[4,8,128]{2,1,0:T(8,128)S(1)} %get-tuple-element.37), channel_id=1, source_target_pairs={{0,1},{1,2},{2,3},{3,0},{4,5},{5,6},{6,7},{7,4},{8,9},{9,10},{10,1... | collective-permute-start | bytes 49160 | tf_op jit(solution)/shard_map/ppermute | solution.py:412
  24.4 2.9 %collective-permute-start.4 = (f32[4,8,128]{2,1,0:T(8,128)S(1)}, f32[4,8,128]{2,1,0:T(8,128)S(1)}, u32[]{:S(2)}, u32[]{:S(2)}) collective-permute-start(f32[4,8,128]{2,1,0:T(8,128)S(1)} %get-tuple-element.36), channel_id=1, source_target_pairs={{0,3},{1,0},{2,1},{3,2},{4,7},{5,4},{6,5},{7,6},{8,11},{9,8},{10,9... | collective-permute-start | bytes 49160 | tf_op jit(solution)/shard_map/ppermute | solution.py:412
  27.3 0.0 collective-permute-done.5
  27.3 1.7 %collective-permute-done.6 = f32[4,8,128]{2,1,0:T(8,128)S(1)} collective-permute-done((f32[4,8,128]{2,1,0:T(8,128)S(1)}, f32[4,8,128]{2,1,0:T(8,128)S(1)}, u32[]{:S(2)}, u32[]{:S(2)}) %collective-permute-start.6) | collective-permute-done | bytes 16416 | tf_op jit(solution)/shard_map/ppermute | solution.py:412
  29.0 0.0 collective-permute-done.4
  29.0 0.6 %maximum_bitcast_fusion = f32[1,4,8,128]{3,2,1,0:T(8,128)} fusion(f32[1,8,128]{2,1,0:T(8,128)S(1)} %get-tuple-element.42, f32[3,8,128]{2,1,0:T(8,128)S(1)} %fusion.4), kind=kLoop, calls=%fused_computation | loop fusion | flops 4096 | bytes 32768 | tf_op jit(solution)/shard_map/broadcast_in_dim | solution.py:549
  (11 shorter events, 0.1 us)
Async XLA Ops:
  0.0 4.8 %copy-start.5 = (bf16[2,16,256]{2,1,0:T(8,128)(2,1)S(1)}, bf16[2,16,256]{2,1,0:T(8,128)(2,1)}, u32[]{:S(2)}) copy-start(bf16[2,16,256]{2,1,0:T(8,128)(2,1)} %constant.41.clone.end_matrix.matrix) | copy-start | bytes 49156
  0.0 4.8 %copy-start.4 = (bf16[128,256]{1,0:T(8,128)(2,1)S(1)}, bf16[128,256]{1,0:T(8,128)(2,1)}, u32[]{:S(2)}) copy-start(bf16[128,256]{1,0:T(8,128)(2,1)} %constant.42.clone.matrix) | copy-start | bytes 196612
  1.0 10.4 %collective-permute-start = (f32[5,4,8,128]{3,2,1,0:T(8,128)S(1)}, f32[5,4,8,128]{3,2,1,0:T(8,128)S(1)}, u32[]{:S(2)}, u32[]{:S(2)}) collective-permute-start(f32[5,4,8,128]{3,2,1,0:T(8,128)S(1)} %get-tuple-element.26), channel_id=1, source_target_pairs={{0,1},{1,0},{2,3},{3,2},{4,8},{5,9},{6,10},{7,11},{8,4},{9,5},{10,... | collective-permute-start | bytes 245768 | tf_op jit(solution)/shard_map/ppermute | solution.py:412
  4.8 6.6 %copy-start = (f32[8,4,6]{0,1,2:T(4,128)S(1)}, f32[8,4,6]{0,1,2:T(4,128)}, u32[]{:S(2)}) copy-start(f32[8,4,6]{0,1,2:T(4,128)} %param.12) | copy-start | bytes 2308
  4.8 6.6 %copy-start.3 = (bf16[128,192]{1,0:T(8,128)(2,1)S(1)}, bf16[128,192]{1,0:T(8,128)(2,1)}, u32[]{:S(2)}) copy-start(bf16[128,192]{1,0:T(8,128)(2,1)} %constant.43.clone.rim_matrix) | copy-start | bytes 147460
  4.8 6.5 %collective-permute-start.1 = (f32[5,4,8,128]{3,2,1,0:T(8,128)S(1)}, f32[5,4,8,128]{3,2,1,0:T(8,128)S(1)}, u32[]{:S(2)}, u32[]{:S(2)}) collective-permute-start(f32[5,4,8,128]{3,2,1,0:T(8,128)S(1)} %get-tuple-element.27), channel_id=1, source_target_pairs={{0,4},{4,0},{8,12},{12,8},{16,20},{20,16},{24,28},{28,24},{32,36},... | collective-permute-start | bytes 245768 | tf_op jit(solution)/shard_map/ppermute | solution.py:435
  8.0 7.5 %copy-start.1 = (bf16[272,256]{1,0:T(8,128)(2,1)S(1)}, bf16[272,256]{1,0:T(8,128)(2,1)}, u32[]{:S(2)}) copy-start(bf16[272,256]{1,0:T(8,128)(2,1)} %constant.44.clone.matrix) | copy-start | bytes 417796
  8.0 10.9 %collective-permute-start.2 = (f32[40,8,128]{2,1,0:T(8,128)S(1)}, f32[40,8,128]{2,1,0:T(8,128)S(1)}, u32[]{:S(2)}, u32[]{:S(2)}) collective-permute-start(f32[40,8,128]{2,1,0:T(8,128)S(1)} %get-tuple-element.34), channel_id=1, source_target_pairs={{0,1},{1,2},{2,3},{3,7},{4,0},{5,4},{6,5},{7,6},{8,9},{9,10},{10,1... | collective-permute-start | bytes 491528 | tf_op jit(solution)/shard_map/ppermute | solution.py:412
  11.8 7.1 %collective-permute-start.3 = (f32[9,8,128]{2,1,0:T(8,128)S(1)}, f32[9,8,128]{2,1,0:T(8,128)S(1)}, u32[]{:S(2)}, u32[]{:S(2)}) collective-permute-start(f32[9,8,128]{2,1,0:T(8,128)S(1)} %get-tuple-element.35), channel_id=1, source_target_pairs={{0,1},{1,2},{2,3},{3,7},{4,0},{5,4},{6,5},{7,6},{8,9},{9,10},{10,1... | collective-permute-start | bytes 110600 | tf_op jit(solution)/shard_map/ppermute | solution.py:412
  15.5 3.5 %copy-start.2 = (bf16[256,128]{1,0:T(8,128)(2,1)S(1)}, bf16[256,128]{1,0:T(8,128)(2,1)}, u32[]{:S(2)}) copy-start(bf16[256,128]{1,0:T(8,128)(2,1)} %constant.45.clone.place) | copy-start | bytes 196612
  19.4 7.9 %collective-permute-start.5 = (f32[4,8,128]{2,1,0:T(8,128)S(1)}, f32[4,8,128]{2,1,0:T(8,128)S(1)}, u32[]{:S(2)}, u32[]{:S(2)}) collective-permute-start(f32[4,8,128]{2,1,0:T(8,128)S(1)} %get-tuple-element.37), channel_id=1, source_target_pairs={{0,2},{1,3},{2,1},{3,0},{4,6},{5,7},{6,5},{7,4},{8,10},{9,11},{10,... | collective-permute-start | bytes 49160 | tf_op jit(solution)/shard_map/ppermute | solution.py:412
  23.1 5.8 %collective-permute-start.6 = (f32[4,8,128]{2,1,0:T(8,128)S(1)}, f32[4,8,128]{2,1,0:T(8,128)S(1)}, u32[]{:S(2)}, u32[]{:S(2)}) collective-permute-start(f32[4,8,128]{2,1,0:T(8,128)S(1)} %get-tuple-element.37), channel_id=1, source_target_pairs={{0,1},{1,2},{2,3},{3,0},{4,5},{5,6},{6,7},{7,4},{8,9},{9,10},{10,1... | collective-permute-start | bytes 49160 | tf_op jit(solution)/shard_map/ppermute | solution.py:412
  24.4 4.6 %collective-permute-start.4 = (f32[4,8,128]{2,1,0:T(8,128)S(1)}, f32[4,8,128]{2,1,0:T(8,128)S(1)}, u32[]{:S(2)}, u32[]{:S(2)}) collective-permute-start(f32[4,8,128]{2,1,0:T(8,128)S(1)} %get-tuple-element.36), channel_id=1, source_target_pairs={{0,3},{1,0},{2,1},{3,2},{4,7},{5,4},{6,5},{7,6},{8,11},{9,8},{10,9... | collective-permute-start | bytes 49160 | tf_op jit(solution)/shard_map/ppermute | solution.py:412

commit v4 on v3

--- a/solution.py
+++ b/solution.py
@@ -28,6 +28,10 @@
 
 
 W = splat_taps()
+
+
+def shades_forward(tile):
+    return tile % 2 == 1
 
 
 def tap(offset):
@@ -152,7 +156,7 @@
             last[field] = out[:, j * DEPTH : (j + 1) * DEPTH].reshape(ROWS, WIDE, DEPTH)
 
     flat_send = send.reshape(40 * ROWS, COLS)
-    own_matrix = end_matrix[lax.axis_index("tile") % 2]
+    own_matrix = end_matrix[jnp.where(shades_forward(lax.axis_index("tile")), 0, 1)]
     zero = jnp.zeros((8, DEPTH), F32)
     for index in range(20):
         field, pair = index // 4, index % 4
@@ -201,6 +205,7 @@
 
     tile = lax.axis_index("tile")
     even = tile % 2 == 0
+    forward = shades_forward(tile)
     has_left = (tile > 0).astype(F32)
     has_right = (tile < n_tile - 1).astype(F32)
     side = RADIUS * ROWS
@@ -229,11 +234,11 @@
         for out in edges[first : first + 2]:
             parts += [out, zero]
         stack = jnp.concatenate(split(jnp.concatenate(parts, 0)), 1)
-        out = depth_product(matrix[tile % 2], stack)
+        out = depth_product(matrix[jnp.where(forward, 0, 1)], stack)
         for j in range(stack.shape[0] // 128):
             send[first + j] = out[:, j * 128 : (j + 1) * 128]
     for k in range(RADIUS):
-        send[5 + k] = jnp.where(even, class_t[DEPTH - RADIUS + k], class_t[k]).astype(F32)
+        send[5 + k] = jnp.where(forward, class_t[DEPTH - RADIUS + k], class_t[k]).astype(F32)
 
 
 def shade_cell(values, label, tables, scale, state):
@@ -286,7 +291,7 @@
 
 
 def inner_kernel(scale, bodies, tails, class_t, tables, matrix, out, halo, end, smooth):
-    even = lax.axis_index("tile") % 2 == 0
+    forward = shades_forward(lax.axis_index("tile"))
     depths = len(INNER_TARGETS)
     flat = smooth.reshape(5, depths * ROWS, COLS)
     flat_halo = halo.reshape(5, 8 * ROWS, COLS)
@@ -300,8 +305,8 @@
         )
         product = depth_product(matrix[...], stack)
         front, back = product[:8], product[8 + depths :]
-        keep = jnp.where(even, front, back)
-        last = jnp.where(even, back[:4], front[4:])
+        keep = jnp.where(forward, front, back)
+        last = jnp.where(forward, back[:4], front[4:])
         for j in range(2):
             row = pair * 2 + j
             lanes = slice(j * 128, (j + 1) * 128)
@@ -332,16 +337,16 @@
 
 def edge_kernel(
     scale, n_slab, halo, end_cells, class_t, tables, inner, place, given, given_rim,
-    full, other, mine, total,
+    full, to_two, to_three, mine, total,
 ):
     slab = lax.axis_index("slab")
-    even = lax.axis_index("tile") % 2 == 0
+    forward = shades_forward(lax.axis_index("tile"))
     is_first, is_last = slab == 0, slab == n_slab - 1
-    alone = jnp.where(even, is_first, is_last)
+    alone = jnp.where(forward, is_first, is_last)
     arrived = jnp.where(alone, 0.0, 1.0)
-    step_one = jnp.where(jnp.logical_and(even, is_first), 0.0, scale)
-    step_two = jnp.where(jnp.logical_and(jnp.logical_not(even), is_last), 0.0, scale)
-    step_end = jnp.where(jnp.where(even, is_last, is_first), scale, 0.0)
+    step_one = jnp.where(jnp.logical_and(forward, is_first), 0.0, scale)
+    step_two = jnp.where(jnp.logical_and(jnp.logical_not(forward), is_last), 0.0, scale)
+    step_end = jnp.where(jnp.where(forward, is_last, is_first), scale, 0.0)
 
     shape = (8, ROWS, COLS)
     own_row = lax.broadcasted_iota(jnp.int32, shape, 2) // 8 == lax.broadcasted_iota(
@@ -360,18 +365,18 @@
         theirs = given_rim[5 + k].astype(jnp.int32)
         front, back = class_t[k], class_t[DEPTH - RADIUS + k]
         values = [total[f, k] for f in range(5)]
-        one = shade_cell(values, jnp.where(even, theirs, back), tables, step_one, one)
+        one = shade_cell(values, jnp.where(forward, theirs, back), tables, step_one, one)
         values = [total[f, RADIUS + k] for f in range(5)]
-        two = shade_cell(values, jnp.where(even, front, theirs), tables, step_two, two)
+        two = shade_cell(values, jnp.where(forward, front, theirs), tables, step_two, two)
         values = [end_cells[f, k] for f in range(5)]
-        end = shade_cell(values, jnp.where(even, back, front), tables, step_end, end)
+        end = shade_cell(values, jnp.where(forward, back, front), tables, step_end, end)
     middle = tuple(inner[i] for i in range(6))
 
     before = join(end, middle)
-    odd_part = join(before, one)
-    odd_full = join(odd_part, two)
-    even_full = join(join(join(one, two), middle), end)
-    all_of_it = choose(even, even_full, odd_full)
+    backward_part = join(before, one)
+    backward_full = join(backward_part, two)
+    forward_full = join(join(join(one, two), middle), end)
+    all_of_it = choose(forward, forward_full, backward_full)
 
     def store(ref, state):
         for i in range(3):
@@ -379,8 +384,37 @@
         ref[3] = pltpu.roll(jnp.exp(-state[5]), RADIUS, 1)
 
     store(full, all_of_it)
-    store(other, choose(jnp.logical_and(even, slab > 0), one, all_of_it))
-    store(mine, choose(even, even_full, odd_part))
+    store(to_two, choose(jnp.logical_and(forward, slab % 2 == 1), one, all_of_it))
+    store(to_three, choose(jnp.logical_and(forward, slab >= 2), one, all_of_it))
+    store(mine, choose(forward, forward_full, backward_part))
+
+
+def pair(ref):
+    return [ref[i] for i in range(4)]
+
+
+def over(near, far):
+    return [near[i] + near[3] * far[i] for i in range(3)] + [near[3] * far[3]]
+
+
+def only(flag, value):
+    return [jnp.where(flag, value[i], 0.0) for i in range(3)] + [jnp.where(flag, value[3], 1.0)]
+
+
+def final_kernel(got_one, got_two, got_three, mine, out):
+    slab = lax.axis_index("slab")
+    forward = shades_forward(lax.axis_index("tile"))
+    by_one, by_two, by_three = pair(got_one), pair(got_two), pair(got_three)
+    total = only(slab == 3, by_one)
+    total = over(total, only(slab >= 2, by_three))
+    total = over(total, only(jnp.logical_and(forward, slab == 2), by_one))
+    total = over(total, only(jnp.where(forward, slab % 2 == 1, slab >= 1), by_two))
+    total = over(total, pair(mine))
+    total = over(total, only(jnp.logical_and(forward, slab % 2 == 0), by_two))
+    total = over(total, only(jnp.logical_and(forward, slab == 1), by_three))
+    for i in range(3):
+        out[0, i] = total[i]
+    out[0, 3] = 1.0 - total[3]
 
 
 def in_vmem(*arrays):
@@ -460,7 +494,7 @@
     )(*in_vmem(jnp.asarray(step_matrix), end_matrix), *in_hbm(counts, fields, class_ids))
 
     def beside(t, s):
-        to = s + 1 if t % 2 == 0 else s - 1
+        to = s + 1 if shades_forward(t) else s - 1
         return (t, to) if 0 <= to < n_slab else (t ^ 1, s)
 
     given = permute(send, beside)
@@ -511,11 +545,11 @@
     place = np.zeros((2, COLS, COLS), np.float32)
     for lane in range(64):
         place[:, lane, INNER + lane % 8] = 1.0
-    full, other, mine = pl.pallas_call(
+    full, to_two, to_three, mine = pl.pallas_call(
         functools.partial(edge_kernel, scale, n_slab),
-        out_shape=[VMEM((4, ROWS, COLS), F32)] * 3,
+        out_shape=[VMEM((4, ROWS, COLS), F32)] * 4,
         in_specs=[SPEC] * 8,
-        out_specs=[SPEC] * 3,
+        out_specs=[SPEC] * 4,
         scratch_shapes=[VMEM((5, 8, ROWS, COLS), F32)],
         compiler_params=PARAMS,
         cost_estimate=cost(0.5),
@@ -527,26 +561,25 @@
         )
     )
 
-    slab = lax.axis_index("slab")
-    even = lax.axis_index("tile") % 2 == 0
-    from_2, from_1, from_3 = (
-        permute(full, lambda t, s: (t, (2, 3, 1, 0)[s])),
-        permute(full, lambda t, s: (t, (s + 1) % n_slab)),
-        permute(other, lambda t, s: (t, (s + 3) % n_slab)),
-    )
-
-    def only(flag, value):
-        return jnp.where(flag, value[:3], 0.0), jnp.where(flag, value[3], 1.0)
-
-    def over(near, far):
-        return near[1] * far[0] + near[0], near[1] * far[1]
-
-    last = slab == n_slab - 1
-    seen = over(only(slab >= 2, from_2), only(slab >= 1, from_1))
-    seen = over(seen, (mine[:3], mine[3]))
-    seen = over(seen, only(jnp.logical_and(even, jnp.logical_not(last)), from_3))
-    seen = over(only(last, from_3), seen)
-    return jnp.concatenate([seen[0], (1.0 - seen[1])[None]], 0)[None]
+    def first(t, s):
+        if shades_forward(t):
+            return ((t, 3), (t, 2), (t ^ 1, 2), (t, 0))[s]
+        return ((t, 3), (t ^ 1, 1), (t, 1), (t, 0))[s]
+
+    def second(t, s):
+        return (t, s ^ 1 if shades_forward(t) else (s + 1) % n_slab)
+
+    got_one = permute(full, first)
+    got_two = permute(to_two, second)
+    got_three = permute(to_three, lambda t, s: (t, (2, 3, 1, 0)[s]))
+    return pl.pallas_call(
+        final_kernel,
+        out_shape=jax.ShapeDtypeStruct((1, 4, ROWS, COLS), F32),
+        in_specs=[SPEC] * 4,
+        out_specs=SPEC,
+        compiler_params=PARAMS,
+        name="final",
+    )(*in_vmem(got_one, got_two, got_three, mine))
 
 
 def solution(mesh):

time: 29.8 us -> 28.6 us (0.960)
  the two profiles are of different devices: /device:TPU:24 before, /device:TPU:1 now
where the time goes in v4:
time: 28.6 us; the launch traced here: 28.5 us
  starting transfers between devices  16.2 us (57%)
  Pallas kernels  9.03 us (32%)
  waiting for transfers between devices  3.21 us (11%)
    ppermute x6, starting transfers between devices, permute(): return lax.ppermute(value, ('tile', 'slab'), pairs)  14.4 us
    pallas_call x1, Pallas kernels, on_device(): pl.pallas_call(functools.partial(inner_kernel, scale), out_shape=[VMEM((6...  3.44 us
    ppermute x6, waiting for transfers between devices, permute(): return lax.ppermute(value, ('tile', 'slab'), pairs)  3.2 us
    pallas_call x1, Pallas kernels, on_device(): pl.pallas_call(columns_kernel, out_shape=[VMEM((20, 2, BODY, 2 * DEPTH),...  3.12 us
    ppermute x1, starting transfers between devices, on_device(): near = lax.ppermute(near, 'tile', [(t, t ^ 1) for t in range(n_tile)])  1.75 us
    pallas_call x1, Pallas kernels, on_device(): pl.pallas_call(pack_kernel, out_shape=[VMEM((5, RADIUS, ROWS, DEPTH), F32...  0.98 us
    pallas_call x1, Pallas kernels, on_device(): pl.pallas_call(final_kernel, out_shape=jax.ShapeDtypeStruct((1, 4, ROWS,...  0.63 us
  transfers between devices with their start and end apart: 7, of which 1 were waited for; matrix products, arithmetic and copies ran while one was open for 0% of the time, Pallas kernels for 25%

profile of v4, /device:TPU:1, one launch (start us, length us, event | category | flops | bytes accessed | tf_op | source)
XLA Modules:
  0.0 28.5 jit_solution(17783292996870409058)
XLA Ops:
  0.0 1.0 %pack.1 = (f32[5,4,8,128]{3,2,1,0:T(8,128)S(1)}, f32[5,4,8,128]{3,2,1,0:T(8,128)S(1)}) custom-call(s32[128,8,128]{2,1,0:T(8,128)} %counts.3, f32[4,128,8,128]{3,2,1,0:T(8,128)} %fields.3), custom_call_target="tpu_custom_call" | custom-call | flops 1000000000 | bytes 3600000 | tf_op jit(solution)/shard_map/pack/pallas_call | solution.py:453
  1.0 3.1 %collective-permute-start = (f32[5,4,8,128]{3,2,1,0:T(8,128)S(1)}, f32[5,4,8,128]{3,2,1,0:T(8,128)S(1)}, u32[]{:S(2)}, u32[]{:S(2)}) collective-permute-start(f32[5,4,8,128]{3,2,1,0:T(8,128)S(1)} %get-tuple-element.27), channel_id=1, source_target_pairs={{0,1},{1,0},{2,3},{3,2},{4,8},{5,9},{6,10},{7,11},{8,4},{9,5},{10,... | collective-permute-start | bytes 245768 | tf_op jit(solution)/shard_map/ppermute | solution.py:446
  4.1 1.7 %collective-permute-start.1 = (f32[5,4,8,128]{3,2,1,0:T(8,128)S(1)}, f32[5,4,8,128]{3,2,1,0:T(8,128)S(1)}, u32[]{:S(2)}, u32[]{:S(2)}) collective-permute-start(f32[5,4,8,128]{3,2,1,0:T(8,128)S(1)} %get-tuple-element.28), channel_id=1, source_target_pairs={{0,4},{4,0},{8,12},{12,8},{16,20},{20,16},{24,28},{28,24},{32,36},... | collective-permute-start | bytes 245768 | tf_op jit(solution)/shard_map/ppermute | solution.py:469
  5.9 0.0 copy-done.4
  5.9 3.1 %columns.1 = (bf16[20,2,112,256]{3,2,1,0:T(8,128)(2,1)S(1)}, f32[5,8,8,128]{3,2,1,0:T(8,128)S(1)}, f32[5,128,128]{2,1,0:T(8,128)S(1)}, s32[128,8,128]{2,1,0:T(8,128)S(1)}, f32[40,8,128]{2,1,0:T(8,128)S(1)}) custom-call(bf16[128,256]{1,0:T(8,128)(2,1)S(1)} %copy-done.4, bf16[2,16,256]{2,1,0:T(8,128)(2,1)S(1)} %copy-done.5, s32[128,8,128]{2,1,0:T(8,128)} %counts.3, ...), custom_call_target="tpu_custom_call" | custom-call | flops 3000000000 | bytes 10800000 | tf_op jit(solution)/shard_map/columns/pallas_call | solution.py:473
  9.0 0.0 copy-start.1
  9.0 1.4 %collective-permute-start.2 = (f32[40,8,128]{2,1,0:T(8,128)S(1)}, f32[40,8,128]{2,1,0:T(8,128)S(1)}, u32[]{:S(2)}, u32[]{:S(2)}) collective-permute-start(f32[40,8,128]{2,1,0:T(8,128)S(1)} %get-tuple-element.35), channel_id=1, source_target_pairs={{0,4},{1,0},{2,1},{3,2},{4,5},{5,6},{6,7},{7,3},{8,12},{9,8},{10,9... | collective-permute-start | bytes 491528 | tf_op jit(solution)/shard_map/ppermute | solution.py:446
  10.4 0.0 collective-permute-done.far
  10.4 0.0 collective-permute-done.1.near
  10.4 0.0 copy-done.3
  10.4 0.4 %rim.1 = (s32[128,8,128]{2,1,0:T(8,128)S(1)}, f32[24,8,128]{2,1,0:T(8,128)S(1)}, bf16[20,2,16,256]{3,2,1,0:T(8,128)(2,1)S(1)}, f32[9,8,128]{2,1,0:T(8,128)S(1)}) custom-call(f32[6,4,8]{2,1,0:T(4,128)S(1)} %bitcast.1, s32[128,8,128]{2,1,0:T(8,128)S(1)} %get-tuple-element.24.class_v, f32[5,8,8,128]{3,2,1,0:T(8,128)S(1)} %get-tuple-element.25.last, ...), custom_call_target="tpu_custom_call" | custom-call | flops 1000000000 | bytes 3600000 | tf_op jit(solution)/shard_map/rim/pallas_call | solution.py:503
  10.8 4.2 %collective-permute-start.3 = (f32[9,8,128]{2,1,0:T(8,128)S(1)}, f32[9,8,128]{2,1,0:T(8,128)S(1)}, u32[]{:S(2)}, u32[]{:S(2)}) collective-permute-start(f32[9,8,128]{2,1,0:T(8,128)S(1)} %get-tuple-element.36), channel_id=1, source_target_pairs={{0,4},{1,0},{2,1},{3,2},{4,5},{5,6},{6,7},{7,3},{8,12},{9,8},{10,9... | collective-permute-start | bytes 110600 | tf_op jit(solution)/shard_map/ppermute | solution.py:446
  15.0 3.4 %inner.1 = (f32[6,8,128]{2,1,0:T(8,128)S(1)}, f32[5,8,8,128]{3,2,1,0:T(8,128)S(1)}, f32[5,4,8,128]{3,2,1,0:T(8,128)S(1)}) custom-call(bf16[20,2,112,256]{3,2,1,0:T(8,128)(2,1)S(1)} %get-tuple-element.23.bodies, bf16[20,2,16,256]{3,2,1,0:T(8,128)(2,1)S(1)} %get-tuple-element.29.tails, s32[128,8,128]{2,1,0:T(8,128)S(1)} %get-tuple-element.30.class_t, ...), custom_call_target="tpu_custom_call" | custom-call | flops 3500000000 | bytes 12600000 | tf_op jit(solution)/shard_map/inner/pallas_call | solution.py:525
  18.5 0.0 collective-permute-done.3.given_rim
  18.5 0.0 collective-permute-done.2.given
  18.5 0.0 copy-done.2
  18.5 0.4 %edges.1 = (f32[4,8,128]{2,1,0:T(8,128)S(1)}, f32[4,8,128]{2,1,0:T(8,128)S(1)}, f32[4,8,128]{2,1,0:T(8,128)S(1)}, f32[4,8,128]{2,1,0:T(8,128)S(1)}) custom-call(f32[5,8,8,128]{3,2,1,0:T(8,128)S(1)} %get-tuple-element.32.halo, f32[5,4,8,128]{3,2,1,0:T(8,128)S(1)} %get-tuple-element.33.end_cells, s32[128,8,128]{2,1,0:T(8,128)S(1)} %get-tuple-element.30.class_t, ...), custom_call_target="tpu_custom_call" | custom-call | flops 500000000 | bytes 1800000 | tf_op jit(solution)/shard_map/edges/pallas_call | solution.py:548
  18.9 1.9 %collective-permute-start.4 = (f32[4,8,128]{2,1,0:T(8,128)S(1)}, f32[4,8,128]{2,1,0:T(8,128)S(1)}, u32[]{:S(2)}, u32[]{:S(2)}) collective-permute-start(f32[4,8,128]{2,1,0:T(8,128)S(1)} %get-tuple-element.37), channel_id=1, source_target_pairs={{0,3},{1,5},{2,1},{3,0},{4,7},{5,6},{6,2},{7,4},{8,11},{9,13},{10,... | collective-permute-start | bytes 49160 | tf_op jit(solution)/shard_map/ppermute | solution.py:446
  20.8 2.4 %collective-permute-start.5 = (f32[4,8,128]{2,1,0:T(8,128)S(1)}, f32[4,8,128]{2,1,0:T(8,128)S(1)}, u32[]{:S(2)}, u32[]{:S(2)}) collective-permute-start(f32[4,8,128]{2,1,0:T(8,128)S(1)} %get-tuple-element.38), channel_id=1, source_target_pairs={{0,1},{1,2},{2,3},{3,0},{4,5},{5,4},{6,7},{7,6},{8,9},{9,10},{10,1... | collective-permute-start | bytes 49160 | tf_op jit(solution)/shard_map/ppermute | solution.py:446
  23.2 1.5 %collective-permute-start.6 = (f32[4,8,128]{2,1,0:T(8,128)S(1)}, f32[4,8,128]{2,1,0:T(8,128)S(1)}, u32[]{:S(2)}, u32[]{:S(2)}) collective-permute-start(f32[4,8,128]{2,1,0:T(8,128)S(1)} %get-tuple-element.39), channel_id=1, source_target_pairs={{0,2},{1,3},{2,1},{3,0},{4,6},{5,7},{6,5},{7,4},{8,10},{9,11},{10,... | collective-permute-start | bytes 49160 | tf_op jit(solution)/shard_map/ppermute | solution.py:446
  24.7 0.0 collective-permute-done.4.got_one
  24.7 0.0 collective-permute-done.5.got_two
  24.7 3.2 %collective-permute-done.6.got_three = f32[4,8,128]{2,1,0:T(8,128)S(1)} collective-permute-done((f32[4,8,128]{2,1,0:T(8,128)S(1)}, f32[4,8,128]{2,1,0:T(8,128)S(1)}, u32[]{:S(2)}, u32[]{:S(2)}) %collective-permute-start.6) | collective-permute-done | bytes 16416 | tf_op jit(solution)/shard_map/ppermute | solution.py:446
  27.9 0.6 %final.1 = f32[1,4,8,128]{3,2,1,0:T(8,128)} custom-call(f32[4,8,128]{2,1,0:T(8,128)S(1)} %collective-permute-done.4.got_one, f32[4,8,128]{2,1,0:T(8,128)S(1)} %collective-permute-done.5.got_two, f32[4,8,128]{2,1,0:T(8,128)S(1)} %collective-permute-done.6.got_three, f32[4,8,128]{2,1,0:T(8,128)S(1)} %get-tuple-element.40.mine), custom_call_target="tpu_custom_call" | custom-call | tf_op jit(solution)/shard_map/final/pallas_call | solution.py:575
  (8 shorter events, 0.0 us)
Async XLA Ops:
  0.0 5.9 %copy-start.5 = (bf16[2,16,256]{2,1,0:T(8,128)(2,1)S(1)}, bf16[2,16,256]{2,1,0:T(8,128)(2,1)}, u32[]{:S(2)}) copy-start(bf16[2,16,256]{2,1,0:T(8,128)(2,1)} %constant.10.clone.end_matrix.matrix) | copy-start | bytes 49156
  0.0 5.9 %copy-start.4 = (bf16[128,256]{1,0:T(8,128)(2,1)S(1)}, bf16[128,256]{1,0:T(8,128)(2,1)}, u32[]{:S(2)}) copy-start(bf16[128,256]{1,0:T(8,128)(2,1)} %constant.11.clone.matrix) | copy-start | bytes 196612
  1.0 9.4 %collective-permute-start = (f32[5,4,8,128]{3,2,1,0:T(8,128)S(1)}, f32[5,4,8,128]{3,2,1,0:T(8,128)S(1)}, u32[]{:S(2)}, u32[]{:S(2)}) collective-permute-start(f32[5,4,8,128]{3,2,1,0:T(8,128)S(1)} %get-tuple-element.27), channel_id=1, source_target_pairs={{0,1},{1,0},{2,3},{3,2},{4,8},{5,9},{6,10},{7,11},{8,4},{9,5},{10,... | collective-permute-start | bytes 245768 | tf_op jit(solution)/shard_map/ppermute | solution.py:446
  4.1 6.3 %copy-start = (f32[8,4,6]{0,1,2:T(4,128)S(1)}, f32[8,4,6]{0,1,2:T(4,128)}, u32[]{:S(2)}) copy-start(f32[8,4,6]{0,1,2:T(4,128)} %param.12) | copy-start | bytes 2308
  4.1 6.3 %copy-start.3 = (bf16[128,192]{1,0:T(8,128)(2,1)S(1)}, bf16[128,192]{1,0:T(8,128)(2,1)}, u32[]{:S(2)}) copy-start(bf16[128,192]{1,0:T(8,128)(2,1)} %constant.12.clone.rim_matrix) | copy-start | bytes 147460
  4.1 6.3 %collective-permute-start.1 = (f32[5,4,8,128]{3,2,1,0:T(8,128)S(1)}, f32[5,4,8,128]{3,2,1,0:T(8,128)S(1)}, u32[]{:S(2)}, u32[]{:S(2)}) collective-permute-start(f32[5,4,8,128]{3,2,1,0:T(8,128)S(1)} %get-tuple-element.28), channel_id=1, source_target_pairs={{0,4},{4,0},{8,12},{12,8},{16,20},{20,16},{24,28},{28,24},{32,36},... | collective-permute-start | bytes 245768 | tf_op jit(solution)/shard_map/ppermute | solution.py:469
  9.0 6.0 %copy-start.1 = (bf16[272,256]{1,0:T(8,128)(2,1)S(1)}, bf16[272,256]{1,0:T(8,128)(2,1)}, u32[]{:S(2)}) copy-start(bf16[272,256]{1,0:T(8,128)(2,1)} %constant.13.clone.matrix) | copy-start | bytes 417796
  9.0 9.5 %collective-permute-start.2 = (f32[40,8,128]{2,1,0:T(8,128)S(1)}, f32[40,8,128]{2,1,0:T(8,128)S(1)}, u32[]{:S(2)}, u32[]{:S(2)}) collective-permute-start(f32[40,8,128]{2,1,0:T(8,128)S(1)} %get-tuple-element.35), channel_id=1, source_target_pairs={{0,4},{1,0},{2,1},{3,2},{4,5},{5,6},{6,7},{7,3},{8,12},{9,8},{10,9... | collective-permute-start | bytes 491528 | tf_op jit(solution)/shard_map/ppermute | solution.py:446
  10.8 7.6 %collective-permute-start.3 = (f32[9,8,128]{2,1,0:T(8,128)S(1)}, f32[9,8,128]{2,1,0:T(8,128)S(1)}, u32[]{:S(2)}, u32[]{:S(2)}) collective-permute-start(f32[9,8,128]{2,1,0:T(8,128)S(1)} %get-tuple-element.36), channel_id=1, source_target_pairs={{0,4},{1,0},{2,1},{3,2},{4,5},{5,6},{6,7},{7,3},{8,12},{9,8},{10,9... | collective-permute-start | bytes 110600 | tf_op jit(solution)/shard_map/ppermute | solution.py:446
  15.0 3.5 %copy-start.2 = (bf16[256,128]{1,0:T(8,128)(2,1)S(1)}, bf16[256,128]{1,0:T(8,128)(2,1)}, u32[]{:S(2)}) copy-start(bf16[256,128]{1,0:T(8,128)(2,1)} %constant.14.clone.place) | copy-start | bytes 196612
  18.9 5.7 %collective-permute-start.4 = (f32[4,8,128]{2,1,0:T(8,128)S(1)}, f32[4,8,128]{2,1,0:T(8,128)S(1)}, u32[]{:S(2)}, u32[]{:S(2)}) collective-permute-start(f32[4,8,128]{2,1,0:T(8,128)S(1)} %get-tuple-element.37), channel_id=1, source_target_pairs={{0,3},{1,5},{2,1},{3,0},{4,7},{5,6},{6,2},{7,4},{8,11},{9,13},{10,... | collective-permute-start | bytes 49160 | tf_op jit(solution)/shard_map/ppermute | solution.py:446
  20.8 3.9 %collective-permute-start.5 = (f32[4,8,128]{2,1,0:T(8,128)S(1)}, f32[4,8,128]{2,1,0:T(8,128)S(1)}, u32[]{:S(2)}, u32[]{:S(2)}) collective-permute-start(f32[4,8,128]{2,1,0:T(8,128)S(1)} %get-tuple-element.38), channel_id=1, source_target_pairs={{0,1},{1,2},{2,3},{3,0},{4,5},{5,4},{6,7},{7,6},{8,9},{9,10},{10,1... | collective-permute-start | bytes 49160 | tf_op jit(solution)/shard_map/ppermute | solution.py:446
  23.2 4.7 %collective-permute-start.6 = (f32[4,8,128]{2,1,0:T(8,128)S(1)}, f32[4,8,128]{2,1,0:T(8,128)S(1)}, u32[]{:S(2)}, u32[]{:S(2)}) collective-permute-start(f32[4,8,128]{2,1,0:T(8,128)S(1)} %get-tuple-element.39), channel_id=1, source_target_pairs={{0,2},{1,3},{2,1},{3,0},{4,6},{5,7},{6,5},{7,4},{8,10},{9,11},{10,... | collective-permute-start | bytes 49160 | tf_op jit(solution)/shard_map/ppermute | solution.py:446

commit v5 on v4

--- a/solution.py
+++ b/solution.py
@@ -103,19 +103,10 @@
 
 
 def columns_kernel(
-    matrix, end_matrix, counts, fields, classes,
-    bodies, last, rim, class_v, send,
-    count_v, field_v, high, low, sems,
+    matrix, end_matrix, count_v, field_v,
+    bodies, last, rim, send,
+    high, low,
 ):
-    copies = [pltpu.make_async_copy(counts, count_v, sems.at[0])]
-    for field in range(4):
-        copies.append(
-            pltpu.make_async_copy(fields.at[field], field_v.at[field], sems.at[field + 1])
-        )
-    copies.append(pltpu.make_async_copy(classes, class_v, sems.at[5]))
-    for copy in copies:
-        copy.start()
-
     def prepare(source, field):
         rim[field, pl.ds(0, 64), :] = source[pl.ds(0, 64), :]
         rim[field, pl.ds(64, 64), :] = source[pl.ds((COLS - 8) * ROWS, 64), :]
@@ -138,14 +129,11 @@
                     split(tile), 1
                 )
 
-    copies[0].wait()
     prepare(jnp.log(1.0 + count_v[...].astype(F32)).reshape(COLS * ROWS, DEPTH), 0)
-    copies[1].wait()
     prepare(field_v.at[0].reshape(COLS * ROWS, DEPTH), 1)
     sweep(0)
     sweep(1)
     for field in range(1, 4):
-        copies[field + 1].wait()
         prepare(field_v.at[field].reshape(COLS * ROWS, DEPTH), field + 1)
     for field in range(2, 5):
         sweep(field)
@@ -169,7 +157,6 @@
             flat_send[pl.ds(field * 64 + pair * 2 + j, 8, stride=ROWS), :] = out[
                 :, j * 128 : (j + 1) * 128
             ]
-    copies[5].wait()
 
 
 def depth_product(matrix, stack):
@@ -258,7 +245,7 @@
     tints = [jnp.tanh(linear) for linear in linears[:3]]
     x = linears[3]
     t = jnp.exp(-jnp.abs(x))
-    series = t * (1.0 - t * (1.0 / 2 - t * (1.0 / 3 - t * (1.0 / 4))))
+    series = t * (1.0 - t * (1.0 / 2 - t * (1.0 / 3)))
     soft = jnp.maximum(x, 0.0) + jnp.where(t < 0.01, series, jnp.log(1.0 + t))
     step = soft * scale
     opacity = step * (
@@ -315,8 +302,8 @@
             flat_end[field, pl.ds(row, RADIUS, stride=ROWS), :] = last[:, lanes]
         return carry
 
-    lax.fori_loop(0, 20, blur, 0, unroll=10)
-    unroll = 12
+    lax.fori_loop(0, 20, blur, 0, unroll=20)
+    unroll = 24
 
     def body(index, state):
         for k in range(unroll):
@@ -470,28 +457,24 @@
 
     step_matrix = plane_matrix(list(range(RADIUS, RADIUS + WIDE)), list(range(2 * WIDE)))
     end_matrix = jnp.asarray(np.stack([depth_matrix(BACK_TARGETS), depth_matrix(FRONT_TARGETS)]))
-    bodies, last, rim, class_v, send = pl.pallas_call(
+    bodies, last, rim, send = pl.pallas_call(
         columns_kernel,
         out_shape=[
             VMEM((20, 2, BODY, 2 * DEPTH), BF16),
             VMEM((5, ROWS, WIDE, DEPTH), F32),
             VMEM((5, 16 * ROWS, DEPTH), F32),
-            VMEM((COLS, ROWS, DEPTH), jnp.int32),
             VMEM((40, ROWS, COLS), F32),
         ],
-        in_specs=[SPEC] * 2 + [HBM_SPEC] * 3,
-        out_specs=[SPEC] * 5,
+        in_specs=[SPEC] * 4,
+        out_specs=[SPEC] * 4,
         scratch_shapes=[
-            VMEM((COLS, ROWS, DEPTH), jnp.int32),
-            VMEM((4, COLS, ROWS, DEPTH), F32),
             VMEM((5, COLS * ROWS, DEPTH), BF16),
             VMEM((5, COLS * ROWS, DEPTH), BF16),
-            pltpu.SemaphoreType.DMA((6,)),
         ],
         compiler_params=PARAMS,
         cost_estimate=cost(3),
         name="columns",
-    )(*in_vmem(jnp.asarray(step_matrix), end_matrix), *in_hbm(counts, fields, class_ids))
+    )(*in_vmem(jnp.asarray(step_matrix), end_matrix, counts, fields))
 
     def beside(t, s):
         to = s + 1 if shades_forward(t) else s - 1
@@ -515,7 +498,7 @@
         name="rim",
     )(
         *in_vmem(
-            jnp.transpose(tf_table, (2, 1, 0)), class_v, last, rim, far, near,
+            jnp.transpose(tf_table, (2, 1, 0)), class_ids, last, rim, far, near,
             jnp.asarray(rim_matrix), end_matrix,
         )
     )

time: 28.6 us -> 27.2 us (0.951)
  the two profiles are of different devices: /device:TPU:1 before, /device:TPU:24 now
where the time goes in v5:
time: 27.2 us; the launch traced here: 26.9 us
  starting transfers between devices  14 us (51%)
  Pallas kernels  7.05 us (26%)
  waiting for transfers between devices  5.79 us (21%)
    ppermute x6, starting transfers between devices, permute(): return lax.ppermute(value, ('tile', 'slab'), pairs)  14 us
    ppermute x6, waiting for transfers between devices, permute(): return lax.ppermute(value, ('tile', 'slab'), pairs)  5.78 us
    pallas_call x1, Pallas kernels, on_device(): pl.pallas_call(functools.partial(inner_kernel, scale), out_shape=[VMEM((6...  2.85 us
    pallas_call x1, Pallas kernels, on_device(): pl.pallas_call(columns_kernel, out_shape=[VMEM((20, 2, BODY, 2 * DEPTH),...  1.59 us
    pallas_call x1, Pallas kernels, on_device(): pl.pallas_call(pack_kernel, out_shape=[VMEM((5, RADIUS, ROWS, DEPTH), F32...  1.12 us
    pallas_call x1, Pallas kernels, on_device(): pl.pallas_call(final_kernel, out_shape=jax.ShapeDtypeStruct((1, 4, ROWS,...  0.63 us
  transfers between devices with their start and end apart: 7, of which 4 were waited for; matrix products, arithmetic and copies ran while one was open for 0% of the time, Pallas kernels for 18%

profile of v5, /device:TPU:24, one launch (start us, length us, event | category | flops | bytes accessed | tf_op | source)
XLA Modules:
  0.0 26.9 jit_solution(18374671004579546138)
XLA Ops:
  0.0 0.0 copy-start.1
  0.0 1.1 %pack.1 = (f32[5,4,8,128]{3,2,1,0:T(8,128)S(1)}, f32[5,4,8,128]{3,2,1,0:T(8,128)S(1)}) custom-call(s32[128,8,128]{2,1,0:T(8,128)} %counts.1, f32[4,128,8,128]{3,2,1,0:T(8,128)} %fields.1), custom_call_target="tpu_custom_call" | custom-call | flops 1000000000 | bytes 3600000 | tf_op jit(solution)/shard_map/pack/pallas_call | solution.py:440
  1.1 3.8 %collective-permute-start = (f32[5,4,8,128]{3,2,1,0:T(8,128)S(1)}, f32[5,4,8,128]{3,2,1,0:T(8,128)S(1)}, u32[]{:S(2)}, u32[]{:S(2)}) collective-permute-start(f32[5,4,8,128]{3,2,1,0:T(8,128)S(1)} %get-tuple-element.25), channel_id=1, source_target_pairs={{0,1},{1,0},{2,3},{3,2},{4,8},{5,9},{6,10},{7,11},{8,4},{9,5},{10,... | collective-permute-start | bytes 245768 | tf_op jit(solution)/shard_map/ppermute | solution.py:433
  5.0 0.0 collective-permute-start.1
  5.0 0.0 copy-done.8
  5.0 0.0 copy-done.7
  5.0 1.6 %columns.1 = (bf16[20,2,112,256]{3,2,1,0:T(8,128)(2,1)S(1)}, f32[5,8,8,128]{3,2,1,0:T(8,128)S(1)}, f32[5,128,128]{2,1,0:T(8,128)S(1)}, f32[40,8,128]{2,1,0:T(8,128)S(1)}) custom-call(bf16[128,256]{1,0:T(8,128)(2,1)S(1)} %copy-done.7, bf16[2,16,256]{2,1,0:T(8,128)(2,1)S(1)} %copy-done.8, s32[128,8,128]{2,1,0:T(8,128)S(1)} %copy-done.1, ...), custom_call_target="tpu_custom_call" | custom-call | flops 3000000000 | bytes 10800000 | tf_op jit(solution)/shard_map/columns/pallas_call | solution.py:460
  6.6 0.6 %collective-permute-start.2 = (f32[40,8,128]{2,1,0:T(8,128)S(1)}, f32[40,8,128]{2,1,0:T(8,128)S(1)}, u32[]{:S(2)}, u32[]{:S(2)}) collective-permute-start(f32[40,8,128]{2,1,0:T(8,128)S(1)} %get-tuple-element.33), channel_id=1, source_target_pairs={{0,4},{1,0},{2,1},{3,2},{4,5},{5,6},{6,7},{7,3},{8,12},{9,8},{10,9... | collective-permute-start | bytes 491528 | tf_op jit(solution)/shard_map/ppermute | solution.py:433
  7.2 1.6 %collective-permute-done.far = f32[5,4,8,128]{3,2,1,0:T(8,128)S(1)} collective-permute-done((f32[5,4,8,128]{3,2,1,0:T(8,128)S(1)}, f32[5,4,8,128]{3,2,1,0:T(8,128)S(1)}, u32[]{:S(2)}, u32[]{:S(2)}) %collective-permute-start) | collective-permute-done | bytes 81952 | tf_op jit(solution)/shard_map/ppermute | solution.py:433
  8.8 0.0 collective-permute-done.1.near
  8.8 0.0 copy-done.2
  8.8 0.4 %rim.1 = (s32[128,8,128]{2,1,0:T(8,128)S(1)}, f32[24,8,128]{2,1,0:T(8,128)S(1)}, bf16[20,2,16,256]{3,2,1,0:T(8,128)(2,1)S(1)}, f32[9,8,128]{2,1,0:T(8,128)S(1)}) custom-call(f32[6,4,8]{2,1,0:T(4,128)S(1)} %bitcast.1, s32[128,8,128]{2,1,0:T(8,128)S(1)} %copy-done.2, f32[5,8,8,128]{3,2,1,0:T(8,128)S(1)} %get-tuple-element.23.last, ...), custom_call_target="tpu_custom_call" | custom-call | flops 1000000000 | bytes 3600000 | tf_op jit(solution)/shard_map/rim/pallas_call | solution.py:486
  9.3 1.4 %collective-permute-start.3 = (f32[9,8,128]{2,1,0:T(8,128)S(1)}, f32[9,8,128]{2,1,0:T(8,128)S(1)}, u32[]{:S(2)}, u32[]{:S(2)}) collective-permute-start(f32[9,8,128]{2,1,0:T(8,128)S(1)} %get-tuple-element.34), channel_id=1, source_target_pairs={{0,4},{1,0},{2,1},{3,2},{4,5},{5,6},{6,7},{7,3},{8,12},{9,8},{10,9... | collective-permute-start | bytes 110600 | tf_op jit(solution)/shard_map/ppermute | solution.py:433
  10.7 2.8 %inner.1 = (f32[6,8,128]{2,1,0:T(8,128)S(1)}, f32[5,8,8,128]{3,2,1,0:T(8,128)S(1)}, f32[5,4,8,128]{3,2,1,0:T(8,128)S(1)}) custom-call(bf16[20,2,112,256]{3,2,1,0:T(8,128)(2,1)S(1)} %get-tuple-element.22.bodies, bf16[20,2,16,256]{3,2,1,0:T(8,128)(2,1)S(1)} %get-tuple-element.27.tails, s32[128,8,128]{2,1,0:T(8,128)S(1)} %get-tuple-element.28.class_t, ...), custom_call_target="tpu_custom_call" | custom-call | flops 3500000000 | bytes 12600000 | tf_op jit(solution)/shard_map/inner/pallas_call | solution.py:508
  13.6 1.0 %collective-permute-done.3.given_rim = f32[9,8,128]{2,1,0:T(8,128)S(1)} collective-permute-done((f32[9,8,128]{2,1,0:T(8,128)S(1)}, f32[9,8,128]{2,1,0:T(8,128)S(1)}, u32[]{:S(2)}, u32[]{:S(2)}) %collective-permute-start.3) | collective-permute-done | bytes 36896 | tf_op jit(solution)/shard_map/ppermute | solution.py:433
  14.6 0.0 collective-permute-done.2.given
  14.6 0.4 %edges.1 = (f32[4,8,128]{2,1,0:T(8,128)S(1)}, f32[4,8,128]{2,1,0:T(8,128)S(1)}, f32[4,8,128]{2,1,0:T(8,128)S(1)}, f32[4,8,128]{2,1,0:T(8,128)S(1)}) custom-call(f32[5,8,8,128]{3,2,1,0:T(8,128)S(1)} %get-tuple-element.30.halo, f32[5,4,8,128]{3,2,1,0:T(8,128)S(1)} %get-tuple-element.31.end_cells, s32[128,8,128]{2,1,0:T(8,128)S(1)} %get-tuple-element.28.class_t, ...), custom_call_target="tpu_custom_call" | custom-call | flops 500000000 | bytes 1800000 | tf_op jit(solution)/shard_map/edges/pallas_call | solution.py:531
  15.0 5.1 %collective-permute-start.4 = (f32[4,8,128]{2,1,0:T(8,128)S(1)}, f32[4,8,128]{2,1,0:T(8,128)S(1)}, u32[]{:S(2)}, u32[]{:S(2)}) collective-permute-start(f32[4,8,128]{2,1,0:T(8,128)S(1)} %get-tuple-element.35), channel_id=1, source_target_pairs={{0,3},{1,5},{2,1},{3,0},{4,7},{5,6},{6,2},{7,4},{8,11},{9,13},{10,... | collective-permute-start | bytes 49160 | tf_op jit(solution)/shard_map/ppermute | solution.py:433
  20.1 0.0 collective-permute-start.5
  20.1 3.1 %collective-permute-start.6 = (f32[4,8,128]{2,1,0:T(8,128)S(1)}, f32[4,8,128]{2,1,0:T(8,128)S(1)}, u32[]{:S(2)}, u32[]{:S(2)}) collective-permute-start(f32[4,8,128]{2,1,0:T(8,128)S(1)} %get-tuple-element.37), channel_id=1, source_target_pairs={{0,2},{1,3},{2,1},{3,0},{4,6},{5,7},{6,5},{7,4},{8,10},{9,11},{10,... | collective-permute-start | bytes 49160 | tf_op jit(solution)/shard_map/ppermute | solution.py:433
  23.1 0.0 collective-permute-done.4.got_one
  23.1 2.9 %collective-permute-done.5.got_two = f32[4,8,128]{2,1,0:T(8,128)S(1)} collective-permute-done((f32[4,8,128]{2,1,0:T(8,128)S(1)}, f32[4,8,128]{2,1,0:T(8,128)S(1)}, u32[]{:S(2)}, u32[]{:S(2)}) %collective-permute-start.5) | collective-permute-done | bytes 16416 | tf_op jit(solution)/shard_map/ppermute | solution.py:433
  26.1 0.2 collective-permute-done.6.got_three
  26.3 0.6 %final.1 = f32[1,4,8,128]{3,2,1,0:T(8,128)} custom-call(f32[4,8,128]{2,1,0:T(8,128)S(1)} %collective-permute-done.4.got_one, f32[4,8,128]{2,1,0:T(8,128)S(1)} %collective-permute-done.5.got_two, f32[4,8,128]{2,1,0:T(8,128)S(1)} %collective-permute-done.6.got_three, f32[4,8,128]{2,1,0:T(8,128)S(1)} %get-tuple-element.38.mine), custom_call_target="tpu_custom_call" | custom-call | tf_op jit(solution)/shard_map/final/pallas_call | solution.py:558
  (14 shorter events, 0.0 us)
Async XLA Ops:
  0.0 5.0 %copy-start.8 = (bf16[2,16,256]{2,1,0:T(8,128)(2,1)S(1)}, bf16[2,16,256]{2,1,0:T(8,128)(2,1)}, u32[]{:S(2)}) copy-start(bf16[2,16,256]{2,1,0:T(8,128)(2,1)} %constant.10.clone.end_matrix.matrix) | copy-start | bytes 49156
  0.0 5.0 %copy-start.7 = (bf16[128,256]{1,0:T(8,128)(2,1)S(1)}, bf16[128,256]{1,0:T(8,128)(2,1)}, u32[]{:S(2)}) copy-start(bf16[128,256]{1,0:T(8,128)(2,1)} %constant.11.clone.matrix) | copy-start | bytes 196612
  0.0 5.0 %copy-start = (f32[4,128,8,128]{3,2,1,0:T(8,128)S(1)}, f32[4,128,8,128]{3,2,1,0:T(8,128)}, u32[]{:S(2)}) copy-start(f32[4,128,8,128]{3,2,1,0:T(8,128)} %fields.1) | copy-start | bytes 6291460
  0.0 5.0 %copy-start.1 = (s32[128,8,128]{2,1,0:T(8,128)S(1)}, s32[128,8,128]{2,1,0:T(8,128)}, u32[]{:S(2)}) copy-start(s32[128,8,128]{2,1,0:T(8,128)} %counts.1) | copy-start | bytes 1572868
  1.1 7.7 %collective-permute-start = (f32[5,4,8,128]{3,2,1,0:T(8,128)S(1)}, f32[5,4,8,128]{3,2,1,0:T(8,128)S(1)}, u32[]{:S(2)}, u32[]{:S(2)}) collective-permute-start(f32[5,4,8,128]{3,2,1,0:T(8,128)S(1)} %get-tuple-element.25), channel_id=1, source_target_pairs={{0,1},{1,0},{2,3},{3,2},{4,8},{5,9},{6,10},{7,11},{8,4},{9,5},{10,... | collective-permute-start | bytes 245768 | tf_op jit(solution)/shard_map/ppermute | solution.py:433
  5.0 3.9 %copy-start.2 = (s32[128,8,128]{2,1,0:T(8,128)S(1)}, s32[128,8,128]{2,1,0:T(8,128)}, u32[]{:S(2)}) copy-start(s32[128,8,128]{2,1,0:T(8,128)} %class_v.1) | copy-start | bytes 1572868
  5.0 3.9 %copy-start.3 = (f32[8,4,6]{0,1,2:T(4,128)S(1)}, f32[8,4,6]{0,1,2:T(4,128)}, u32[]{:S(2)}) copy-start(f32[8,4,6]{0,1,2:T(4,128)} %param.12) | copy-start | bytes 2308
  5.0 3.9 %copy-start.6 = (bf16[128,192]{1,0:T(8,128)(2,1)S(1)}, bf16[128,192]{1,0:T(8,128)(2,1)}, u32[]{:S(2)}) copy-start(bf16[128,192]{1,0:T(8,128)(2,1)} %constant.12.clone.rim_matrix) | copy-start | bytes 147460
  5.0 3.9 %collective-permute-start.1 = (f32[5,4,8,128]{3,2,1,0:T(8,128)S(1)}, f32[5,4,8,128]{3,2,1,0:T(8,128)S(1)}, u32[]{:S(2)}, u32[]{:S(2)}) collective-permute-start(f32[5,4,8,128]{3,2,1,0:T(8,128)S(1)} %get-tuple-element.26), channel_id=1, source_target_pairs={{0,4},{4,0},{8,12},{12,8},{16,20},{20,16},{24,28},{28,24},{32,36},... | collective-permute-start | bytes 245768 | tf_op jit(solution)/shard_map/ppermute | solution.py:456
  6.6 4.1 %copy-start.4 = (bf16[272,256]{1,0:T(8,128)(2,1)S(1)}, bf16[272,256]{1,0:T(8,128)(2,1)}, u32[]{:S(2)}) copy-start(bf16[272,256]{1,0:T(8,128)(2,1)} %constant.13.clone.matrix) | copy-start | bytes 417796
  6.6 7.9 %collective-permute-start.2 = (f32[40,8,128]{2,1,0:T(8,128)S(1)}, f32[40,8,128]{2,1,0:T(8,128)S(1)}, u32[]{:S(2)}, u32[]{:S(2)}) collective-permute-start(f32[40,8,128]{2,1,0:T(8,128)S(1)} %get-tuple-element.33), channel_id=1, source_target_pairs={{0,4},{1,0},{2,1},{3,2},{4,5},{5,6},{6,7},{7,3},{8,12},{9,8},{10,9... | collective-permute-start | bytes 491528 | tf_op jit(solution)/shard_map/ppermute | solution.py:433
  9.3 5.3 %collective-permute-start.3 = (f32[9,8,128]{2,1,0:T(8,128)S(1)}, f32[9,8,128]{2,1,0:T(8,128)S(1)}, u32[]{:S(2)}, u32[]{:S(2)}) collective-permute-start(f32[9,8,128]{2,1,0:T(8,128)S(1)} %get-tuple-element.34), channel_id=1, source_target_pairs={{0,4},{1,0},{2,1},{3,2},{4,5},{5,6},{6,7},{7,3},{8,12},{9,8},{10,9... | collective-permute-start | bytes 110600 | tf_op jit(solution)/shard_map/ppermute | solution.py:433
  10.7 3.8 %copy-start.5 = (bf16[256,128]{1,0:T(8,128)(2,1)S(1)}, bf16[256,128]{1,0:T(8,128)(2,1)}, u32[]{:S(2)}) copy-start(bf16[256,128]{1,0:T(8,128)(2,1)} %constant.14.clone.place) | copy-start | bytes 196612
  15.0 8.1 %collective-permute-start.4 = (f32[4,8,128]{2,1,0:T(8,128)S(1)}, f32[4,8,128]{2,1,0:T(8,128)S(1)}, u32[]{:S(2)}, u32[]{:S(2)}) collective-permute-start(f32[4,8,128]{2,1,0:T(8,128)S(1)} %get-tuple-element.35), channel_id=1, source_target_pairs={{0,3},{1,5},{2,1},{3,0},{4,7},{5,6},{6,2},{7,4},{8,11},{9,13},{10,... | collective-permute-start | bytes 49160 | tf_op jit(solution)/shard_map/ppermute | solution.py:433
  20.1 6.0 %collective-permute-start.5 = (f32[4,8,128]{2,1,0:T(8,128)S(1)}, f32[4,8,128]{2,1,0:T(8,128)S(1)}, u32[]{:S(2)}, u32[]{:S(2)}) collective-permute-start(f32[4,8,128]{2,1,0:T(8,128)S(1)} %get-tuple-element.36), channel_id=1, source_target_pairs={{0,1},{1,2},{2,3},{3,0},{4,5},{5,4},{6,7},{7,6},{8,9},{9,10},{10,1... | collective-permute-start | bytes 49160 | tf_op jit(solution)/shard_map/ppermute | solution.py:433
  20.1 6.2 %collective-permute-start.6 = (f32[4,8,128]{2,1,0:T(8,128)S(1)}, f32[4,8,128]{2,1,0:T(8,128)S(1)}, u32[]{:S(2)}, u32[]{:S(2)}) collective-permute-start(f32[4,8,128]{2,1,0:T(8,128)S(1)} %get-tuple-element.37), channel_id=1, source_target_pairs={{0,2},{1,3},{2,1},{3,0},{4,6},{5,7},{6,5},{7,4},{8,10},{9,11},{10,... | collective-permute-start | bytes 49160 | tf_op jit(solution)/shard_map/ppermute | solution.py:433

commit v6 on v5

--- a/solution.py
+++ b/solution.py
@@ -103,73 +103,9 @@
 
 
 def columns_kernel(
-    matrix, end_matrix, count_v, field_v,
-    bodies, last, rim, send,
+    matrix, end_matrix, table, class_v, count_v, field_v,
+    bodies, last, rim, class_t, tables, send,
     high, low,
-):
-    def prepare(source, field):
-        rim[field, pl.ds(0, 64), :] = source[pl.ds(0, 64), :]
-        rim[field, pl.ds(64, 64), :] = source[pl.ds((COLS - 8) * ROWS, 64), :]
-        high[field], low[field] = split(source[...])
-
-    def product(windows):
-        sides = []
-        for field, step in windows:
-            cells = pl.ds(step * WIDE * ROWS, 2 * WIDE * ROWS)
-            sides.append(jnp.concatenate([high[field, cells, :], low[field, cells, :]], 0))
-        return plane_blur(matrix, jnp.concatenate(sides, 1))
-
-    def sweep(field):
-        for step in range(0, BODY // WIDE, 2):
-            out = product([(field, step), (field, step + 1)])
-            for row in range(ROWS):
-                cut = out[row * WIDE : (row + 1) * WIDE]
-                tile = jnp.concatenate([cut[:, :DEPTH], cut[:, DEPTH:]], 0)
-                bodies[field * 4 + row // 2, row % 2, pl.ds(step * WIDE, 16)] = jnp.concatenate(
-                    split(tile), 1
-                )
-
-    prepare(jnp.log(1.0 + count_v[...].astype(F32)).reshape(COLS * ROWS, DEPTH), 0)
-    prepare(field_v.at[0].reshape(COLS * ROWS, DEPTH), 1)
-    sweep(0)
-    sweep(1)
-    for field in range(1, 4):
-        prepare(field_v.at[field].reshape(COLS * ROWS, DEPTH), field + 1)
-    for field in range(2, 5):
-        sweep(field)
-    for first in range(0, 5, 2):
-        windows = [(field, BODY // WIDE) for field in range(first, min(first + 2, 5))]
-        out = product(windows)
-        for j, (field, _) in enumerate(windows):
-            last[field] = out[:, j * DEPTH : (j + 1) * DEPTH].reshape(ROWS, WIDE, DEPTH)
-
-    flat_send = send.reshape(40 * ROWS, COLS)
-    own_matrix = end_matrix[jnp.where(shades_forward(lax.axis_index("tile")), 0, 1)]
-    zero = jnp.zeros((8, DEPTH), F32)
-    for index in range(20):
-        field, pair = index // 4, index % 4
-        parts = []
-        for j in range(2):
-            tail = jnp.concatenate([last[field, pair * 2 + j], zero], 0)
-            parts += [bodies[index, j], jnp.concatenate(split(tail), 1)]
-        out = depth_product(own_matrix, jnp.concatenate(parts, 0))
-        for j in range(2):
-            flat_send[pl.ds(field * 64 + pair * 2 + j, 8, stride=ROWS), :] = out[
-                :, j * 128 : (j + 1) * 128
-            ]
-
-
-def depth_product(matrix, stack):
-    out = lax.dot_general(
-        matrix, stack, (((1,), (1,)), ((), ())), preferred_element_type=F32
-    )
-    half = matrix.shape[0] // 2
-    return out[:half] + out[half:]
-
-
-def rim_kernel(
-    n_tile, table, class_v, last, rim, far, near, rim_matrix, matrix,
-    class_t, tables, tails, send,
 ):
     lane = lax.broadcasted_iota(jnp.int32, (CLASSES, CLASSES), 1)
     row_index = lax.broadcasted_iota(jnp.int32, (CLASSES, CLASSES), 0)
@@ -186,10 +122,79 @@
 
     flat = class_v.reshape(COLS * ROWS, DEPTH)
     flat_t = class_t.reshape(DEPTH * ROWS, COLS)
-    for row in range(ROWS):
+
+    def turn(row):
         plane = flat[pl.ds(row, COLS, stride=ROWS), :]
         flat_t[pl.ds(row, DEPTH, stride=ROWS), :] = pltpu.roll(plane.T, COLS - RADIUS, 1)
 
+    def prepare(source, field):
+        rim[field, pl.ds(0, 64), :] = source[pl.ds(0, 64), :]
+        rim[field, pl.ds(64, 64), :] = source[pl.ds((COLS - 8) * ROWS, 64), :]
+        high[field], low[field] = split(source[...])
+
+    def product(windows):
+        sides = []
+        for field, step in windows:
+            cells = pl.ds(step * WIDE * ROWS, 2 * WIDE * ROWS)
+            sides.append(jnp.concatenate([high[field, cells, :], low[field, cells, :]], 0))
+        return plane_blur(matrix, jnp.concatenate(sides, 1))
+
+    def sweep(field):
+        for step in range(0, BODY // WIDE, 2):
+            out = product([(field, step), (field, step + 1)])
+            for row in range(ROWS):
+                cut = out[row * WIDE : (row + 1) * WIDE]
+                tile = jnp.concatenate([cut[:, :DEPTH], cut[:, DEPTH:]], 0)
+                bodies[field * 4 + row // 2, row % 2, pl.ds(step * WIDE, 16)] = jnp.concatenate(
+                    split(tile), 1
+                )
+
+    prepare(jnp.log(1.0 + count_v[...].astype(F32)).reshape(COLS * ROWS, DEPTH), 0)
+    prepare(field_v.at[0].reshape(COLS * ROWS, DEPTH), 1)
+    sweep(0)
+    sweep(1)
+    for field in range(1, 4):
+        prepare(field_v.at[field].reshape(COLS * ROWS, DEPTH), field + 1)
+    for field in range(2, 5):
+        sweep(field)
+        for row in range((field - 2) * 3, min((field - 1) * 3, ROWS)):
+            turn(row)
+    for first in range(0, 5, 2):
+        windows = [(field, BODY // WIDE) for field in range(first, min(first + 2, 5))]
+        out = product(windows)
+        for j, (field, _) in enumerate(windows):
+            last[field] = out[:, j * DEPTH : (j + 1) * DEPTH].reshape(ROWS, WIDE, DEPTH)
+
+    forward = shades_forward(lax.axis_index("tile"))
+    for k in range(RADIUS):
+        send[40 + k] = jnp.where(forward, class_t[DEPTH - RADIUS + k], class_t[k]).astype(F32)
+    flat_send = send.reshape(44 * ROWS, COLS)
+    own_matrix = end_matrix[jnp.where(forward, 0, 1)]
+    zero = jnp.zeros((8, DEPTH), F32)
+    for index in range(20):
+        field, pair = index // 4, index % 4
+        parts = []
+        for j in range(2):
+            tail = jnp.concatenate([last[field, pair * 2 + j], zero], 0)
+            parts += [bodies[index, j], jnp.concatenate(split(tail), 1)]
+        out = depth_product(own_matrix, jnp.concatenate(parts, 0))
+        for j in range(2):
+            flat_send[pl.ds(field * 64 + pair * 2 + j, 8, stride=ROWS), :] = out[
+                :, j * 128 : (j + 1) * 128
+            ]
+
+
+def depth_product(matrix, stack):
+    out = lax.dot_general(
+        matrix, stack, (((1,), (1,)), ((), ())), preferred_element_type=F32
+    )
+    half = matrix.shape[0] // 2
+    return out[:half] + out[half:]
+
+
+def rim_kernel(
+    n_tile, last, rim, far, near, rim_matrix, matrix, tails, send
+):
     tile = lax.axis_index("tile")
     even = tile % 2 == 0
     forward = shades_forward(tile)
@@ -224,8 +229,6 @@
         out = depth_product(matrix[jnp.where(forward, 0, 1)], stack)
         for j in range(stack.shape[0] // 128):
             send[first + j] = out[:, j * 128 : (j + 1) * 128]
-    for k in range(RADIUS):
-        send[5 + k] = jnp.where(forward, class_t[DEPTH - RADIUS + k], class_t[k]).astype(F32)
 
 
 def shade_cell(values, label, tables, scale, state):
@@ -349,7 +352,7 @@
 
     one = two = end = fresh_state()
     for k in range(RADIUS):
-        theirs = given_rim[5 + k].astype(jnp.int32)
+        theirs = given[40 + k].astype(jnp.int32)
         front, back = class_t[k], class_t[DEPTH - RADIUS + k]
         values = [total[f, k] for f in range(5)]
         one = shade_cell(values, jnp.where(forward, theirs, back), tables, step_one, one)
@@ -371,8 +374,8 @@
         ref[3] = pltpu.roll(jnp.exp(-state[5]), RADIUS, 1)
 
     store(full, all_of_it)
-    store(to_two, choose(jnp.logical_and(forward, slab % 2 == 1), one, all_of_it))
-    store(to_three, choose(jnp.logical_and(forward, slab >= 2), one, all_of_it))
+    store(to_two, choose(jnp.logical_and(forward, slab >= 2), one, all_of_it))
+    store(to_three, choose(jnp.logical_and(forward, slab % 2 == 1), one, all_of_it))
     store(mine, choose(forward, forward_full, backward_part))
 
 
@@ -391,13 +394,18 @@
 def final_kernel(got_one, got_two, got_three, mine, out):
     slab = lax.axis_index("slab")
     forward = shades_forward(lax.axis_index("tile"))
-    by_one, by_two, by_three = pair(got_one), pair(got_two), pair(got_three)
-    total = only(slab == 3, by_one)
-    total = over(total, only(slab >= 2, by_three))
-    total = over(total, only(jnp.logical_and(forward, slab == 2), by_one))
-    total = over(total, only(jnp.where(forward, slab % 2 == 1, slab >= 1), by_two))
+    sets = pair(got_one), pair(got_two), pair(got_three)
+
+    def either(if_forward, if_not):
+        return [jnp.where(forward, a, b) for a, b in zip(sets[if_forward], sets[if_not])]
+
+    by_three, by_two, by_one = either(1, 0), either(0, 2), either(2, 1)
+    total = only(slab == 3, by_three)
+    total = over(total, only(slab >= 2, by_two))
+    total = over(total, only(jnp.logical_and(forward, slab == 2), by_three))
+    total = over(total, only(jnp.where(forward, slab % 2 == 1, slab >= 1), by_one))
     total = over(total, pair(mine))
-    total = over(total, only(jnp.logical_and(forward, slab % 2 == 0), by_two))
+    total = over(total, only(jnp.logical_and(forward, slab % 2 == 0), by_one))
     total = over(total, only(jnp.logical_and(forward, slab == 1), by_three))
     for i in range(3):
         out[0, i] = total[i]
@@ -457,16 +465,18 @@
 
     step_matrix = plane_matrix(list(range(RADIUS, RADIUS + WIDE)), list(range(2 * WIDE)))
     end_matrix = jnp.asarray(np.stack([depth_matrix(BACK_TARGETS), depth_matrix(FRONT_TARGETS)]))
-    bodies, last, rim, send = pl.pallas_call(
+    bodies, last, rim, class_t, tables, send = pl.pallas_call(
         columns_kernel,
         out_shape=[
             VMEM((20, 2, BODY, 2 * DEPTH), BF16),
             VMEM((5, ROWS, WIDE, DEPTH), F32),
             VMEM((5, 16 * ROWS, DEPTH), F32),
-            VMEM((40, ROWS, COLS), F32),
+            VMEM((DEPTH, ROWS, COLS), jnp.int32),
+            VMEM((24, ROWS, 128), F32),
+            VMEM((44, ROWS, COLS), F32),
         ],
-        in_specs=[SPEC] * 4,
-        out_specs=[SPEC] * 4,
+        in_specs=[SPEC] * 6,
+        out_specs=[SPEC] * 6,
         scratch_shapes=[
             VMEM((5, COLS * ROWS, DEPTH), BF16),
             VMEM((5, COLS * ROWS, DEPTH), BF16),
@@ -474,7 +484,12 @@
         compiler_params=PARAMS,
         cost_estimate=cost(3),
         name="columns",
-    )(*in_vmem(jnp.asarray(step_matrix), end_matrix, counts, fields))
+    )(
+        *in_vmem(
+            jnp.asarray(step_matrix), end_matrix, jnp.transpose(tf_table, (2, 1, 0)),
+            class_ids, counts, fields,
+        )
+    )
 
     def beside(t, s):
         to = s + 1 if shades_forward(t) else s - 1
@@ -483,25 +498,15 @@
     given = permute(send, beside)
 
     rim_matrix = plane_matrix(2 * list(range(RADIUS, 2 * RADIUS)), list(range(3 * RADIUS)))
-    class_t, tables, tails, send_rim = pl.pallas_call(
+    tails, send_rim = pl.pallas_call(
         functools.partial(rim_kernel, n_tile),
-        out_shape=[
-            VMEM((DEPTH, ROWS, COLS), jnp.int32),
-            VMEM((24, ROWS, 128), F32),
-            VMEM((20, 2, COLS - BODY, 2 * DEPTH), BF16),
-            VMEM((9, 8, 128), F32),
-        ],
-        in_specs=[SPEC] * 8,
-        out_specs=[SPEC] * 4,
+        out_shape=[VMEM((20, 2, COLS - BODY, 2 * DEPTH), BF16), VMEM((5, 8, 128), F32)],
+        in_specs=[SPEC] * 6,
+        out_specs=[SPEC] * 2,
         compiler_params=PARAMS,
-        cost_estimate=cost(1),
+        cost_estimate=cost(0.5),
         name="rim",
-    )(
-        *in_vmem(
-            jnp.transpose(tf_table, (2, 1, 0)), class_ids, last, rim, far, near,
-            jnp.asarray(rim_matrix), end_matrix,
-        )
-    )
+    )(*in_vmem(last, rim, far, near, jnp.asarray(rim_matrix), end_matrix))
     given_rim = permute(send_rim, beside)
 
     depths = len(INNER_TARGETS)
@@ -546,15 +551,18 @@
 
     def first(t, s):
         if shades_forward(t):
-            return ((t, 3), (t, 2), (t ^ 1, 2), (t, 0))[s]
+            return ((t, 2), (t, 3), (t ^ 1, 2), (t, 0))[s]
         return ((t, 3), (t ^ 1, 1), (t, 1), (t, 0))[s]
 
     def second(t, s):
-        return (t, s ^ 1 if shades_forward(t) else (s + 1) % n_slab)
+        return (t, s ^ 3 if shades_forward(t) else (s + 1) % n_slab)
+
+    def third(t, s):
+        return (t, s ^ 1 if shades_forward(t) else (2, 3, 1, 0)[s])
 
     got_one = permute(full, first)
     got_two = permute(to_two, second)
-    got_three = permute(to_three, lambda t, s: (t, (2, 3, 1, 0)[s]))
+    got_three = permute(to_three, third)
     return pl.pallas_call(
         final_kernel,
         out_shape=jax.ShapeDtypeStruct((1, 4, ROWS, COLS), F32),

time: 27.2 us -> 27.1 us (level)
  transfers between devices with their start and end apart: 7 -> 7, of which waited for: 4 -> 4; matrix products, arithmetic and copies ran while one was open for 0% -> 0% of each run, Pallas kernels for 18% -> 19%
where the time goes in v6:
time: 27.1 us; the launch traced here: 26.7 us
  starting transfers between devices  13.9 us (51%)
  Pallas kernels  7.14 us (26%)
  waiting for transfers between devices  5.52 us (20%)
    ppermute x6, starting transfers between devices, permute(): return lax.ppermute(value, ('tile', 'slab'), pairs)  13.9 us
    ppermute x6, waiting for transfers between devices, permute(): return lax.ppermute(value, ('tile', 'slab'), pairs)  5.51 us
    pallas_call x1, Pallas kernels, on_device(): pl.pallas_call(functools.partial(inner_kernel, scale), out_shape=[VMEM((6...  2.92 us
    pallas_call x1, Pallas kernels, on_device(): pl.pallas_call(columns_kernel, out_shape=[VMEM((20, 2, BODY, 2 * DEPTH),...  1.64 us
    pallas_call x1, Pallas kernels, on_device(): pl.pallas_call(pack_kernel, out_shape=[VMEM((5, RADIUS, ROWS, DEPTH), F32...  1.12 us
    pallas_call x1, Pallas kernels, on_device(): pl.pallas_call(final_kernel, out_shape=jax.ShapeDtypeStruct((1, 4, ROWS,...  0.63 us
  transfers between devices with their start and end apart: 7, of which 4 were waited for; matrix products, arithmetic and copies ran while one was open for 0% of the time, Pallas kernels for 19%

profile of v6, /device:TPU:24, one launch (start us, length us, event | category | flops | bytes accessed | tf_op | source)
XLA Modules:
  0.0 26.7 jit_solution(8181483855722097412)
XLA Ops:
  0.0 1.1 %pack.1 = (f32[5,4,8,128]{3,2,1,0:T(8,128)S(1)}, f32[5,4,8,128]{3,2,1,0:T(8,128)S(1)}) custom-call(s32[128,8,128]{2,1,0:T(8,128)} %counts.1, f32[4,128,8,128]{3,2,1,0:T(8,128)} %fields.1), custom_call_target="tpu_custom_call" | custom-call | flops 1000000000 | bytes 3600000 | tf_op jit(solution)/shard_map/pack/pallas_call | solution.py:448
  1.2 3.8 %collective-permute-start = (f32[5,4,8,128]{3,2,1,0:T(8,128)S(1)}, f32[5,4,8,128]{3,2,1,0:T(8,128)S(1)}, u32[]{:S(2)}, u32[]{:S(2)}) collective-permute-start(f32[5,4,8,128]{3,2,1,0:T(8,128)S(1)} %get-tuple-element.25), channel_id=1, source_target_pairs={{0,1},{1,0},{2,3},{3,2},{4,8},{5,9},{6,10},{7,11},{8,4},{9,5},{10,... | collective-permute-start | bytes 245768 | tf_op jit(solution)/shard_map/ppermute | solution.py:441
  5.0 0.0 collective-permute-start.1
  5.0 0.0 copy-done.8
  5.0 0.0 copy-start.6
  5.0 0.0 copy-start.4
  5.1 1.6 %columns.1 = (bf16[20,2,112,256]{3,2,1,0:T(8,128)(2,1)S(1)}, f32[5,8,8,128]{3,2,1,0:T(8,128)S(1)}, f32[5,128,128]{2,1,0:T(8,128)S(1)}, s32[128,8,128]{2,1,0:T(8,...) custom-call(bf16[128,256]{1,0:T(8,128)(2,1)S(1)} %copy-done.7, bf16[2,16,256]{2,1,0:T(8,128)(2,1)S(1)} %copy-done.8, ...), custom_call_target="tpu_custom_call" | custom-call | flops 3000000000 | bytes 10800000 | tf_op jit(solution)/shard_map/columns/pallas_call | solution.py:468
  6.7 0.5 %collective-permute-start.2 = (f32[44,8,128]{2,1,0:T(8,128)S(1)}, f32[44,8,128]{2,1,0:T(8,128)S(1)}, u32[]{:S(2)}, u32[]{:S(2)}) collective-permute-start(f32[44,8,128]{2,1,0:T(8,128)S(1)} %get-tuple-element.33), channel_id=1, source_target_pairs={{0,4},{1,0},{2,1},{3,2},{4,5},{5,6},{6,7},{7,3},{8,12},{9,8},{10,9... | collective-permute-start | bytes 540680 | tf_op jit(solution)/shard_map/ppermute | solution.py:441
  7.3 1.6 %collective-permute-done.far = f32[5,4,8,128]{3,2,1,0:T(8,128)S(1)} collective-permute-done((f32[5,4,8,128]{3,2,1,0:T(8,128)S(1)}, f32[5,4,8,128]{3,2,1,0:T(8,128)S(1)}, u32[]{:S(2)}, u32[]{:S(2)}) %collective-permute-start) | collective-permute-done | bytes 81952 | tf_op jit(solution)/shard_map/ppermute | solution.py:441
  8.8 0.0 collective-permute-done.1.near
  8.8 0.4 %rim.1 = (bf16[20,2,16,256]{3,2,1,0:T(8,128)(2,1)S(1)}, f32[5,8,128]{2,1,0:T(8,128)S(1)}) custom-call(f32[5,8,8,128]{3,2,1,0:T(8,128)S(1)} %get-tuple-element.23.last, f32[5,128,128]{2,1,0:T(8,128)S(1)} %get-tuple-element.24.rim, f32[5,4,8,128]{3,2,1,0:T(8,128)S(1)} %collective-permute-done.far, f32[5,4,8,128]{3,2,1,0:T(8,128)S(1)} %collective-permute-done.1.near, ...), custom_call_target="tpu_custom_call" | custom-call | flops 500000000 | bytes 1800000 | tf_op jit(solution)/shard_map/rim/pallas_call | solution.py:501
  9.3 1.4 %collective-permute-start.3 = (f32[5,8,128]{2,1,0:T(8,128)S(1)}, f32[5,8,128]{2,1,0:T(8,128)S(1)}, u32[]{:S(2)}, u32[]{:S(2)}) collective-permute-start(f32[5,8,128]{2,1,0:T(8,128)S(1)} %get-tuple-element.34), channel_id=1, source_target_pairs={{0,4},{1,0},{2,1},{3,2},{4,5},{5,6},{6,7},{7,3},{8,12},{9,8},{10,9... | collective-permute-start | bytes 61448 | tf_op jit(solution)/shard_map/ppermute | solution.py:441
  10.7 2.9 %inner.1 = (f32[6,8,128]{2,1,0:T(8,128)S(1)}, f32[5,8,8,128]{3,2,1,0:T(8,128)S(1)}, f32[5,4,8,128]{3,2,1,0:T(8,128)S(1)}) custom-call(bf16[20,2,112,256]{3,2,1,0:T(8,128)(2,1)S(1)} %get-tuple-element.22.bodies, bf16[20,2,16,256]{3,2,1,0:T(8,128)(2,1)S(1)} %get-tuple-element.27.tails, s32[128,8,128]{2,1,0:T(8,128)S(1)} %get-tuple-element.28.class_t, ...), custom_call_target="tpu_custom_call" | custom-call | flops 3500000000 | bytes 12600000 | tf_op jit(solution)/shard_map/inner/pallas_call | solution.py:513
  13.6 1.0 %collective-permute-done.3.given_rim = f32[5,8,128]{2,1,0:T(8,128)S(1)} collective-permute-done((f32[5,8,128]{2,1,0:T(8,128)S(1)}, f32[5,8,128]{2,1,0:T(8,128)S(1)}, u32[]{:S(2)}, u32[]{:S(2)}) %collective-permute-start.3) | collective-permute-done | bytes 20512 | tf_op jit(solution)/shard_map/ppermute | solution.py:441
  14.6 0.0 collective-permute-done.2.given
  14.6 0.0 copy-done.5
  14.6 0.4 %edges.1 = (f32[4,8,128]{2,1,0:T(8,128)S(1)}, f32[4,8,128]{2,1,0:T(8,128)S(1)}, f32[4,8,128]{2,1,0:T(8,128)S(1)}, f32[4,8,128]{2,1,0:T(8,128)S(1)}) custom-call(f32[5,8,8,128]{3,2,1,0:T(8,128)S(1)} %get-tuple-element.30.halo, f32[5,4,8,128]{3,2,1,0:T(8,128)S(1)} %get-tuple-element.31.end_cells, s32[128,8,128]{2,1,0:T(8,128)S(1)} %get-tuple-element.28.class_t, ...), custom_call_target="tpu_custom_call" | custom-call | flops 500000000 | bytes 1800000 | tf_op jit(solution)/shard_map/edges/pallas_call | solution.py:536
  15.1 5.0 %collective-permute-start.4 = (f32[4,8,128]{2,1,0:T(8,128)S(1)}, f32[4,8,128]{2,1,0:T(8,128)S(1)}, u32[]{:S(2)}, u32[]{:S(2)}) collective-permute-start(f32[4,8,128]{2,1,0:T(8,128)S(1)} %get-tuple-element.35), channel_id=1, source_target_pairs={{0,3},{1,5},{2,1},{3,0},{4,6},{5,7},{6,2},{7,4},{8,11},{9,13},{10,... | collective-permute-start | bytes 49160 | tf_op jit(solution)/shard_map/ppermute | solution.py:441
  20.0 0.0 collective-permute-start.5
  20.0 3.2 %collective-permute-start.6 = (f32[4,8,128]{2,1,0:T(8,128)S(1)}, f32[4,8,128]{2,1,0:T(8,128)S(1)}, u32[]{:S(2)}, u32[]{:S(2)}) collective-permute-start(f32[4,8,128]{2,1,0:T(8,128)S(1)} %get-tuple-element.37), channel_id=1, source_target_pairs={{0,2},{1,3},{2,1},{3,0},{4,5},{5,4},{6,7},{7,6},{8,10},{9,11},{10,... | collective-permute-start | bytes 49160 | tf_op jit(solution)/shard_map/ppermute | solution.py:441
  23.2 0.0 collective-permute-done.4.got_one
  23.2 2.7 %collective-permute-done.5.got_two = f32[4,8,128]{2,1,0:T(8,128)S(1)} collective-permute-done((f32[4,8,128]{2,1,0:T(8,128)S(1)}, f32[4,8,128]{2,1,0:T(8,128)S(1)}, u32[]{:S(2)}, u32[]{:S(2)}) %collective-permute-start.5) | collective-permute-done | bytes 16416 | tf_op jit(solution)/shard_map/ppermute | solution.py:441
  25.9 0.2 collective-permute-done.6.got_three
  26.1 0.6 %final.1 = f32[1,4,8,128]{3,2,1,0:T(8,128)} custom-call(f32[4,8,128]{2,1,0:T(8,128)S(1)} %collective-permute-done.4.got_one, f32[4,8,128]{2,1,0:T(8,128)S(1)} %collective-permute-done.5.got_two, f32[4,8,128]{2,1,0:T(8,128)S(1)} %collective-permute-done.6.got_three, f32[4,8,128]{2,1,0:T(8,128)S(1)} %get-tuple-element.38.mine), custom_call_target="tpu_custom_call" | custom-call | tf_op jit(solution)/shard_map/final/pallas_call | solution.py:566
  (14 shorter events, 0.0 us)
Async XLA Ops:
  0.0 5.0 %copy-start.8 = (bf16[2,16,256]{2,1,0:T(8,128)(2,1)S(1)}, bf16[2,16,256]{2,1,0:T(8,128)(2,1)}, u32[]{:S(2)}) copy-start(bf16[2,16,256]{2,1,0:T(8,128)(2,1)} %constant.10.clone.end_matrix.matrix) | copy-start | bytes 49156
  0.0 5.0 %copy-start.7 = (bf16[128,256]{1,0:T(8,128)(2,1)S(1)}, bf16[128,256]{1,0:T(8,128)(2,1)}, u32[]{:S(2)}) copy-start(bf16[128,256]{1,0:T(8,128)(2,1)} %constant.11.clone.matrix) | copy-start | bytes 196612
  0.0 5.0 %copy-start = (f32[4,128,8,128]{3,2,1,0:T(8,128)S(1)}, f32[4,128,8,128]{3,2,1,0:T(8,128)}, u32[]{:S(2)}) copy-start(f32[4,128,8,128]{3,2,1,0:T(8,128)} %fields.1) | copy-start | bytes 6291460
  0.0 5.0 %copy-start.2 = (s32[128,8,128]{2,1,0:T(8,128)S(1)}, s32[128,8,128]{2,1,0:T(8,128)}, u32[]{:S(2)}) copy-start(s32[128,8,128]{2,1,0:T(8,128)} %counts.1) | copy-start | bytes 1572868
  0.0 5.0 %copy-start.3 = (f32[8,4,6]{0,1,2:T(4,128)S(1)}, f32[8,4,6]{0,1,2:T(4,128)}, u32[]{:S(2)}) copy-start(f32[8,4,6]{0,1,2:T(4,128)} %param.12) | copy-start | bytes 2308
  0.0 5.0 %copy-start.1 = (s32[128,8,128]{2,1,0:T(8,128)S(1)}, s32[128,8,128]{2,1,0:T(8,128)}, u32[]{:S(2)}) copy-start(s32[128,8,128]{2,1,0:T(8,128)} %class_v.1) | copy-start | bytes 1572868
  1.2 7.7 %collective-permute-start = (f32[5,4,8,128]{3,2,1,0:T(8,128)S(1)}, f32[5,4,8,128]{3,2,1,0:T(8,128)S(1)}, u32[]{:S(2)}, u32[]{:S(2)}) collective-permute-start(f32[5,4,8,128]{3,2,1,0:T(8,128)S(1)} %get-tuple-element.25), channel_id=1, source_target_pairs={{0,1},{1,0},{2,3},{3,2},{4,8},{5,9},{6,10},{7,11},{8,4},{9,5},{10,... | collective-permute-start | bytes 245768 | tf_op jit(solution)/shard_map/ppermute | solution.py:441
  5.0 3.9 %collective-permute-start.1 = (f32[5,4,8,128]{3,2,1,0:T(8,128)S(1)}, f32[5,4,8,128]{3,2,1,0:T(8,128)S(1)}, u32[]{:S(2)}, u32[]{:S(2)}) collective-permute-start(f32[5,4,8,128]{3,2,1,0:T(8,128)S(1)} %get-tuple-element.26), channel_id=1, source_target_pairs={{0,4},{4,0},{8,12},{12,8},{16,20},{20,16},{24,28},{28,24},{32,36},... | collective-permute-start | bytes 245768 | tf_op jit(solution)/shard_map/ppermute | solution.py:464
  5.0 3.8 %copy-start.6 = (bf16[128,192]{1,0:T(8,128)(2,1)S(1)}, bf16[128,192]{1,0:T(8,128)(2,1)}, u32[]{:S(2)}) copy-start(bf16[128,192]{1,0:T(8,128)(2,1)} %constant.12.clone.rim_matrix) | copy-start | bytes 147460
  5.0 5.6 %copy-start.4 = (bf16[272,256]{1,0:T(8,128)(2,1)S(1)}, bf16[272,256]{1,0:T(8,128)(2,1)}, u32[]{:S(2)}) copy-start(bf16[272,256]{1,0:T(8,128)(2,1)} %constant.13.clone.matrix) | copy-start | bytes 417796
  6.7 7.9 %collective-permute-start.2 = (f32[44,8,128]{2,1,0:T(8,128)S(1)}, f32[44,8,128]{2,1,0:T(8,128)S(1)}, u32[]{:S(2)}, u32[]{:S(2)}) collective-permute-start(f32[44,8,128]{2,1,0:T(8,128)S(1)} %get-tuple-element.33), channel_id=1, source_target_pairs={{0,4},{1,0},{2,1},{3,2},{4,5},{5,6},{6,7},{7,3},{8,12},{9,8},{10,9... | collective-permute-start | bytes 540680 | tf_op jit(solution)/shard_map/ppermute | solution.py:441
  9.3 5.4 %collective-permute-start.3 = (f32[5,8,128]{2,1,0:T(8,128)S(1)}, f32[5,8,128]{2,1,0:T(8,128)S(1)}, u32[]{:S(2)}, u32[]{:S(2)}) collective-permute-start(f32[5,8,128]{2,1,0:T(8,128)S(1)} %get-tuple-element.34), channel_id=1, source_target_pairs={{0,4},{1,0},{2,1},{3,2},{4,5},{5,6},{6,7},{7,3},{8,12},{9,8},{10,9... | collective-permute-start | bytes 61448 | tf_op jit(solution)/shard_map/ppermute | solution.py:441
  10.7 3.9 %copy-start.5 = (bf16[256,128]{1,0:T(8,128)(2,1)S(1)}, bf16[256,128]{1,0:T(8,128)(2,1)}, u32[]{:S(2)}) copy-start(bf16[256,128]{1,0:T(8,128)(2,1)} %constant.14.clone.place) | copy-start | bytes 196612
  15.1 8.1 %collective-permute-start.4 = (f32[4,8,128]{2,1,0:T(8,128)S(1)}, f32[4,8,128]{2,1,0:T(8,128)S(1)}, u32[]{:S(2)}, u32[]{:S(2)}) collective-permute-start(f32[4,8,128]{2,1,0:T(8,128)S(1)} %get-tuple-element.35), channel_id=1, source_target_pairs={{0,3},{1,5},{2,1},{3,0},{4,6},{5,7},{6,2},{7,4},{8,11},{9,13},{10,... | collective-permute-start | bytes 49160 | tf_op jit(solution)/shard_map/ppermute | solution.py:441
  20.0 5.9 %collective-permute-start.5 = (f32[4,8,128]{2,1,0:T(8,128)S(1)}, f32[4,8,128]{2,1,0:T(8,128)S(1)}, u32[]{:S(2)}, u32[]{:S(2)}) collective-permute-start(f32[4,8,128]{2,1,0:T(8,128)S(1)} %get-tuple-element.36), channel_id=1, source_target_pairs={{0,1},{1,2},{2,3},{3,0},{4,7},{5,6},{6,5},{7,4},{8,9},{9,10},{10,1... | collective-permute-start | bytes 49160 | tf_op jit(solution)/shard_map/ppermute | solution.py:441
  20.0 6.1 %collective-permute-start.6 = (f32[4,8,128]{2,1,0:T(8,128)S(1)}, f32[4,8,128]{2,1,0:T(8,128)S(1)}, u32[]{:S(2)}, u32[]{:S(2)}) collective-permute-start(f32[4,8,128]{2,1,0:T(8,128)S(1)} %get-tuple-element.37), channel_id=1, source_target_pairs={{0,2},{1,3},{2,1},{3,0},{4,5},{5,4},{6,7},{7,6},{8,10},{9,11},{10,... | collective-permute-start | bytes 49160 | tf_op jit(solution)/shard_map/ppermute | solution.py:441

commit v7 on v6

--- a/solution.py
+++ b/solution.py
@@ -280,7 +280,7 @@
     return tuple(jnp.where(flag, a, b) for a, b in zip(one, other))
 
 
-def inner_kernel(scale, bodies, tails, class_t, tables, matrix, out, halo, end, smooth):
+def inner_kernel(scale, n_slab, bodies, tails, class_t, tables, matrix, out, halo, end, smooth):
     forward = shades_forward(lax.axis_index("tile"))
     depths = len(INNER_TARGETS)
     flat = smooth.reshape(5, depths * ROWS, COLS)
@@ -321,12 +321,21 @@
         return state
 
     state = lax.fori_loop(0, depths // unroll, body, fresh_state())
+    slab = lax.axis_index("slab")
+    shades_end = jnp.where(forward, slab == n_slab - 1, slab == 0)
+    step_end = jnp.where(shades_end, scale, 0.0)
+    last_state = fresh_state()
+    for k in range(RADIUS):
+        label = jnp.where(forward, class_t[DEPTH - RADIUS + k], class_t[k])
+        values = [end[f, k] for f in range(5)]
+        last_state = shade_cell(values, label, tables, step_end, last_state)
     for i in range(6):
         out[i] = state[i]
+        out[6 + i] = last_state[i]
 
 
 def edge_kernel(
-    scale, n_slab, halo, end_cells, class_t, tables, inner, place, given, given_rim,
+    scale, n_slab, halo, class_t, tables, inner, place, given, given_rim,
     full, to_two, to_three, mine, total,
 ):
     slab = lax.axis_index("slab")
@@ -336,7 +345,6 @@
     arrived = jnp.where(alone, 0.0, 1.0)
     step_one = jnp.where(jnp.logical_and(forward, is_first), 0.0, scale)
     step_two = jnp.where(jnp.logical_and(jnp.logical_not(forward), is_last), 0.0, scale)
-    step_end = jnp.where(jnp.where(forward, is_last, is_first), scale, 0.0)
 
     shape = (8, ROWS, COLS)
     own_row = lax.broadcasted_iota(jnp.int32, shape, 2) // 8 == lax.broadcasted_iota(
@@ -350,7 +358,7 @@
         ).reshape(shape)
         total[f] = halo[f] + (given[pl.ds(f * 8, 8)] + moved) * arrived
 
-    one = two = end = fresh_state()
+    one = two = fresh_state()
     for k in range(RADIUS):
         theirs = given[40 + k].astype(jnp.int32)
         front, back = class_t[k], class_t[DEPTH - RADIUS + k]
@@ -358,9 +366,8 @@
         one = shade_cell(values, jnp.where(forward, theirs, back), tables, step_one, one)
         values = [total[f, RADIUS + k] for f in range(5)]
         two = shade_cell(values, jnp.where(forward, front, theirs), tables, step_two, two)
-        values = [end_cells[f, k] for f in range(5)]
-        end = shade_cell(values, jnp.where(forward, back, front), tables, step_end, end)
     middle = tuple(inner[i] for i in range(6))
+    end = tuple(inner[6 + i] for i in range(6))
 
     before = join(end, middle)
     backward_part = join(before, one)
@@ -510,16 +517,18 @@
     given_rim = permute(send_rim, beside)
 
     depths = len(INNER_TARGETS)
-    inner, halo, end_cells = pl.pallas_call(
-        functools.partial(inner_kernel, scale),
+    inner, halo = pl.pallas_call(
+        functools.partial(inner_kernel, scale, n_slab),
         out_shape=[
-            VMEM((6, ROWS, COLS), F32),
+            VMEM((12, ROWS, COLS), F32),
             VMEM((5, 8, ROWS, COLS), F32),
-            VMEM((5, RADIUS, ROWS, COLS), F32),
         ],
         in_specs=[SPEC] * 5,
-        out_specs=[SPEC] * 3,
-        scratch_shapes=[VMEM((5, depths, ROWS, COLS), F32)],
+        out_specs=[SPEC] * 2,
+        scratch_shapes=[
+            VMEM((5, RADIUS, ROWS, COLS), F32),
+            VMEM((5, depths, ROWS, COLS), F32),
+        ],
         compiler_params=PARAMS,
         cost_estimate=cost(3.5),
         name="inner",
@@ -536,7 +545,7 @@
     full, to_two, to_three, mine = pl.pallas_call(
         functools.partial(edge_kernel, scale, n_slab),
         out_shape=[VMEM((4, ROWS, COLS), F32)] * 4,
-        in_specs=[SPEC] * 8,
+        in_specs=[SPEC] * 7,
         out_specs=[SPEC] * 4,
         scratch_shapes=[VMEM((5, 8, ROWS, COLS), F32)],
         compiler_params=PARAMS,
@@ -544,7 +553,7 @@
         name="edges",
     )(
         *in_vmem(
-            halo, end_cells, class_t, tables, inner,
+            halo, class_t, tables, inner,
             jnp.asarray(place.reshape(2 * COLS, COLS), BF16), given, given_rim,
         )
     )

time: 27.1 us -> 27 us (level)
  no operation moved by 1% of the time
where the time goes in v7:
time: 27 us; the launch traced here: 26.7 us
  starting transfers between devices  13.9 us (51%)
  Pallas kernels  7.15 us (26%)
  waiting for transfers between devices  5.48 us (20%)
    ppermute x6, starting transfers between devices, permute(): return lax.ppermute(value, ('tile', 'slab'), pairs)  13.9 us
    ppermute x6, waiting for transfers between devices, permute(): return lax.ppermute(value, ('tile', 'slab'), pairs)  5.47 us
    pallas_call x1, Pallas kernels, on_device(): pl.pallas_call(functools.partial(inner_kernel, scale, n_slab), out_shape=...  2.98 us
    pallas_call x1, Pallas kernels, on_device(): pl.pallas_call(columns_kernel, out_shape=[VMEM((20, 2, BODY, 2 * DEPTH),...  1.64 us
    pallas_call x1, Pallas kernels, on_device(): pl.pallas_call(pack_kernel, out_shape=[VMEM((5, RADIUS, ROWS, DEPTH), F32...  1.12 us
    pallas_call x1, Pallas kernels, on_device(): pl.pallas_call(final_kernel, out_shape=jax.ShapeDtypeStruct((1, 4, ROWS,...  0.63 us
  transfers between devices with their start and end apart: 7, of which 4 were waited for; matrix products, arithmetic and copies ran while one was open for 0% of the time, Pallas kernels for 19%

profile of v7, /device:TPU:24, one launch (start us, length us, event | category | flops | bytes accessed | tf_op | source)
XLA Modules:
  0.0 26.7 jit_solution(5062967165525053906)
XLA Ops:
  0.0 0.0 copy-start.2
  0.0 1.1 %pack.1 = (f32[5,4,8,128]{3,2,1,0:T(8,128)S(1)}, f32[5,4,8,128]{3,2,1,0:T(8,128)S(1)}) custom-call(s32[128,8,128]{2,1,0:T(8,128)} %counts.1, f32[4,128,8,128]{3,2,1,0:T(8,128)} %fields.1), custom_call_target="tpu_custom_call" | custom-call | flops 1000000000 | bytes 3600000 | tf_op jit(solution)/shard_map/pack/pallas_call | solution.py:455
  1.2 3.8 %collective-permute-start = (f32[5,4,8,128]{3,2,1,0:T(8,128)S(1)}, f32[5,4,8,128]{3,2,1,0:T(8,128)S(1)}, u32[]{:S(2)}, u32[]{:S(2)}) collective-permute-start(f32[5,4,8,128]{3,2,1,0:T(8,128)S(1)} %get-tuple-element.24), channel_id=1, source_target_pairs={{0,1},{1,0},{2,3},{3,2},{4,8},{5,9},{6,10},{7,11},{8,4},{9,5},{10,... | collective-permute-start | bytes 245768 | tf_op jit(solution)/shard_map/ppermute | solution.py:448
  5.0 0.0 collective-permute-start.1
  5.0 0.0 copy-done.8
  5.0 0.0 copy-start.6
  5.0 0.0 copy-start.4
  5.1 1.6 %columns.1 = (bf16[20,2,112,256]{3,2,1,0:T(8,128)(2,1)S(1)}, f32[5,8,8,128]{3,2,1,0:T(8,128)S(1)}, f32[5,128,128]{2,1,0:T(8,128)S(1)}, s32[128,8,128]{2,1,0:T(8,...) custom-call(bf16[128,256]{1,0:T(8,128)(2,1)S(1)} %copy-done.7, bf16[2,16,256]{2,1,0:T(8,128)(2,1)S(1)} %copy-done.8, ...), custom_call_target="tpu_custom_call" | custom-call | flops 3000000000 | bytes 10800000 | tf_op jit(solution)/shard_map/columns/pallas_call | solution.py:475
  6.7 0.5 %collective-permute-start.2 = (f32[44,8,128]{2,1,0:T(8,128)S(1)}, f32[44,8,128]{2,1,0:T(8,128)S(1)}, u32[]{:S(2)}, u32[]{:S(2)}) collective-permute-start(f32[44,8,128]{2,1,0:T(8,128)S(1)} %get-tuple-element.31), channel_id=1, source_target_pairs={{0,4},{1,0},{2,1},{3,2},{4,5},{5,6},{6,7},{7,3},{8,12},{9,8},{10,9... | collective-permute-start | bytes 540680 | tf_op jit(solution)/shard_map/ppermute | solution.py:448
  7.3 1.6 %collective-permute-done.far = f32[5,4,8,128]{3,2,1,0:T(8,128)S(1)} collective-permute-done((f32[5,4,8,128]{3,2,1,0:T(8,128)S(1)}, f32[5,4,8,128]{3,2,1,0:T(8,128)S(1)}, u32[]{:S(2)}, u32[]{:S(2)}) %collective-permute-start) | collective-permute-done | bytes 81952 | tf_op jit(solution)/shard_map/ppermute | solution.py:448
  8.8 0.0 collective-permute-done.1.near
  8.8 0.4 %rim.1 = (bf16[20,2,16,256]{3,2,1,0:T(8,128)(2,1)S(1)}, f32[5,8,128]{2,1,0:T(8,128)S(1)}) custom-call(f32[5,8,8,128]{3,2,1,0:T(8,128)S(1)} %get-tuple-element.22.last, f32[5,128,128]{2,1,0:T(8,128)S(1)} %get-tuple-element.23.rim, f32[5,4,8,128]{3,2,1,0:T(8,128)S(1)} %collective-permute-done.far, f32[5,4,8,128]{3,2,1,0:T(8,128)S(1)} %collective-permute-done.1.near, ...), custom_call_target="tpu_custom_call" | custom-call | flops 500000000 | bytes 1800000 | tf_op jit(solution)/shard_map/rim/pallas_call | solution.py:508
  9.3 1.4 %collective-permute-start.3 = (f32[5,8,128]{2,1,0:T(8,128)S(1)}, f32[5,8,128]{2,1,0:T(8,128)S(1)}, u32[]{:S(2)}, u32[]{:S(2)}) collective-permute-start(f32[5,8,128]{2,1,0:T(8,128)S(1)} %get-tuple-element.32), channel_id=1, source_target_pairs={{0,4},{1,0},{2,1},{3,2},{4,5},{5,6},{6,7},{7,3},{8,12},{9,8},{10,9... | collective-permute-start | bytes 61448 | tf_op jit(solution)/shard_map/ppermute | solution.py:448
  10.7 3.0 %inner.1 = (f32[12,8,128]{2,1,0:T(8,128)S(1)}, f32[5,8,8,128]{3,2,1,0:T(8,128)S(1)}) custom-call(bf16[20,2,112,256]{3,2,1,0:T(8,128)(2,1)S(1)} %get-tuple-element.21.bodies, bf16[20,2,16,256]{3,2,1,0:T(8,128)(2,1)S(1)} %get-tuple-element.26.tails, s32[128,8,128]{2,1,0:T(8,128)S(1)} %get-tuple-element.27.class_t, f32[24,8,128]{2,1,0:T(8,128)S(1)} %get-tuple-element.28.tables, ...), custom_call_target="tpu_custom_call" | custom-call | flops 3500000000 | bytes 12600000 | tf_op jit(solution)/shard_map/inner/pallas_call | solution.py:520
  13.7 1.0 %collective-permute-done.3.given_rim = f32[5,8,128]{2,1,0:T(8,128)S(1)} collective-permute-done((f32[5,8,128]{2,1,0:T(8,128)S(1)}, f32[5,8,128]{2,1,0:T(8,128)S(1)}, u32[]{:S(2)}, u32[]{:S(2)}) %collective-permute-start.3) | collective-permute-done | bytes 20512 | tf_op jit(solution)/shard_map/ppermute | solution.py:448
  14.6 0.0 collective-permute-done.2.given
  14.6 0.4 %edges.1 = (f32[4,8,128]{2,1,0:T(8,128)S(1)}, f32[4,8,128]{2,1,0:T(8,128)S(1)}, f32[4,8,128]{2,1,0:T(8,128)S(1)}, f32[4,8,128]{2,1,0:T(8,128)S(1)}) custom-call(f32[5,8,8,128]{3,2,1,0:T(8,128)S(1)} %get-tuple-element.29.halo, s32[128,8,128]{2,1,0:T(8,128)S(1)} %get-tuple-element.27.class_t, f32[24,8,128]{2,1,0:T(8,128)S(1)} %get-tuple-element.28.tables, ...), custom_call_target="tpu_custom_call" | custom-call | flops 500000000 | bytes 1800000 | tf_op jit(solution)/shard_map/edges/pallas_call | solution.py:545
  15.0 5.0 %collective-permute-start.4 = (f32[4,8,128]{2,1,0:T(8,128)S(1)}, f32[4,8,128]{2,1,0:T(8,128)S(1)}, u32[]{:S(2)}, u32[]{:S(2)}) collective-permute-start(f32[4,8,128]{2,1,0:T(8,128)S(1)} %get-tuple-element.33), channel_id=1, source_target_pairs={{0,3},{1,5},{2,1},{3,0},{4,6},{5,7},{6,2},{7,4},{8,11},{9,13},{10,... | collective-permute-start | bytes 49160 | tf_op jit(solution)/shard_map/ppermute | solution.py:448
  20.1 0.0 collective-permute-start.5
  20.1 3.1 %collective-permute-start.6 = (f32[4,8,128]{2,1,0:T(8,128)S(1)}, f32[4,8,128]{2,1,0:T(8,128)S(1)}, u32[]{:S(2)}, u32[]{:S(2)}) collective-permute-start(f32[4,8,128]{2,1,0:T(8,128)S(1)} %get-tuple-element.35), channel_id=1, source_target_pairs={{0,2},{1,3},{2,1},{3,0},{4,5},{5,4},{6,7},{7,6},{8,10},{9,11},{10,... | collective-permute-start | bytes 49160 | tf_op jit(solution)/shard_map/ppermute | solution.py:448
  23.1 0.0 collective-permute-done.4.got_one
  23.2 2.7 %collective-permute-done.5.got_two = f32[4,8,128]{2,1,0:T(8,128)S(1)} collective-permute-done((f32[4,8,128]{2,1,0:T(8,128)S(1)}, f32[4,8,128]{2,1,0:T(8,128)S(1)}, u32[]{:S(2)}, u32[]{:S(2)}) %collective-permute-start.5) | collective-permute-done | bytes 16416 | tf_op jit(solution)/shard_map/ppermute | solution.py:448
  25.9 0.2 collective-permute-done.6.got_three
  26.1 0.6 %final.1 = f32[1,4,8,128]{3,2,1,0:T(8,128)} custom-call(f32[4,8,128]{2,1,0:T(8,128)S(1)} %collective-permute-done.4.got_one, f32[4,8,128]{2,1,0:T(8,128)S(1)} %collective-permute-done.5.got_two, f32[4,8,128]{2,1,0:T(8,128)S(1)} %collective-permute-done.6.got_three, f32[4,8,128]{2,1,0:T(8,128)S(1)} %get-tuple-element.36.mine), custom_call_target="tpu_custom_call" | custom-call | tf_op jit(solution)/shard_map/final/pallas_call | solution.py:575
  (14 shorter events, 0.0 us)
Async XLA Ops:
  0.0 5.0 %copy-start.8 = (bf16[2,16,256]{2,1,0:T(8,128)(2,1)S(1)}, bf16[2,16,256]{2,1,0:T(8,128)(2,1)}, u32[]{:S(2)}) copy-start(bf16[2,16,256]{2,1,0:T(8,128)(2,1)} %constant.10.clone.end_matrix.matrix) | copy-start | bytes 49156
  0.0 5.0 %copy-start.7 = (bf16[128,256]{1,0:T(8,128)(2,1)S(1)}, bf16[128,256]{1,0:T(8,128)(2,1)}, u32[]{:S(2)}) copy-start(bf16[128,256]{1,0:T(8,128)(2,1)} %constant.11.clone.matrix) | copy-start | bytes 196612
  0.0 5.0 %copy-start = (f32[4,128,8,128]{3,2,1,0:T(8,128)S(1)}, f32[4,128,8,128]{3,2,1,0:T(8,128)}, u32[]{:S(2)}) copy-start(f32[4,128,8,128]{3,2,1,0:T(8,128)} %fields.1) | copy-start | bytes 6291460
  0.0 5.0 %copy-start.2 = (s32[128,8,128]{2,1,0:T(8,128)S(1)}, s32[128,8,128]{2,1,0:T(8,128)}, u32[]{:S(2)}) copy-start(s32[128,8,128]{2,1,0:T(8,128)} %counts.1) | copy-start | bytes 1572868
  0.0 5.0 %copy-start.3 = (f32[8,4,6]{0,1,2:T(4,128)S(1)}, f32[8,4,6]{0,1,2:T(4,128)}, u32[]{:S(2)}) copy-start(f32[8,4,6]{0,1,2:T(4,128)} %param.12) | copy-start | bytes 2308
  0.0 5.0 %copy-start.1 = (s32[128,8,128]{2,1,0:T(8,128)S(1)}, s32[128,8,128]{2,1,0:T(8,128)}, u32[]{:S(2)}) copy-start(s32[128,8,128]{2,1,0:T(8,128)} %class_v.1) | copy-start | bytes 1572868
  1.2 7.7 %collective-permute-start = (f32[5,4,8,128]{3,2,1,0:T(8,128)S(1)}, f32[5,4,8,128]{3,2,1,0:T(8,128)S(1)}, u32[]{:S(2)}, u32[]{:S(2)}) collective-permute-start(f32[5,4,8,128]{3,2,1,0:T(8,128)S(1)} %get-tuple-element.24), channel_id=1, source_target_pairs={{0,1},{1,0},{2,3},{3,2},{4,8},{5,9},{6,10},{7,11},{8,4},{9,5},{10,... | collective-permute-start | bytes 245768 | tf_op jit(solution)/shard_map/ppermute | solution.py:448
  5.0 3.9 %collective-permute-start.1 = (f32[5,4,8,128]{3,2,1,0:T(8,128)S(1)}, f32[5,4,8,128]{3,2,1,0:T(8,128)S(1)}, u32[]{:S(2)}, u32[]{:S(2)}) collective-permute-start(f32[5,4,8,128]{3,2,1,0:T(8,128)S(1)} %get-tuple-element.25), channel_id=1, source_target_pairs={{0,4},{4,0},{8,12},{12,8},{16,20},{20,16},{24,28},{28,24},{32,36},... | collective-permute-start | bytes 245768 | tf_op jit(solution)/shard_map/ppermute | solution.py:471
  5.0 3.8 %copy-start.6 = (bf16[128,192]{1,0:T(8,128)(2,1)S(1)}, bf16[128,192]{1,0:T(8,128)(2,1)}, u32[]{:S(2)}) copy-start(bf16[128,192]{1,0:T(8,128)(2,1)} %constant.12.clone.rim_matrix) | copy-start | bytes 147460
  5.0 5.6 %copy-start.4 = (bf16[272,256]{1,0:T(8,128)(2,1)S(1)}, bf16[272,256]{1,0:T(8,128)(2,1)}, u32[]{:S(2)}) copy-start(bf16[272,256]{1,0:T(8,128)(2,1)} %constant.13.clone.matrix) | copy-start | bytes 417796
  6.7 7.9 %collective-permute-start.2 = (f32[44,8,128]{2,1,0:T(8,128)S(1)}, f32[44,8,128]{2,1,0:T(8,128)S(1)}, u32[]{:S(2)}, u32[]{:S(2)}) collective-permute-start(f32[44,8,128]{2,1,0:T(8,128)S(1)} %get-tuple-element.31), channel_id=1, source_target_pairs={{0,4},{1,0},{2,1},{3,2},{4,5},{5,6},{6,7},{7,3},{8,12},{9,8},{10,9... | collective-permute-start | bytes 540680 | tf_op jit(solution)/shard_map/ppermute | solution.py:448
  9.3 5.4 %collective-permute-start.3 = (f32[5,8,128]{2,1,0:T(8,128)S(1)}, f32[5,8,128]{2,1,0:T(8,128)S(1)}, u32[]{:S(2)}, u32[]{:S(2)}) collective-permute-start(f32[5,8,128]{2,1,0:T(8,128)S(1)} %get-tuple-element.32), channel_id=1, source_target_pairs={{0,4},{1,0},{2,1},{3,2},{4,5},{5,6},{6,7},{7,3},{8,12},{9,8},{10,9... | collective-permute-start | bytes 61448 | tf_op jit(solution)/shard_map/ppermute | solution.py:448
  10.7 3.9 %copy-start.5 = (bf16[256,128]{1,0:T(8,128)(2,1)S(1)}, bf16[256,128]{1,0:T(8,128)(2,1)}, u32[]{:S(2)}) copy-start(bf16[256,128]{1,0:T(8,128)(2,1)} %constant.14.clone.place) | copy-start | bytes 196612
  15.0 8.1 %collective-permute-start.4 = (f32[4,8,128]{2,1,0:T(8,128)S(1)}, f32[4,8,128]{2,1,0:T(8,128)S(1)}, u32[]{:S(2)}, u32[]{:S(2)}) collective-permute-start(f32[4,8,128]{2,1,0:T(8,128)S(1)} %get-tuple-element.33), channel_id=1, source_target_pairs={{0,3},{1,5},{2,1},{3,0},{4,6},{5,7},{6,2},{7,4},{8,11},{9,13},{10,... | collective-permute-start | bytes 49160 | tf_op jit(solution)/shard_map/ppermute | solution.py:448
  20.1 5.8 %collective-permute-start.5 = (f32[4,8,128]{2,1,0:T(8,128)S(1)}, f32[4,8,128]{2,1,0:T(8,128)S(1)}, u32[]{:S(2)}, u32[]{:S(2)}) collective-permute-start(f32[4,8,128]{2,1,0:T(8,128)S(1)} %get-tuple-element.34), channel_id=1, source_target_pairs={{0,1},{1,2},{2,3},{3,0},{4,7},{5,6},{6,5},{7,4},{8,9},{9,10},{10,1... | collective-permute-start | bytes 49160 | tf_op jit(solution)/shard_map/ppermute | solution.py:448
  20.1 6.0 %collective-permute-start.6 = (f32[4,8,128]{2,1,0:T(8,128)S(1)}, f32[4,8,128]{2,1,0:T(8,128)S(1)}, u32[]{:S(2)}, u32[]{:S(2)}) collective-permute-start(f32[4,8,128]{2,1,0:T(8,128)S(1)} %get-tuple-element.35), channel_id=1, source_target_pairs={{0,2},{1,3},{2,1},{3,0},{4,5},{5,4},{6,7},{7,6},{8,10},{9,11},{10,... | collective-permute-start | bytes 49160 | tf_op jit(solution)/shard_map/ppermute | solution.py:448
